TPU v7x, 32 devices: a whole 2x2x4 slice. The times are simulated.
32 devices in a mesh: dp: 4 (over z), context: 4 (over x, core), expert: 2 (over y).
Axes of the slice: x: 2, y: 2, z: 4, core: 2. Of those that a mesh axis runs over, the one named last changes fastest.
Arguments:
- tokens: bfloat16 [4096, 2048], P(('dp', 'context', 'expert')), may hold values from -6 to 6
- out_grad: bfloat16 [4096, 2048], P(('dp', 'context', 'expert')), may hold values from -6 to 6
- expert_ids: int32 [4096, 4], P(('dp', 'context', 'expert')), may hold values from 0 to 7, all different within a row; in each aligned block of 128 rows (0 to 127, 128 to 255, ...) at most 96 rows name the same one
- norm1_gain: bfloat16 [2048], P(('dp', 'context')), may hold values from 0.5 to 1.5
- w_query: bfloat16 [2048, 2048], P(('dp', 'context'), 'expert'), may hold values from -0.125 to 0.125
- w_key: bfloat16 [2048, 2048], P(('dp', 'context'), 'expert'), may hold values from -0.125 to 0.125
- w_value: bfloat16 [2048, 2048], P(('dp', 'context'), 'expert'), may hold values from -0.125 to 0.125
- query_bias_heads: bfloat16 [16, 128], P('expert'), may hold values from -3 to 3
- bias_key: bfloat16 [16, 128], P('expert'), may hold values from -3 to 3
- bias_value: bfloat16 [16, 128], P('expert'), may hold values from -0.119628906 to 0.119628906
- w_out: bfloat16 [2048, 2048], P('expert', ('dp', 'context')), may hold values from -3 to 3
- norm2_gain: bfloat16 [2048], P(('dp', 'context')), may hold values from 0.5 to 1.5
- w_router: bfloat16 [2048, 8], P(('dp', 'context')), may hold values from -0.0625 to 0.0625
- shared_mix: bfloat16 [2048], P(('dp', 'context')), may hold values from -0.125 to 0.125
- shared_in_gate: bfloat16 [2048, 5632], P(('dp', 'context'), 'expert'), may hold values from -0.125 to 0.125
- shared_in_up: bfloat16 [2048, 5632], P(('dp', 'context'), 'expert'), may hold values from -0.125 to 0.125
- shared_down: bfloat16 [5632, 2048], P('expert', ('dp', 'context')), may hold values from -0.21875 to 0.21875
- expert_gate: bfloat16 [8, 2048, 1408], P(('dp', 'expert')), may hold values from -0.125 to 0.125
- expert_up: bfloat16 [8, 2048, 1408], P(('dp', 'expert')), may hold values from -0.125 to 0.125
- expert_down: bfloat16 [8, 1408, 2048], P(('dp', 'expert')), may hold values from -1.25 to 1.25
Outputs:
- mixed: bfloat16 [4096, 2048], P(('dp', 'context', 'expert'))
- input_grad: bfloat16 [4096, 2048], P(('dp', 'context', 'expert'))
- norm1_gain_grad: float32 [2048], P(('dp', 'context'))
- w_query_grad: float32 [2048, 2048], P(('dp', 'context'), 'expert')
- w_key_grad: float32 [2048, 2048], P(('dp', 'context'), 'expert')
- w_value_grad: float32 [2048, 2048], P(('dp', 'context'), 'expert')
- bias_query_grad: float32 [16, 128], P('expert', ('dp', 'context'))
- bias_key_grad: float32 [16, 128], P('expert', ('dp', 'context'))
- bias_value_grad: float32 [16, 128], P('expert', ('dp', 'context'))
- w_out_grad: float32 [2048, 2048], P('expert', ('dp', 'context'))
- norm2_gain_grad: float32 [2048], P(('dp', 'context'))
- w_router_grad: float32 [2048, 8], P(('dp', 'context'))
- shared_mix_grad: float32 [2048], P(('dp', 'context'))
- shared_in_gate_grad: float32 [2048, 5632], P(('dp', 'context'), 'expert')
- shared_in_up_grad: float32 [2048, 5632], P(('dp', 'context'), 'expert')
- shared_down_grad: float32 [5632, 2048], P('expert', ('dp', 'context'))
- expert_gate_grad: float32 [8, 2048, 1408], P(('dp', 'expert'), 'context')
- expert_up_grad: float32 [8, 2048, 1408], P(('dp', 'expert'), 'context')
- expert_down_grad: float32 [8, 1408, 2048], P(('dp', 'expert'), None, 'context')
Inputs may be any that keep to these rules, and one draw needn't show every extreme that they name: `expert_ids`: each row names 4 different experts. In the rows of one device no expert is named more than 96 times, and 96 is reached on some device in every draw.
All inputs are finite; a program needn't handle non-finite values.
Results may differ from a plain program's by a relative error of at most 0.023.
Values may be sent and summed in bfloat16 or wider, within the bound.
A program may use at most 320 MiB of HBM per device.

v0:
```python
import math

import jax
import jax.numpy as jnp
from jax import lax
from jax.sharding import PartitionSpec as P

BLOCK = 256
CAP = 96


EPS = 1e-06
THETA = 1000000.0
HIGH = lax.Precision.HIGHEST


def rope_tables(positions, head_dim):
    half = head_dim // 2
    freq = THETA ** (-(2.0 * jnp.arange(half, dtype=jnp.float32)) / head_dim)
    angle = positions.astype(jnp.float32)[:, None] * freq[None, :]
    return (jnp.cos(angle)[:, None, :], jnp.sin(angle)[:, None, :])


def rotate(values, cosine, sine):
    half = values.shape[-1] // 2
    first = values[..., :half]
    second = values[..., half:]
    return jnp.concatenate(
        [first * cosine - second * sine, second * cosine + first * sine], axis=-1
    )


def rotate_back(values, cosine, sine):
    half = values.shape[-1] // 2
    first = values[..., :half]
    second = values[..., half:]
    return jnp.concatenate(
        [first * cosine + second * sine, second * cosine - first * sine], axis=-1
    )


def to_groups(matrix, groups, group_size, head_dim):
    return matrix.reshape(matrix.shape[0], groups, group_size, head_dim).transpose(1, 2, 0, 3)


def from_groups(stacked):
    return stacked.transpose(2, 0, 1, 3).reshape(stacked.shape[2], -1)


def silu_slope(values):
    sigma = jax.nn.sigmoid(values)
    return sigma * (1.0 + values * (1.0 - sigma))


def left_operand(left, right):
    return jnp.dot(left.T, right, preferred_element_type=jnp.float32)


def mat_right(left, right):
    return jnp.dot(left, right.T, preferred_element_type=jnp.float32)


def on_device(
    tokens,
    out_grad,
    expert_ids,
    norm1_gain,
    w_query,
    w_key,
    w_value,
    query_bias_heads,
    bias_key,
    bias_value,
    w_out,
    norm2_gain,
    w_router,
    shared_mix,
    shared_in_gate,
    shared_in_up,
    shared_down,
    expert_gate,
    expert_up,
    expert_down,
):
    tok_rows = tokens.shape[0]
    width = tokens.shape[1]
    my_half = lax.axis_index("expert")
    my_piece = lax.axis_index("context")
    n_pieces = lax.axis_size("context")
    local_heads = query_bias_heads.shape[0]
    head_dim = query_bias_heads.shape[1]
    group_size = 2
    groups = local_heads // group_size
    score_scale = 1.0 / math.sqrt(head_dim)
    (
        full_query,
        full_key,
        full_value,
        full_out,
        full_sgate,
        full_sup,
        full_sdown,
        full_router,
        full_mix,
        full_gain_one,
        full_gain_two,
    ) = (
        lax.all_gather(w_query, ("dp", "context"), axis=0, tiled=True),
        lax.all_gather(w_key, ("dp", "context"), axis=0, tiled=True),
        lax.all_gather(w_value, ("dp", "context"), axis=0, tiled=True),
        lax.all_gather(w_out, ("dp", "context"), axis=1, tiled=True),
        lax.all_gather(shared_in_gate, ("dp", "context"), axis=0, tiled=True),
        lax.all_gather(shared_in_up, ("dp", "context"), axis=0, tiled=True),
        lax.all_gather(shared_down, ("dp", "context"), axis=1, tiled=True),
        lax.all_gather(w_router, ("dp", "context"), axis=0, tiled=True),
        lax.all_gather(shared_mix, ("dp", "context"), axis=0, tiled=True),
        lax.all_gather(norm1_gain, ("dp", "context"), axis=0, tiled=True),
        lax.all_gather(norm2_gain, ("dp", "context"), axis=0, tiled=True),
    )
    x_piece, dy_piece = (
        lax.all_gather(tokens, "expert", axis=0, tiled=True),
        lax.all_gather(out_grad, "expert", axis=0, tiled=True),
    )
    piece_rows = x_piece.shape[0]
    seq_len = piece_rows * n_pieces
    own_start = my_half * tok_rows
    positions = my_piece * piece_rows + jnp.arange(piece_rows)
    cosine, sine = rope_tables(positions, head_dim)
    query_blocks = positions // BLOCK
    key_blocks = jnp.arange(seq_len) // BLOCK
    visible = key_blocks[None, :] <= query_blocks[:, None]
    x_float = x_piece.astype(jnp.float32)
    rstd_one = lax.rsqrt(jnp.mean(x_float * x_float, axis=1, keepdims=True) + EPS)
    normed_one = x_float * rstd_one
    gain_one = full_gain_one.astype(jnp.float32)
    attn_in = (normed_one * gain_one).astype(jnp.bfloat16)
    q_pre = jnp.dot(
        attn_in, full_query, preferred_element_type=jnp.float32
    ) + query_bias_heads.astype(jnp.float32).reshape(-1)
    k_pre = jnp.dot(attn_in, full_key, preferred_element_type=jnp.float32) + bias_key.astype(
        jnp.float32
    ).reshape(-1)
    v_pre = jnp.dot(attn_in, full_value, preferred_element_type=jnp.float32) + bias_value.astype(
        jnp.float32
    ).reshape(-1)
    q_rot = (
        rotate(q_pre.reshape(piece_rows, local_heads, head_dim), cosine, sine)
        .reshape(piece_rows, -1)
        .astype(jnp.bfloat16)
    )
    k_rot = (
        rotate(k_pre.reshape(piece_rows, local_heads, head_dim), cosine, sine)
        .reshape(piece_rows, -1)
        .astype(jnp.bfloat16)
    )
    v_low = v_pre.astype(jnp.bfloat16)
    keys_all, values_all = (
        lax.all_gather(k_rot, "context", axis=0, tiled=True),
        lax.all_gather(v_low, "context", axis=0, tiled=True),
    )
    query_grp = to_groups(q_rot, groups, group_size, head_dim)
    keys_grp = to_groups(keys_all, groups, group_size, head_dim)
    values_grp = to_groups(values_all, groups, group_size, head_dim)

    def attend_group(args):
        group_query, group_keys, group_values = args
        scores = (
            jnp.einsum("hqd,hkd->hqk", group_query, group_keys, preferred_element_type=jnp.float32)
            * score_scale
        )
        scores = jnp.where(visible[None], scores, -jnp.inf)
        row_top = jnp.max(scores, axis=2, keepdims=True)
        expo = jnp.exp(scores - row_top)
        totals = jnp.sum(expo, axis=2, keepdims=True)
        probs = (expo / totals).astype(jnp.bfloat16)
        result = jnp.einsum("hqk,hkd->hqd", probs, group_values, preferred_element_type=jnp.float32)
        return (result, row_top[..., 0] + jnp.log(totals[..., 0]))

    attn_grp, lse_grp = lax.map(attend_group, (query_grp, keys_grp, values_grp))
    attn_low = from_groups(attn_grp).astype(jnp.bfloat16)
    out_partial = jnp.dot(attn_low, full_out, preferred_element_type=jnp.float32)
    out_full = lax.psum(out_partial, "expert")
    hidden_one = x_float + out_full
    rstd_two = lax.rsqrt(jnp.mean(hidden_one * hidden_one, axis=1, keepdims=True) + EPS)
    normed_two = hidden_one * rstd_two
    gain_two = full_gain_two.astype(jnp.float32)
    moe_in = (normed_two * gain_two).astype(jnp.bfloat16)
    mix = jax.nn.sigmoid(jnp.dot(moe_in, full_mix, preferred_element_type=jnp.float32))
    s_gate = jnp.dot(moe_in, full_sgate, preferred_element_type=jnp.float32)
    s_up = jnp.dot(moe_in, full_sup, preferred_element_type=jnp.float32)
    s_silu = jax.nn.silu(s_gate)
    s_hidden = (s_silu * s_up).astype(jnp.bfloat16)
    shared_own = lax.psum_scatter(
        jnp.dot(s_hidden, full_sdown, preferred_element_type=jnp.float32),
        "expert",
        scatter_dimension=0,
        tiled=True,
    )
    moe_own = lax.dynamic_slice_in_dim(moe_in, own_start, tok_rows, 0)
    hidden_own = lax.dynamic_slice_in_dim(hidden_one, own_start, tok_rows, 0)
    mix_own = lax.dynamic_slice_in_dim(mix, own_start, tok_rows, 0)
    dy_own = out_grad.astype(jnp.float32)
    n_experts = full_router.shape[1]
    router_probs = jax.nn.softmax(
        jnp.dot(moe_own, full_router, preferred_element_type=jnp.float32), axis=1
    )
    picked = (expert_ids[:, :, None] == jnp.arange(n_experts)[None, None, :]).astype(jnp.float32)
    gates = jnp.sum(picked * router_probs[:, None, :], axis=2)
    route_hot = (
        (expert_ids[:, :, None] == jnp.arange(n_experts)[None, None, :])
        .astype(jnp.int32)
        .reshape(-1, n_experts)
    )
    earlier = jnp.cumsum(route_hot, axis=0) - route_hot
    slots = jnp.sum(earlier * route_hot, axis=1)
    places = expert_ids.reshape(-1) * CAP + slots
    route_rows = jnp.repeat(moe_own, expert_ids.shape[1], axis=0)
    route_grads = (
        gates.reshape(-1)[:, None] * jnp.repeat(dy_own, expert_ids.shape[1], axis=0)
    ).astype(jnp.bfloat16)
    send_rows = (
        jnp.zeros((n_experts * CAP, width), jnp.bfloat16)
        .at[places]
        .set(route_rows)
        .reshape(n_experts, CAP, width)
    )
    send_grads = (
        jnp.zeros((n_experts * CAP, width), jnp.bfloat16)
        .at[places]
        .set(route_grads)
        .reshape(n_experts, CAP, width)
    )
    gate_weight = expert_gate[0]
    up_weight = expert_up[0]
    down_weight = expert_down[0]
    rows_in = lax.all_to_all(send_rows, ("dp", "expert"), split_axis=0, concat_axis=0, tiled=True)
    grads_in = lax.all_to_all(send_grads, ("dp", "expert"), split_axis=0, concat_axis=0, tiled=True)
    sources = rows_in.shape[0]
    items = rows_in.shape[1]
    flat_in = rows_in.reshape(-1, width)
    flat_grad = grads_in.reshape(-1, width)
    e_gate = jnp.dot(flat_in, gate_weight, preferred_element_type=jnp.float32)
    e_up = jnp.dot(flat_in, up_weight, preferred_element_type=jnp.float32)
    e_silu = jax.nn.silu(e_gate)
    e_hidden = (e_silu * e_up).astype(jnp.bfloat16)
    e_out = jnp.dot(e_hidden, down_weight, preferred_element_type=jnp.float32).astype(jnp.bfloat16)
    d_hidden = mat_right(flat_grad, down_weight)
    d_gate = (d_hidden * e_up * silu_slope(e_gate)).astype(jnp.bfloat16)
    d_up = (d_hidden * e_silu).astype(jnp.bfloat16)
    d_in = (mat_right(d_gate, gate_weight) + mat_right(d_up, up_weight)).astype(jnp.bfloat16)
    back_out = lax.all_to_all(
        e_out.reshape(sources, items, width),
        ("dp", "expert"),
        split_axis=0,
        concat_axis=0,
        tiled=True,
    )
    back_in = lax.all_to_all(
        d_in.reshape(sources, items, width),
        ("dp", "expert"),
        split_axis=0,
        concat_axis=0,
        tiled=True,
    )
    back_out, back_in, rows_seen, grads_seen, hidden_seen, dgate_seen, duplicate_visits = (
        back_out,
        back_in,
        rows_in,
        grads_in,
        e_hidden.reshape(sources, items, -1),
        d_gate.reshape(sources, items, -1),
        d_up.reshape(sources, items, -1),
    )
    flattened_rows = rows_seen.reshape(-1, width)
    routed_gate_gradient = left_operand(
        flattened_rows, dgate_seen.reshape(flattened_rows.shape[0], -1)
    )
    routed_up_gradient = left_operand(
        flattened_rows, duplicate_visits.reshape(flattened_rows.shape[0], -1)
    )
    routed_down_gradient = left_operand(
        hidden_seen.reshape(flattened_rows.shape[0], -1), grads_seen.reshape(-1, width)
    )
    routed_gate_gradient, routed_up_gradient, routed_down_gradient = (
        lax.psum_scatter(
            routed_gate_gradient[None].astype(jnp.bfloat16),
            "context",
            scatter_dimension=1,
            tiled=True,
        ).astype(jnp.float32),
        lax.psum_scatter(
            routed_up_gradient[None].astype(jnp.bfloat16),
            "context",
            scatter_dimension=1,
            tiled=True,
        ).astype(jnp.float32),
        lax.psum_scatter(
            routed_down_gradient[None].astype(jnp.bfloat16),
            "context",
            scatter_dimension=2,
            tiled=True,
        ).astype(jnp.float32),
    )
    route_out = back_out.reshape(-1, width)[places].astype(jnp.float32).reshape(tok_rows, -1, width)
    route_din = back_in.reshape(-1, width)[places].astype(jnp.float32).reshape(tok_rows, -1, width)
    moe_sum = jnp.sum(gates[:, :, None] * route_out, axis=1)
    mixed = (hidden_own + moe_sum + mix_own[:, None] * shared_own).astype(jnp.bfloat16)
    d_gates = jnp.sum(route_out * dy_own[:, None, :], axis=2)
    d_rprobs = jnp.sum(picked * d_gates[:, :, None], axis=1)
    d_logits = router_probs * (d_rprobs - jnp.sum(router_probs * d_rprobs, axis=1, keepdims=True))
    moe_own_float = moe_own.astype(jnp.float32)
    router_part = jnp.dot(moe_own_float.T, d_logits, precision=HIGH)
    d_mixlogit = jnp.sum(shared_own * dy_own, axis=1) * mix_own * (1.0 - mix_own)
    mix_part = jnp.dot(moe_own_float.T, d_mixlogit, precision=HIGH)
    d_in_own = (
        jnp.sum(route_din, axis=1)
        + jnp.dot(d_logits, full_router.astype(jnp.float32).T, precision=HIGH)
        + d_mixlogit[:, None] * full_mix.astype(jnp.float32)[None, :]
    )
    dy_float = dy_piece.astype(jnp.float32)
    d_shared = (mix[:, None] * dy_float).astype(jnp.bfloat16)
    grad_sdown = left_operand(s_hidden, d_shared)
    d_shidden = mat_right(d_shared, full_sdown)
    d_sgate = (d_shidden * s_up * silu_slope(s_gate)).astype(jnp.bfloat16)
    d_sup = (d_shidden * s_silu).astype(jnp.bfloat16)
    grad_sgate = left_operand(moe_in, d_sgate)
    grad_sup = left_operand(moe_in, d_sup)
    d_in_part = mat_right(d_sgate, full_sgate) + mat_right(d_sup, full_sup)
    d_in_part = lax.dynamic_update_slice_in_dim(
        d_in_part,
        lax.dynamic_slice_in_dim(d_in_part, own_start, tok_rows, 0) + d_in_own,
        own_start,
        0,
    )
    d_moe_in, router_grad, mix_grad = lax.psum((d_in_part, router_part, mix_part), "expert")
    d_norm_two = d_moe_in * gain_two
    gain_two_grad = jnp.sum(d_moe_in * normed_two, axis=0)
    d_hidden_one = dy_float + rstd_two * (
        d_norm_two - normed_two * jnp.mean(d_norm_two * normed_two, axis=1, keepdims=True)
    )
    d_proj = d_hidden_one.astype(jnp.bfloat16)
    grad_out = left_operand(attn_low, d_proj)
    d_attn = mat_right(d_proj, full_out).astype(jnp.bfloat16)
    dattn_grp = to_groups(d_attn, groups, group_size, head_dim)

    def query_side(args):
        group_query, group_keys, group_values, group_lse, group_attention_gradient = args
        scores = (
            jnp.einsum("hqd,hkd->hqk", group_query, group_keys, preferred_element_type=jnp.float32)
            * score_scale
        )
        probs = jnp.where(
            visible[None],
            jnp.exp(jnp.where(visible[None], scores, 0.0) - group_lse[..., None]),
            0.0,
        )
        d_probs = jnp.einsum(
            "hqd,hkd->hqk",
            group_attention_gradient,
            group_values,
            preferred_element_type=jnp.float32,
        )
        delta = jnp.sum(probs * d_probs, axis=2)
        d_scores = (probs * (d_probs - delta[..., None])).astype(jnp.bfloat16)
        d_query = (
            jnp.einsum("hqk,hkd->hqd", d_scores, group_keys, preferred_element_type=jnp.float32)
            * score_scale
        )
        return (probs, d_scores, d_query, delta)

    def both_sides(args):
        probs, d_scores, d_query, delta = query_side(args)
        d_key = (
            jnp.einsum("hqk,hqd->hkd", d_scores, args[0], preferred_element_type=jnp.float32)
            * score_scale
        )
        d_value = jnp.einsum(
            "hqk,hqd->hkd", probs.astype(jnp.bfloat16), args[4], preferred_element_type=jnp.float32
        )
        return (d_query, d_key, d_value)

    dq_grp, dk_grp, dv_grp = lax.map(
        both_sides, (query_grp, keys_grp, values_grp, lse_grp, dattn_grp)
    )
    d_query = from_groups(dq_grp)
    d_key_own, d_value_own = (
        lax.psum_scatter(from_groups(dk_grp), "context", scatter_dimension=0, tiled=True),
        lax.psum_scatter(from_groups(dv_grp), "context", scatter_dimension=0, tiled=True),
    )
    d_q_pre = (
        rotate_back(d_query.reshape(piece_rows, local_heads, head_dim), cosine, sine)
        .reshape(piece_rows, -1)
        .astype(jnp.bfloat16)
    )
    d_k_pre = (
        rotate_back(d_key_own.reshape(piece_rows, local_heads, head_dim), cosine, sine)
        .reshape(piece_rows, -1)
        .astype(jnp.bfloat16)
    )
    d_v_pre = d_value_own.astype(jnp.bfloat16)
    grad_bq = jnp.sum(d_q_pre.astype(jnp.float32), axis=0).reshape(local_heads, head_dim)
    grad_bk = jnp.sum(d_k_pre.astype(jnp.float32), axis=0).reshape(local_heads, head_dim)
    grad_bv = jnp.sum(d_v_pre.astype(jnp.float32), axis=0).reshape(local_heads, head_dim)
    grad_query = left_operand(attn_in, d_q_pre)
    grad_key = left_operand(attn_in, d_k_pre)
    grad_value = left_operand(attn_in, d_v_pre)
    d_attn_in = (
        mat_right(d_q_pre, full_query)
        + mat_right(d_k_pre, full_key)
        + mat_right(d_v_pre, full_value)
    )
    d_attn_in = lax.psum(d_attn_in.astype(jnp.bfloat16), "expert").astype(jnp.float32)
    d_norm_one = d_attn_in * gain_one
    gain_one_grad = jnp.sum(d_attn_in * normed_one, axis=0)
    d_x = d_hidden_one + rstd_one * (
        d_norm_one - normed_one * jnp.mean(d_norm_one * normed_one, axis=1, keepdims=True)
    )
    input_grad = lax.dynamic_slice_in_dim(d_x, own_start, tok_rows, 0).astype(jnp.bfloat16)
    (
        grad_query,
        grad_key,
        grad_value,
        grad_out,
        grad_sgate,
        grad_sup,
        grad_sdown,
        router_grad,
        mix_grad,
        gain_one_grad,
        gain_two_grad,
        grad_bq,
        grad_bk,
        grad_bv,
    ) = (
        lax.psum_scatter(grad_query, ("dp", "context"), scatter_dimension=0, tiled=True),
        lax.psum_scatter(grad_key, ("dp", "context"), scatter_dimension=0, tiled=True),
        lax.psum_scatter(grad_value, ("dp", "context"), scatter_dimension=0, tiled=True),
        lax.psum_scatter(grad_out, ("dp", "context"), scatter_dimension=1, tiled=True),
        lax.psum_scatter(grad_sgate, ("dp", "context"), scatter_dimension=0, tiled=True),
        lax.psum_scatter(grad_sup, ("dp", "context"), scatter_dimension=0, tiled=True),
        lax.psum_scatter(grad_sdown, ("dp", "context"), scatter_dimension=1, tiled=True),
        lax.psum_scatter(router_grad, ("dp", "context"), scatter_dimension=0, tiled=True),
        lax.psum_scatter(mix_grad, ("dp", "context"), scatter_dimension=0, tiled=True),
        lax.psum_scatter(gain_one_grad, ("dp", "context"), scatter_dimension=0, tiled=True),
        lax.psum_scatter(gain_two_grad, ("dp", "context"), scatter_dimension=0, tiled=True),
        lax.psum_scatter(grad_bq, ("dp", "context"), scatter_dimension=1, tiled=True),
        lax.psum_scatter(grad_bk, ("dp", "context"), scatter_dimension=1, tiled=True),
        lax.psum_scatter(grad_bv, ("dp", "context"), scatter_dimension=1, tiled=True),
    )
    return (
        mixed,
        input_grad,
        gain_one_grad,
        grad_query,
        grad_key,
        grad_value,
        grad_bq,
        grad_bk,
        grad_bv,
        grad_out,
        gain_two_grad,
        router_grad,
        mix_grad,
        grad_sgate,
        grad_sup,
        grad_sdown,
        routed_gate_gradient,
        routed_up_gradient,
        routed_down_gradient,
    )


def solution(mesh):
    placed = (
        P(("dp", "context", "expert"), None),
        P(("dp", "context", "expert"), None),
        P(("dp", "context", "expert"), None),
        P(("dp", "context")),
        P(("dp", "context"), "expert"),
        P(("dp", "context"), "expert"),
        P(("dp", "context"), "expert"),
        P("expert", None),
        P("expert", None),
        P("expert", None),
        P("expert", ("dp", "context")),
        P(("dp", "context")),
        P(("dp", "context"), None),
        P(("dp", "context")),
        P(("dp", "context"), "expert"),
        P(("dp", "context"), "expert"),
        P("expert", ("dp", "context")),
        P(("dp", "expert"), None, None),
        P(("dp", "expert"), None, None),
        P(("dp", "expert"), None, None),
    )
    return jax.shard_map(
        on_device,
        mesh=mesh,
        in_specs=placed,
        out_specs=(
            P(("dp", "context", "expert"), None),
            P(("dp", "context", "expert"), None),
            P(("dp", "context")),
            P(("dp", "context"), "expert"),
            P(("dp", "context"), "expert"),
            P(("dp", "context"), "expert"),
            P("expert", ("dp", "context")),
            P("expert", ("dp", "context")),
            P("expert", ("dp", "context")),
            P("expert", ("dp", "context")),
            P(("dp", "context")),
            P(("dp", "context"), None),
            P(("dp", "context")),
            P(("dp", "context"), "expert"),
            P(("dp", "context"), "expert"),
            P("expert", ("dp", "context")),
            P(("dp", "expert"), "context", None),
            P(("dp", "expert"), "context", None),
            P(("dp", "expert"), None, "context"),
        ),
        check_vma=False,
    )
```

profile of v0, /device:TPU:9, one launch (start us, length us, event | category | flops | bytes accessed | tf_op | source)
XLA Modules:
  0.0 2539.5 jit_solution(13470407484680070528)
XLA Ops:
  10.0 19.3 all-gather
  33.6 51.8 %all-gather.19.cloned.1.call-done = bf16[2048,1024]{1,0:T(8,128)(2,1)} async-done(((bf16[128,1024]{1,0:T(8,128)(2,1)}), bf16[2048,1024]{1,0:T(8,128)(2,1)}) %all-gather.19.cloned.1.call-update) | async-done | bytes 4194320 | tf_op jit(solution)/shard_map/all_gather | solution.py:109
  89.5 47.2 %all-gather.17.cloned.1.call-done = bf16[2048,1024]{1,0:T(8,128)(2,1)} async-done(((bf16[128,1024]{1,0:T(8,128)(2,1)}), bf16[2048,1024]{1,0:T(8,128)(2,1)}) %all-gather.17.cloned.1.call-update) | async-done | bytes 4194320 | tf_op jit(solution)/shard_map/all_gather | solution.py:108
  142.9 44.8 %all-gather.23.cloned.1.call-done = bf16[2048,1024]{1,0:T(8,128)(2,1)} async-done(((bf16[128,1024]{1,0:T(8,128)(2,1)}), bf16[2048,1024]{1,0:T(8,128)(2,1)}) %all-gather.23.cloned.1.call-update) | async-done | bytes 4194320 | tf_op jit(solution)/shard_map/all_gather | solution.py:110
  193.8 17.3 all-gather.21.cloned.1.call-done
  214.2 21.6 all-gather.25.cloned.1.call-done
  243.4 20.7 while.28
  264.0 25.3 all-gather.27.cloned.1.call-done
  297.3 17.9 all-gather.1
  325.2 17.6 all_gather.54
  343.0 14.0 all-reduce.12.cloned.1.call-done
  360.9 7.3 scatter_custom_fusion.1
  383.0 114.3 %all-to-all-done.2 = bf16[8,96,2048]{2,1,0:T(8,128)(2,1)} async-done(((bf16[8,96,2048]{2,1,0:T(8,128)(2,1)}), bf16[8,96,2048]{2,1,0:T(8,128)(2,1)}, u32[]{:S(2)}, u32[]{:S(2)}) %all-to-all-start.2) | async-done | bytes 3145760 | tf_op jit(solution)/shard_map/all_to_all | solution.py:237
  497.3 8.3 all-to-all-start
  505.6 9.7 fusion.48
  515.3 90.2 %all-to-all-done = bf16[8,96,2048]{2,1,0:T(8,128)(2,1)S(1)} async-done(((bf16[8,96,2048]{2,1,0:T(8,128)(2,1)}), bf16[8,96,2048]{2,1,0:T(8,128)(2,1)S(1)}, u32[]{:S(2)}, u32[]{:S(2)}) %all-to-all-start) | async-done | bytes 3145760 | tf_op jit(solution)/shard_map/all_to_all | solution.py:236
  605.5 8.6 fusion.54
  614.2 10.8 multiply_convert_fusion.2
  637.7 86.1 %all-gather.2 = bf16[16,1,128]{2,1,0:T(2,128)(2,1)S(1)} all-gather(bf16[1,1,128]{2,1,0:T(2,128)(2,1)S(1)} %bitcast.302), channel_id=1, replica_groups=mesh['dp'=4,'context'=4,'expert'=2] {'dp','context'}, dimensions={0}, use_global_device_ids=true | all-gather | bytes 4352 | tf_op jit(solution)/shard_map/all_gather | solution.py:116
  725.4 8.0 fusion.52
  733.4 9.3 add_convert_fusion
  742.7 9.3 fusion.124
  752.0 9.6 fusion.125
  766.4 62.7 %all-gather.33.cloned.1.call-done = bf16[2816,2048]{1,0:T(8,128)(2,1)} async-done(((bf16[2816,128]{1,0:T(8,128)(2,1)}), bf16[2816,2048]{1,0:T(8,128)(2,1)}) %all-gather.33.cloned.1.call-update) | async-done | bytes 11534352 | tf_op jit(solution)/shard_map/all_gather | solution.py:114
  829.1 11.8 multiply_convert_fusion.5
  842.0 8.9 fusion.126
  860.1 8.8 convolution_add_fusion.2
  904.2 76.7 %all-reduce.14.cloned.1.call-done = f32[256,2048]{1,0:T(8,128)} async-done(((f32[256,2048]{1,0:T(8,128)}), f32[256,2048]{1,0:T(8,128)}) %all-reduce.14.cloned.1.call-update) | async-done | bytes 2097168 | tf_op jit(solution)/shard_map/psum | solution.py:335
  989.3 54.8 %while.29 = (s32[]{:T(128)}, f32[4,2,256,128]{3,2,1,0:T(8,128)S(1)}, f32[4,2,1024,128]{2,3,1,0:T(8,128)}, f32[4,2,1024,128]{2,3,1,0:T(8,128)}, bf16[4,2,256,128]...) while((s32[]{:T(128)}, ...), condition=%wide.region_26.27_spmd.clone, body=%wide.region_24.26_spmd.clone.sunk | while | flops 676920832 | bytes 41700572 | solution.py:382
  1044.8 9.4 fusion.45
  1054.2 9.2 fusion.46
  1063.6 9.9 fusion.47
  1075.4 13.4 reduce-scatter.20.cloned.1.call-done
  1102.1 33.7 %reduce-scatter.22.cloned.1.call-done = f32[256,1024]{0,1:T(8,128)} async-done(((f32[1024,1024]{0,1:T(8,128)}), f32[256,1024]{0,1:T(8,128)}) %reduce-scatter.22.cloned.1.call-update) | async-done | bytes 1048592 | tf_op jit(solution)/shard_map/reduce_scatter | solution.py:388
  1168.2 9.5 fusion.128
  1179.1 9.5 fusion.129
  1190.2 10.1 fusion.100
  1210.6 40.0 %reduce-scatter.40.cloned.1.call-done = bf16[1,512,1408]{2,1,0:T(8,128)(2,1)} async-done(((bf16[1,2048,1408]{2,1,0:T(8,128)(2,1)}), bf16[1,512,1408]{2,1,0:T(8,128)(2,1)}) %reduce-scatter.40.cloned.1.call-update) | async-done | bytes 1441808 | tf_op jit(solution)/shard_map/reduce_scatter | solution.py:291
  1253.7 54.5 %reduce-scatter.42.cloned.1.call-done = bf16[1,1408,512]{2,1,0:T(8,128)(2,1)} async-done(((bf16[1,1408,2048]{2,1,0:T(8,128)(2,1)}), bf16[1,1408,512]{2,1,0:T(8,128)(2,1)}) %reduce-scatter.42.cloned.1.call-update) | async-done | bytes 1441808 | tf_op jit(solution)/shard_map/reduce_scatter | solution.py:297
  1311.7 38.7 %all-reduce.16.cloned.1.call-done = bf16[256,2048]{1,0:T(8,128)(2,1)} async-done(((bf16[256,2048]{1,0:T(8,128)(2,1)}), bf16[256,2048]{1,0:T(8,128)(2,1)}) %all-reduce.16.cloned.1.call-update) | async-done | bytes 1048592 | tf_op jit(solution)/shard_map/psum | solution.py:412
  1354.4 48.9 %all-reduce.6 = (f32[2048]{0:T(1024)S(1)}, f32[8,128]{1,0:T(8,128)S(1)}, f32[8,128]{1,0:T(8,128)S(1)}, f32[8,128]{1,0:T(8,128)S(1)}, f32[2048]{0:T(1024)S(1)}, /*index=5*/f32[2048]{0:T(1024)S(1)}) all-reduce(f32[2048]{0:T(1024)S(1)} %get-tuple-element.242, ...), channel_id=5, replica_groups=mesh['dp'=4,'context'=4,'expert'=2] {'dp','context'}, use_global_device_ids=true, to_apply=%region_32.33.clone | all-reduce | flops 9216 | bytes 73728
  1413.7 101.0 %reduce-scatter.30.cloned.1.call-done = f32[1024,128]{1,0:T(8,128)} async-done(((f32[1024,2048]{1,0:T(8,128)}), f32[1024,128]{1,0:T(8,128)}) %reduce-scatter.30.cloned.1.call-update) | async-done | bytes 524304 | tf_op jit(solution)/shard_map/reduce_scatter | solution.py:438
  1514.7 109.0 %reduce-scatter.24.cloned.1.call-done = f32[128,1024]{1,0:T(8,128)} async-done(((f32[2048,1024]{1,0:T(8,128)}), f32[128,1024]{1,0:T(8,128)}) %reduce-scatter.24.cloned.1.call-update) | async-done | bytes 524304 | tf_op jit(solution)/shard_map/reduce_scatter | solution.py:435
  1623.7 108.9 %reduce-scatter.26.cloned.1.call-done = f32[128,1024]{1,0:T(8,128)} async-done(((f32[2048,1024]{1,0:T(8,128)}), f32[128,1024]{1,0:T(8,128)}) %reduce-scatter.26.cloned.1.call-update) | async-done | bytes 524304 | tf_op jit(solution)/shard_map/reduce_scatter | solution.py:436
  1732.6 109.0 %reduce-scatter.28.cloned.1.call-done = f32[128,1024]{1,0:T(8,128)} async-done(((f32[2048,1024]{1,0:T(8,128)}), f32[128,1024]{1,0:T(8,128)}) %reduce-scatter.28.cloned.1.call-update) | async-done | bytes 524304 | tf_op jit(solution)/shard_map/reduce_scatter | solution.py:437
  1841.6 229.4 %reduce-scatter.32.cloned.1.call-done = f32[128,2816]{1,0:T(8,128)} async-done(((f32[2048,2816]{1,0:T(8,128)}), f32[128,2816]{1,0:T(8,128)}) %reduce-scatter.32.cloned.1.call-update) | async-done | bytes 1441808 | tf_op jit(solution)/shard_map/reduce_scatter | solution.py:439
  2071.0 230.5 %reduce-scatter.34.cloned.1.call-done = f32[128,2816]{1,0:T(8,128)} async-done(((f32[2048,2816]{1,0:T(8,128)}), f32[128,2816]{1,0:T(8,128)}) %reduce-scatter.34.cloned.1.call-update) | async-done | bytes 1441808 | tf_op jit(solution)/shard_map/reduce_scatter | solution.py:440
  2301.5 230.7 %reduce-scatter.36.cloned.1.call-done = f32[2816,128]{1,0:T(8,128)} async-done(((f32[2816,2048]{1,0:T(8,128)}), f32[2816,128]{1,0:T(8,128)}) %reduce-scatter.36.cloned.1.call-update) | async-done | bytes 1441808 | tf_op jit(solution)/shard_map/reduce_scatter | solution.py:441
  (413 shorter events, 299.5 us)
Async XLA Ops:
  7.2 24.9 all-gather.15.cloned.1.call-start
  7.9 77.5 %all-gather.19.cloned.1.call-start = ((), (), s32[]{:S(2)}) async-start(), calls=%async_computation.20 | async-start | bytes 4456448 | tf_op jit(solution)/shard_map/all_gather | solution.py:109
  8.7 128.0 %all-gather.17.cloned.1.call-start = ((), (), s32[]{:S(2)}) async-start(), calls=%async_computation.19 | async-start | bytes 4456448 | tf_op jit(solution)/shard_map/all_gather | solution.py:108
  9.4 178.4 %all-gather.23.cloned.1.call-start = ((), (), s32[]{:S(2)}) async-start(), calls=%async_computation.22 | async-start | bytes 4456448 | tf_op jit(solution)/shard_map/all_gather | solution.py:110
  10.0 201.1 %all-gather.21.cloned.1.call-start = ((), (), s32[]{:S(2)}) async-start(), calls=%async_computation.21 | async-start | bytes 2621440 | tf_op jit(solution)/shard_map/all_gather | solution.py:158
  29.4 158.4 %copy-start.39 = (f32[16,1,128]{2,1,0:T(1,128)}, f32[16,1,128]{2,1,0:T(1,128)S(1)}, u32[]{:S(2)}) copy-start(f32[16,1,128]{2,1,0:T(1,128)S(1)} %convert_element_type.252) | copy-start | bytes 24580
  31.3 109.0 %copy-start.35 = (f32[256,64]{1,0:T(8,128)}, f32[256,64]{1,0:T(8,128)S(1)}, u32[]{:S(2)}) copy-start(f32[256,64]{1,0:T(8,128)S(1)} %get-tuple-element.326) | copy-start | bytes 196612
  31.4 109.0 %copy-start.37 = (f32[256,64]{1,0:T(8,128)}, f32[256,64]{1,0:T(8,128)S(1)}, u32[]{:S(2)}) copy-start(f32[256,64]{1,0:T(8,128)S(1)} %get-tuple-element.327) | copy-start | bytes 196612
  33.6 154.2 %copy-start.47 = (f32[256]{0:T(256)}, f32[256]{0:T(256)S(1)}, u32[]{:S(2)}) copy-start(f32[256]{0:T(256)S(1)} %add_rsqrt_fusion.1) | copy-start | bytes 3076
  85.4 51.3 %copy-start = (bf16[256,2048]{1,0:T(8,128)(2,1)S(1)}, bf16[256,2048]{1,0:T(8,128)(2,1)}, u32[]{:S(2)}) copy-start(bf16[256,2048]{1,0:T(8,128)(2,1)} %all-gather.15.cloned.1.call-done) | copy-start | bytes 3145732
  142.9 92.8 %all-gather.25.cloned.1.call-start = ((), (), s32[]{:S(2)}) async-start(), calls=%async_computation.23 | async-start | bytes 2621440 | tf_op jit(solution)/shard_map/all_gather | solution.py:159
  192.1 97.2 %all-gather.27.cloned.1.call-start = ((), (), s32[]{:S(2)}) async-start(), calls=%async_computation.24 | async-start | bytes 4456448 | tf_op jit(solution)/shard_map/all_gather | solution.py:111
  192.8 164.1 %all-reduce.12.cloned.1.call-start = ((), (), s32[]{:S(2)}) async-start(), calls=%async_computation.25 | async-start | bytes 4194304 | tf_op jit(solution)/shard_map/psum | solution.py:182
  264.0 30.2 %copy-start.7 = (bf16[4,2,1024,128]{3,2,1,0:T(8,128)(2,1)}, bf16[4,2,1024,128]{3,2,1,0:T(8,128)(2,1)S(1)}, u32[]{:S(2)}) copy-start(bf16[4,2,1024,128]{3,2,1,0:T(8,128)(2,1)S(1)} %get-tuple-element.563) | copy-start | bytes 6291460
  264.0 30.2 %copy-start.43 = (s32[1024]{0:T(1024)}, s32[1024]{0:T(1024)S(1)}, u32[]{:S(2)}) copy-start(s32[1024]{0:T(1024)S(1)} %get-tuple-element.618) | copy-start | bytes 12292
  264.0 30.2 %copy-start.45 = (s32[256]{0:T(256)}, s32[256]{0:T(256)S(1)}, u32[]{:S(2)}) copy-start(s32[256]{0:T(256)S(1)} %get-tuple-element.629) | copy-start | bytes 3076
  294.3 448.4 %all-gather.29.cloned.1.call-start = ((), (), s32[]{:S(2)}) async-start(), calls=%async_computation.26 | async-start | bytes 12255232 | tf_op jit(solution)/shard_map/all_gather | solution.py:112
  295.0 457.0 %all-gather.31.cloned.1.call-start = ((), (), s32[]{:S(2)}) async-start(), calls=%async_computation.27 | async-start | bytes 12255232 | tf_op jit(solution)/shard_map/all_gather | solution.py:113
  295.6 470.7 %all-gather.35.cloned.1.call-start = ((), (), s32[]{:S(2)}) async-start(), calls=%async_computation.30 | async-start | bytes 1572864 | tf_op jit(solution)/shard_map/all_gather | solution.py:122
  296.4 532.7 %all-gather.33.cloned.1.call-start = ((), (), s32[]{:S(2)}) async-start(), calls=%async_computation.28 | async-start | bytes 12255232 | tf_op jit(solution)/shard_map/all_gather | solution.py:114
  368.2 129.0 %all-to-all-start.2 = ((bf16[8,96,2048]{2,1,0:T(8,128)(2,1)}), bf16[8,96,2048]{2,1,0:T(8,128)(2,1)}, u32[]{:S(2)}, u32[]{:S(2)}) async-start(bf16[8,96,2048]{2,1,0:T(8,128)(2,1)} %bitcast.261), calls=%async_computation.3 | async-start | bytes 6291456 | tf_op jit(solution)/shard_map/all_to_all | solution.py:237
  497.3 108.2 %all-to-all-start = ((bf16[8,96,2048]{2,1,0:T(8,128)(2,1)}), bf16[8,96,2048]{2,1,0:T(8,128)(2,1)S(1)}, u32[]{:S(2)}, u32[]{:S(2)}) async-start(bf16[8,96,2048]{2,1,0:T(8,128)(2,1)} %bitcast.19), calls=%async_computation | async-start | bytes 6291456 | tf_op jit(solution)/shard_map/all_to_all | solution.py:236
  631.5 130.2 %all-to-all-start.1 = ((bf16[8,96,2048]{2,1,0:T(8,128)(2,1)}), bf16[8,96,2048]{2,1,0:T(8,128)(2,1)S(1)}, u32[]{:S(2)}, u32[]{:S(2)}) async-start(bf16[8,96,2048]{2,1,0:T(8,128)(2,1)} %bitcast.275), calls=%async_computation.1 | async-start | bytes 6291456 | tf_op jit(solution)/shard_map/all_to_all | solution.py:251
  725.4 175.0 %copy-start.52 = (f32[256]{0:T(256)}, f32[256]{0:T(256)S(1)}, u32[]{:S(2)}) copy-start(f32[256]{0:T(256)S(1)} %add_divide_fusion.2) | copy-start | bytes 3076
  761.6 115.3 %all-to-all-start.3 = ((bf16[8,96,2048]{2,1,0:T(8,128)(2,1)}), bf16[8,96,2048]{2,1,0:T(8,128)(2,1)}, u32[]{:S(2)}, u32[]{:S(2)}) async-start(bf16[8,96,2048]{2,1,0:T(8,128)(2,1)} %bitcast.274), calls=%async_computation.4 | async-start | bytes 6291456 | tf_op jit(solution)/shard_map/all_to_all | solution.py:258
  766.1 132.8 %reduce-scatter.18.cloned.1.call-start = ((), (), s32[]{:S(2)}) async-start(), calls=%async_computation.29 | async-start | bytes 3145728 | tf_op jit(solution)/shard_map/reduce_scatter | solution.py:193
  851.0 129.9 %all-reduce.14.cloned.1.call-start = ((), (), s32[]{:S(2)}) async-start(), calls=%async_computation.31 | async-start | bytes 4194304 | tf_op jit(solution)/shard_map/psum | solution.py:335
  901.0 79.9 %copy-start.3 = (f32[256,2048]{1,0:T(8,128)S(1)}, f32[256,2048]{1,0:T(8,128)}, u32[]{:S(2)}) copy-start(f32[256,2048]{1,0:T(8,128)} %copy-done.2) | copy-start | bytes 6291460
  904.1 79.7 %copy-start.19 = (bf16[256,2048]{1,0:T(8,128)(2,1)S(1)}, bf16[256,2048]{1,0:T(8,128)(2,1)}, u32[]{:S(2)}) copy-start(bf16[256,2048]{1,0:T(8,128)(2,1)} %all-gather.35.cloned.1.call-done) | copy-start | bytes 3145732
  904.1 184.7 %reduce-scatter.20.cloned.1.call-start = ((), (), s32[]{:S(2)}) async-start(), calls=%async_computation.32 | async-start | bytes 5242880 | tf_op jit(solution)/shard_map/reduce_scatter | solution.py:387
  1044.2 91.6 %reduce-scatter.22.cloned.1.call-start = ((), (), s32[]{:S(2)}) async-start(), calls=%async_computation.33 | async-start | bytes 5242880 | tf_op jit(solution)/shard_map/reduce_scatter | solution.py:388
  1044.7 162.6 %reduce-scatter.38.cloned.1.call-start = ((), (), s32[]{:S(2)}) async-start(), calls=%async_computation.42 | async-start | bytes 7208960 | tf_op jit(solution)/shard_map/reduce_scatter | solution.py:285
  1054.2 196.4 %reduce-scatter.40.cloned.1.call-start = ((), (), s32[]{:S(2)}) async-start(), calls=%async_computation.43 | async-start | bytes 7208960 | tf_op jit(solution)/shard_map/reduce_scatter | solution.py:291
  1063.5 244.6 %reduce-scatter.42.cloned.1.call-start = ((), (), s32[]{:S(2)}) async-start(), calls=%async_computation.44 | async-start | bytes 7208960 | tf_op jit(solution)/shard_map/reduce_scatter | solution.py:297
  1073.5 276.9 %all-reduce.16.cloned.1.call-start = ((), (), s32[]{:S(2)}) async-start(), calls=%async_computation.34 | async-start | bytes 2097152 | tf_op jit(solution)/shard_map/psum | solution.py:412
  1102.1 39.4 %copy-start.13 = (bf16[128,2048]{1,0:T(8,128)(2,1)S(1)}, bf16[128,2048]{1,0:T(8,128)(2,1)}, u32[]{:S(2)}) copy-start(bf16[128,2048]{1,0:T(8,128)(2,1)} %copy-done.12) | copy-start | bytes 1572868
  1141.4 263.1 %reduce-scatter.44.cloned.1.call-start = ((), (), s32[]{:S(2)}) async-start(), calls=%async_computation.45 | async-start | bytes 69632 | tf_op jit(solution)/shard_map/reduce_scatter | solution.py:442
  1142.4 372.2 %reduce-scatter.30.cloned.1.call-start = ((), (), s32[]{:S(2)}) async-start(), calls=%async_computation.38 | async-start | bytes 8912896 | tf_op jit(solution)/shard_map/reduce_scatter | solution.py:438
  1149.1 474.6 %reduce-scatter.24.cloned.1.call-start = ((), (), s32[]{:S(2)}) async-start(), calls=%async_computation.35 | async-start | bytes 8912896 | tf_op jit(solution)/shard_map/reduce_scatter | solution.py:435
  1155.4 577.2 %reduce-scatter.26.cloned.1.call-start = ((), (), s32[]{:S(2)}) async-start(), calls=%async_computation.36 | async-start | bytes 8912896 | tf_op jit(solution)/shard_map/reduce_scatter | solution.py:436
  1160.6 681.0 %reduce-scatter.28.cloned.1.call-start = ((), (), s32[]{:S(2)}) async-start(), calls=%async_computation.37 | async-start | bytes 8912896 | tf_op jit(solution)/shard_map/reduce_scatter | solution.py:437
  1166.6 904.4 %reduce-scatter.32.cloned.1.call-start = ((), (), s32[]{:S(2)}) async-start(), calls=%async_computation.39 | async-start | bytes 24510464 | tf_op jit(solution)/shard_map/reduce_scatter | solution.py:439
  1177.7 1123.8 %reduce-scatter.34.cloned.1.call-start = ((), (), s32[]{:S(2)}) async-start(), calls=%async_computation.40 | async-start | bytes 24510464 | tf_op jit(solution)/shard_map/reduce_scatter | solution.py:440
  1188.5 1343.6 %reduce-scatter.36.cloned.1.call-start = ((), (), s32[]{:S(2)}) async-start(), calls=%async_computation.41 | async-start | bytes 24510464 | tf_op jit(solution)/shard_map/reduce_scatter | solution.py:441
  1253.7 57.8 %copy-start.15 = (f32[256,1024]{0,1:T(8,128)S(1)}, f32[256,1024]{0,1:T(8,128)}, u32[]{:S(2)}) copy-start(f32[256,1024]{0,1:T(8,128)} %reduce-scatter.22.cloned.1.call-done) | copy-start | bytes 3145732
  1311.7 42.7 %copy-start.49 = (f32[2048]{0:T(1024)S(1)}, f32[2048]{0:T(1024)}, u32[]{:S(2)}) copy-start(f32[2048]{0:T(1024)} %get-tuple-element.238) | copy-start | bytes 24580
  1311.7 42.7 %copy-start.51 = (f32[8,128]{1,0:T(8,128)S(1)}, f32[8,128]{1,0:T(8,128)}, u32[]{:S(2)}) copy-start(f32[8,128]{1,0:T(8,128)} %get-tuple-element.290) | copy-start | bytes 12292
  1311.7 99.4 %copy-start.11 = (f32[256,2048]{1,0:T(8,128)S(1)}, f32[256,2048]{1,0:T(8,128)}, u32[]{:S(2)}) copy-start(f32[256,2048]{1,0:T(8,128)} %copy-done.9) | copy-start | bytes 6291460
  (67 other events, 242.9 us)
Sparse Core Ops, SparseCore 0:
  9.6 22.4 all-gather.14
  34.2 51.1 all-gather.18
  87.6 49.0 all-gather.16
  138.7 49.0 all-gather.22
  189.8 21.3 all-gather.20
  213.1 22.5 all-gather.24
  237.9 51.3 all-gather.26
  294.4 62.5 all-reduce.11
  359.5 147.6 all-gather.28
  509.6 146.7 all-gather.30
  658.0 49.3 all-gather.34
  709.6 119.4 all-gather.32
  851.1 45.5 reduce-scatter.17
  904.2 76.6 all-reduce.13
  1044.3 44.5 reduce-scatter.19
  1091.2 44.5 reduce-scatter.21
  1138.3 54.8 reduce-scatter.37
  1195.6 54.8 reduce-scatter.39
  1253.2 54.8 reduce-scatter.41
  1310.3 40.0 all-reduce.15
  1354.1 49.5 reduce-scatter.43
  1408.4 106.2 reduce-scatter.29
  1519.3 104.3 reduce-scatter.23
  1628.2 104.3 reduce-scatter.25
  1737.2 104.3 reduce-scatter.27
  1846.1 224.8 reduce-scatter.31
  2075.5 225.9 reduce-scatter.33
  2306.2 225.9 reduce-scatter.35
where the time goes:
time: 2550 us; the launch traced here: 2540 us
  waiting for transfers between devices  1870 us (73%)
  matrix products  271 us (11%)
  blocking collectives  194 us (8%)
  local copies, waits for them, and re-layouts  92.3 us (4%)
  other arithmetic  67 us (3%)
  starting transfers between devices  25.6 us (1%)
    reduce_scatter x1, waiting for transfers between devices, on_device(): lax.psum_scatter(grad_sdown, ('dp', 'context'), scatter_dimension=1, tile...  231 us
    reduce_scatter x1, waiting for transfers between devices, on_device(): lax.psum_scatter(grad_sup, ('dp', 'context'), scatter_dimension=0, tiled=...  231 us
    reduce_scatter x1, waiting for transfers between devices, on_device(): lax.psum_scatter(grad_sgate, ('dp', 'context'), scatter_dimension=0, tile...  229 us
    all_to_all x1, waiting for transfers between devices, on_device(): lax.all_to_all(send_grads, ('dp', 'expert'), split_axis=0, concat_axis=0,...  114 us
    reduce_scatter x1, waiting for transfers between devices, on_device(): lax.psum_scatter(grad_value, ('dp', 'context'), scatter_dimension=0, tile...  109 us
    reduce_scatter x1, waiting for transfers between devices, on_device(): lax.psum_scatter(grad_query, ('dp', 'context'), scatter_dimension=0, tile...  109 us
    reduce_scatter x1, waiting for transfers between devices, on_device(): lax.psum_scatter(grad_key, ('dp', 'context'), scatter_dimension=0, tiled=...  109 us
    reduce_scatter x1, waiting for transfers between devices, on_device(): lax.psum_scatter(grad_out, ('dp', 'context'), scatter_dimension=1, tiled=...  101 us
  transfers between devices with their start and end apart: 32, of which 24 were waited for; matrix products, arithmetic and copies ran while one was open for 14% of the time, Pallas kernels for 0%

commit v1 on v0

--- a/solution.py
+++ b/solution.py
@@ -3,8 +3,11 @@
 import jax
 import jax.numpy as jnp
 from jax import lax
+from jax.experimental import pallas as pl
+from jax.experimental.pallas import tpu as pltpu
 from jax.sharding import PartitionSpec as P
 
+DP, CONTEXT, EXPERT = "dp", "context", "expert"
 BLOCK = 256
 CAP = 96
 
@@ -60,7 +63,7 @@
     return jnp.dot(left, right.T, preferred_element_type=jnp.float32)
 
 
-def on_device(
+def weights_plan(
     tokens,
     out_grad,
     expert_ids,
@@ -84,9 +87,9 @@
 ):
     tok_rows = tokens.shape[0]
     width = tokens.shape[1]
-    my_half = lax.axis_index("expert")
-    my_piece = lax.axis_index("context")
-    n_pieces = lax.axis_size("context")
+    my_half = lax.axis_index(EXPERT)
+    my_piece = lax.axis_index(CONTEXT)
+    n_pieces = lax.axis_size(CONTEXT)
     local_heads = query_bias_heads.shape[0]
     head_dim = query_bias_heads.shape[1]
     group_size = 2
@@ -105,21 +108,21 @@
         full_gain_one,
         full_gain_two,
     ) = (
-        lax.all_gather(w_query, ("dp", "context"), axis=0, tiled=True),
-        lax.all_gather(w_key, ("dp", "context"), axis=0, tiled=True),
-        lax.all_gather(w_value, ("dp", "context"), axis=0, tiled=True),
-        lax.all_gather(w_out, ("dp", "context"), axis=1, tiled=True),
-        lax.all_gather(shared_in_gate, ("dp", "context"), axis=0, tiled=True),
-        lax.all_gather(shared_in_up, ("dp", "context"), axis=0, tiled=True),
-        lax.all_gather(shared_down, ("dp", "context"), axis=1, tiled=True),
-        lax.all_gather(w_router, ("dp", "context"), axis=0, tiled=True),
-        lax.all_gather(shared_mix, ("dp", "context"), axis=0, tiled=True),
-        lax.all_gather(norm1_gain, ("dp", "context"), axis=0, tiled=True),
-        lax.all_gather(norm2_gain, ("dp", "context"), axis=0, tiled=True),
+        lax.all_gather(w_query, (DP, CONTEXT), axis=0, tiled=True),
+        lax.all_gather(w_key, (DP, CONTEXT), axis=0, tiled=True),
+        lax.all_gather(w_value, (DP, CONTEXT), axis=0, tiled=True),
+        lax.all_gather(w_out, (DP, CONTEXT), axis=1, tiled=True),
+        lax.all_gather(shared_in_gate, (DP, CONTEXT), axis=0, tiled=True),
+        lax.all_gather(shared_in_up, (DP, CONTEXT), axis=0, tiled=True),
+        lax.all_gather(shared_down, (DP, CONTEXT), axis=1, tiled=True),
+        lax.all_gather(w_router, (DP, CONTEXT), axis=0, tiled=True),
+        lax.all_gather(shared_mix, (DP, CONTEXT), axis=0, tiled=True),
+        lax.all_gather(norm1_gain, (DP, CONTEXT), axis=0, tiled=True),
+        lax.all_gather(norm2_gain, (DP, CONTEXT), axis=0, tiled=True),
     )
     x_piece, dy_piece = (
-        lax.all_gather(tokens, "expert", axis=0, tiled=True),
-        lax.all_gather(out_grad, "expert", axis=0, tiled=True),
+        lax.all_gather(tokens, EXPERT, axis=0, tiled=True),
+        lax.all_gather(out_grad, EXPERT, axis=0, tiled=True),
     )
     piece_rows = x_piece.shape[0]
     seq_len = piece_rows * n_pieces
@@ -155,8 +158,8 @@
     )
     v_low = v_pre.astype(jnp.bfloat16)
     keys_all, values_all = (
-        lax.all_gather(k_rot, "context", axis=0, tiled=True),
-        lax.all_gather(v_low, "context", axis=0, tiled=True),
+        lax.all_gather(k_rot, CONTEXT, axis=0, tiled=True),
+        lax.all_gather(v_low, CONTEXT, axis=0, tiled=True),
     )
     query_grp = to_groups(q_rot, groups, group_size, head_dim)
     keys_grp = to_groups(keys_all, groups, group_size, head_dim)
@@ -179,7 +182,7 @@
     attn_grp, lse_grp = lax.map(attend_group, (query_grp, keys_grp, values_grp))
     attn_low = from_groups(attn_grp).astype(jnp.bfloat16)
     out_partial = jnp.dot(attn_low, full_out, preferred_element_type=jnp.float32)
-    out_full = lax.psum(out_partial, "expert")
+    out_full = lax.psum(out_partial, EXPERT)
     hidden_one = x_float + out_full
     rstd_two = lax.rsqrt(jnp.mean(hidden_one * hidden_one, axis=1, keepdims=True) + EPS)
     normed_two = hidden_one * rstd_two
@@ -192,7 +195,7 @@
     s_hidden = (s_silu * s_up).astype(jnp.bfloat16)
     shared_own = lax.psum_scatter(
         jnp.dot(s_hidden, full_sdown, preferred_element_type=jnp.float32),
-        "expert",
+        EXPERT,
         scatter_dimension=0,
         tiled=True,
     )
@@ -233,8 +236,8 @@
     gate_weight = expert_gate[0]
     up_weight = expert_up[0]
     down_weight = expert_down[0]
-    rows_in = lax.all_to_all(send_rows, ("dp", "expert"), split_axis=0, concat_axis=0, tiled=True)
-    grads_in = lax.all_to_all(send_grads, ("dp", "expert"), split_axis=0, concat_axis=0, tiled=True)
+    rows_in = lax.all_to_all(send_rows, (DP, EXPERT), split_axis=0, concat_axis=0, tiled=True)
+    grads_in = lax.all_to_all(send_grads, (DP, EXPERT), split_axis=0, concat_axis=0, tiled=True)
     sources = rows_in.shape[0]
     items = rows_in.shape[1]
     flat_in = rows_in.reshape(-1, width)
@@ -250,14 +253,14 @@
     d_in = (mat_right(d_gate, gate_weight) + mat_right(d_up, up_weight)).astype(jnp.bfloat16)
     back_out = lax.all_to_all(
         e_out.reshape(sources, items, width),
-        ("dp", "expert"),
+        (DP, EXPERT),
         split_axis=0,
         concat_axis=0,
         tiled=True,
     )
     back_in = lax.all_to_all(
         d_in.reshape(sources, items, width),
-        ("dp", "expert"),
+        (DP, EXPERT),
         split_axis=0,
         concat_axis=0,
         tiled=True,
@@ -284,19 +287,19 @@
     routed_gate_gradient, routed_up_gradient, routed_down_gradient = (
         lax.psum_scatter(
             routed_gate_gradient[None].astype(jnp.bfloat16),
-            "context",
+            CONTEXT,
             scatter_dimension=1,
             tiled=True,
         ).astype(jnp.float32),
         lax.psum_scatter(
             routed_up_gradient[None].astype(jnp.bfloat16),
-            "context",
+            CONTEXT,
             scatter_dimension=1,
             tiled=True,
         ).astype(jnp.float32),
         lax.psum_scatter(
             routed_down_gradient[None].astype(jnp.bfloat16),
-            "context",
+            CONTEXT,
             scatter_dimension=2,
             tiled=True,
         ).astype(jnp.float32),
@@ -332,7 +335,7 @@
         own_start,
         0,
     )
-    d_moe_in, router_grad, mix_grad = lax.psum((d_in_part, router_part, mix_part), "expert")
+    d_moe_in, router_grad, mix_grad = lax.psum((d_in_part, router_part, mix_part), EXPERT)
     d_norm_two = d_moe_in * gain_two
     gain_two_grad = jnp.sum(d_moe_in * normed_two, axis=0)
     d_hidden_one = dy_float + rstd_two * (
@@ -384,8 +387,8 @@
     )
     d_query = from_groups(dq_grp)
     d_key_own, d_value_own = (
-        lax.psum_scatter(from_groups(dk_grp), "context", scatter_dimension=0, tiled=True),
-        lax.psum_scatter(from_groups(dv_grp), "context", scatter_dimension=0, tiled=True),
+        lax.psum_scatter(from_groups(dk_grp), CONTEXT, scatter_dimension=0, tiled=True),
+        lax.psum_scatter(from_groups(dv_grp), CONTEXT, scatter_dimension=0, tiled=True),
     )
     d_q_pre = (
         rotate_back(d_query.reshape(piece_rows, local_heads, head_dim), cosine, sine)
@@ -409,7 +412,7 @@
         + mat_right(d_k_pre, full_key)
         + mat_right(d_v_pre, full_value)
     )
-    d_attn_in = lax.psum(d_attn_in.astype(jnp.bfloat16), "expert").astype(jnp.float32)
+    d_attn_in = lax.psum(d_attn_in.astype(jnp.bfloat16), EXPERT).astype(jnp.float32)
     d_norm_one = d_attn_in * gain_one
     gain_one_grad = jnp.sum(d_attn_in * normed_one, axis=0)
     d_x = d_hidden_one + rstd_one * (
@@ -432,20 +435,20 @@
         grad_bk,
         grad_bv,
     ) = (
-        lax.psum_scatter(grad_query, ("dp", "context"), scatter_dimension=0, tiled=True),
-        lax.psum_scatter(grad_key, ("dp", "context"), scatter_dimension=0, tiled=True),
-        lax.psum_scatter(grad_value, ("dp", "context"), scatter_dimension=0, tiled=True),
-        lax.psum_scatter(grad_out, ("dp", "context"), scatter_dimension=1, tiled=True),
-        lax.psum_scatter(grad_sgate, ("dp", "context"), scatter_dimension=0, tiled=True),
-        lax.psum_scatter(grad_sup, ("dp", "context"), scatter_dimension=0, tiled=True),
-        lax.psum_scatter(grad_sdown, ("dp", "context"), scatter_dimension=1, tiled=True),
-        lax.psum_scatter(router_grad, ("dp", "context"), scatter_dimension=0, tiled=True),
-        lax.psum_scatter(mix_grad, ("dp", "context"), scatter_dimension=0, tiled=True),
-        lax.psum_scatter(gain_one_grad, ("dp", "context"), scatter_dimension=0, tiled=True),
-        lax.psum_scatter(gain_two_grad, ("dp", "context"), scatter_dimension=0, tiled=True),
-        lax.psum_scatter(grad_bq, ("dp", "context"), scatter_dimension=1, tiled=True),
-        lax.psum_scatter(grad_bk, ("dp", "context"), scatter_dimension=1, tiled=True),
-        lax.psum_scatter(grad_bv, ("dp", "context"), scatter_dimension=1, tiled=True),
+        lax.psum_scatter(grad_query, (DP, CONTEXT), scatter_dimension=0, tiled=True),
+        lax.psum_scatter(grad_key, (DP, CONTEXT), scatter_dimension=0, tiled=True),
+        lax.psum_scatter(grad_value, (DP, CONTEXT), scatter_dimension=0, tiled=True),
+        lax.psum_scatter(grad_out, (DP, CONTEXT), scatter_dimension=1, tiled=True),
+        lax.psum_scatter(grad_sgate, (DP, CONTEXT), scatter_dimension=0, tiled=True),
+        lax.psum_scatter(grad_sup, (DP, CONTEXT), scatter_dimension=0, tiled=True),
+        lax.psum_scatter(grad_sdown, (DP, CONTEXT), scatter_dimension=1, tiled=True),
+        lax.psum_scatter(router_grad, (DP, CONTEXT), scatter_dimension=0, tiled=True),
+        lax.psum_scatter(mix_grad, (DP, CONTEXT), scatter_dimension=0, tiled=True),
+        lax.psum_scatter(gain_one_grad, (DP, CONTEXT), scatter_dimension=0, tiled=True),
+        lax.psum_scatter(gain_two_grad, (DP, CONTEXT), scatter_dimension=0, tiled=True),
+        lax.psum_scatter(grad_bq, (DP, CONTEXT), scatter_dimension=1, tiled=True),
+        lax.psum_scatter(grad_bk, (DP, CONTEXT), scatter_dimension=1, tiled=True),
+        lax.psum_scatter(grad_bv, (DP, CONTEXT), scatter_dimension=1, tiled=True),
     )
     return (
         mixed,
@@ -470,53 +473,931 @@
     )
 
 
+def dot_f32(left, right, left_dim, right_dim):
+    return lax.dot_general(
+        left, right, (((left_dim,), (right_dim,)), ((), ())), preferred_element_type=jnp.float32
+    )
+
+
+def whole_vmem(count):
+    return [pl.BlockSpec(memory_space=pltpu.VMEM)] * count
+
+
+def like(shape, dtype):
+    return jax.ShapeDtypeStruct(shape, dtype)
+
+
+MESH_ID = pl.DeviceIdType.MESH
+
+
+class Wire:
+    def __init__(self, send, recv):
+        self.send = send
+        self.recv = recv
+        self.sent = 0
+        self.received = 0
+        self.own = []
+
+    def copy(self, src, dst, device):
+        out = self.copy_to(src, dst, device, self.take(1), self.take_send(1))
+        self.own.append(out)
+        return out
+
+    def take(self, count):
+        self.received += count
+        assert self.received <= self.recv.shape[0], self.received
+        return self.received - count
+
+    def take_send(self, count):
+        self.sent += count
+        assert self.sent <= self.send.shape[0], self.sent
+        return self.sent - count
+
+    def copy_to(self, src, dst, device, recv_slot, send_slot):
+        return pltpu.make_async_remote_copy(
+            src_ref=src,
+            dst_ref=dst,
+            send_sem=self.send.at[send_slot],
+            recv_sem=self.recv.at[recv_slot],
+            device_id=device,
+            device_id_type=MESH_ID,
+        )
+
+    def drain(self):
+        for item in self.own:
+            item.wait_send()
+        self.own = []
+
+
+class Local:
+    def __init__(self, sems):
+        self.sems = sems
+        self.count = 0
+
+    def start(self, src, dst):
+        assert self.count < self.sems.shape[0], self.count
+        item = pltpu.make_async_copy(src, dst, self.sems.at[self.count])
+        self.count += 1
+        item.start()
+        return item
+
+
+class Place:
+    def __init__(self, n_dp):
+        self.n_dp = n_dp
+        self.z = lax.axis_index(DP)
+        self.c = lax.axis_index(CONTEXT)
+        self.y = lax.axis_index(EXPERT)
+        self.cx = lax.bitwise_xor(self.c, jnp.int32(2))
+        self.cs = lax.bitwise_xor(self.c, jnp.int32(1))
+        self.cd = lax.bitwise_xor(self.c, jnp.int32(3))
+        self.yn = lax.bitwise_xor(self.y, jnp.int32(1))
+        self.core = (self.z, self.cs, self.y)
+        self.over_x = (self.z, self.cx, self.y)
+        self.over_y = (self.z, self.c, self.yn)
+        self.up = (self.z + 1, self.c, self.y)
+        self.down = (self.z - 1, self.c, self.y)
+
+    def block(self, c, y):
+        return c * 2 + y
+
+
+def barrier(devices):
+    sem = pltpu.get_barrier_semaphore()
+    for device in devices:
+        pl.semaphore_signal(sem, inc=1, device_id=device, device_id_type=MESH_ID)
+    pl.semaphore_wait(sem, len(devices))
+
+
+def rows_of(index, count):
+    return pl.ds(pl.multiple_of(index * count, count), count)
+
+
+def by_rows(total, step, body):
+    def one(index, carry):
+        body(rows_of(index, step))
+        return carry
+
+    lax.fori_loop(0, total // step, one, 0)
+
+
+def chain_gather(wire, place, refs, arrived=None):
+    n = place.n_dp
+    z = place.z
+    width = len(refs(z))
+    recv = wire.take(n * width)
+    send = wire.take_send(2 * n * width)
+
+    def copies(slot, up, dist):
+        return [
+            wire.copy_to(
+                ref,
+                ref,
+                place.up if up else place.down,
+                recv + slot * width + index,
+                send + (2 * dist + (0 if up else 1)) * width + index,
+            )
+            for index, ref in enumerate(refs(slot))
+        ]
+
+    def start(slot, up, dist):
+        for item in copies(slot, up, dist):
+            item.start()
+
+    def land(slot, up, dist):
+        for item in copies(slot, up, dist):
+            item.wait_recv()
+        if arrived is not None:
+            arrived(slot)
+
+    def sent(slot, up, dist):
+        for item in copies(slot, up, dist):
+            item.wait_send()
+
+    pl.when(z < n - 1)(lambda: start(z, True, 0))
+    pl.when(z > 0)(lambda: start(z, False, 0))
+    yield
+    for dist in range(1, n):
+        below, above = z - dist, z + dist
+
+        @pl.when(below >= 0)
+        def _():
+            land(below, True, dist)
+            pl.when(z < n - 1)(lambda: start(below, True, dist))
+
+        @pl.when(above < n)
+        def _():
+            land(above, False, dist)
+            pl.when(z > 0)(lambda: start(above, False, dist))
+
+        yield
+    for dist in range(n):
+        below, above = z - dist, z + dist
+        pl.when((below >= 0) & (z < n - 1))(lambda: sent(below, True, dist))
+        pl.when((above < n) & (z > 0))(lambda: sent(above, False, dist))
+
+
+def finish(*steps):
+    for step in steps:
+        for _ in step:
+            pass
+
+
+def plane_gather(wire, place, buf):
+    rows = buf.shape[0] // 8
+    half = buf.shape[1] // 2
+    left, right = pl.ds(0, half), pl.ds(half, half)
+    own = rows_of(place.block(place.c, place.y), rows)
+    from_x = rows_of(place.block(place.cx, place.y), rows)
+    from_y = rows_of(place.block(place.c, place.yn), rows)
+    across = rows_of(place.block(place.cx, place.yn), rows)
+
+    def go(where, lanes, device):
+        ref = buf.at[where, lanes] if lanes is not None else buf.at[where, :]
+        item = wire.copy(ref, ref, device)
+        item.start()
+        return item
+
+    x_left = go(own, left, place.over_x)
+    y_right = go(own, right, place.over_y)
+    x_right = go(own, right, place.over_x)
+    y_left = go(own, left, place.over_y)
+    waits = [go(own, None, place.core)]
+    yield
+    x_left.wait_recv()
+    far_left = go(from_x, left, place.over_y)
+    y_right.wait_recv()
+    far_right = go(from_y, right, place.over_x)
+    yield
+    x_right.wait_recv()
+    waits.append(go(from_x, None, place.core))
+    y_left.wait_recv()
+    waits.append(go(from_y, None, place.core))
+    yield
+    far_left.wait_recv()
+    far_right.wait_recv()
+    waits.append(go(across, None, place.core))
+    for item in waits:
+        item.wait_recv()
+
+
+def add_into(target, lanes, rows, extra):
+    count = extra.shape[0]
+    step = 16
+
+    def one(index, carry):
+        here = pl.ds(pl.multiple_of(rows + index * step, step), step)
+        there = rows_of(index, step)
+        total = target[here, lanes].astype(jnp.float32) + extra[there, :].astype(jnp.float32)
+        target[here, lanes] = total.astype(target.dtype)
+        return carry
+
+    lax.fori_loop(0, count // step, one, 0)
+
+
+def plane_reduce(wire, place, part, got_core, got_one, got_two):
+    rows = part.shape[0] // 8
+    half = part.shape[1] // 2
+    left, right = pl.ds(0, half), pl.ds(half, half)
+    chips = ((place.cx, place.yn), (place.cx, place.y), (place.c, place.yn), (place.c, place.y))
+    starts = [place.block(c, y) * rows for c, y in chips]
+    blocks = [pl.ds(pl.multiple_of(start, rows), rows) for start in starts]
+    sibling = [
+        rows_of(place.block(lax.bitwise_xor(c, jnp.int32(1)), y), rows) for c, y in chips
+    ]
+    swaps = []
+    for index in range(4):
+        item = wire.copy(part.at[sibling[index], :], got_core.at[index], place.core)
+        item.start()
+        swaps.append(item)
+    whole = pl.ds(0, 2 * half)
+
+    def one(index, lanes, slot, device):
+        item = wire.copy(part.at[blocks[index], lanes], got_one.at[slot], device)
+        item.start()
+        return item
+
+    swaps[0].wait_recv()
+    add_into(part, whole, starts[0], got_core.at[0])
+    far_x = one(0, left, 0, place.over_x)
+    far_y = one(0, right, 2, place.over_y)
+    swaps[1].wait_recv()
+    add_into(part, whole, starts[1], got_core.at[1])
+    near_x = one(1, left, 1, place.over_x)
+    swaps[2].wait_recv()
+    add_into(part, whole, starts[2], got_core.at[2])
+    near_y = one(2, right, 3, place.over_y)
+    yield
+    swaps[3].wait_recv()
+    add_into(part, whole, starts[3], got_core.at[3])
+    far_x.wait_recv()
+    add_into(part, left, starts[2], got_one.at[0])
+    last_y = wire.copy(part.at[blocks[2], left], got_two.at[0], place.over_y)
+    last_y.start()
+    far_y.wait_recv()
+    add_into(part, right, starts[1], got_one.at[2])
+    last_x = wire.copy(part.at[blocks[1], right], got_two.at[1], place.over_x)
+    last_x.start()
+    yield
+    near_x.wait_recv()
+    near_y.wait_recv()
+    last_x.wait_recv()
+    last_y.wait_recv()
+
+
+def plane_sum(place, part, got_one, got_two, here):
+    rows = part.shape[0] // 8
+    half = part.shape[1] // 2
+    start = place.block(place.c, place.y) * rows + here.start
+    at = pl.ds(pl.multiple_of(start, here.size), here.size)
+
+    def value(ref):
+        return ref.astype(jnp.float32)
+
+    left = value(part[at, 0:half]) + value(got_one[1, here, :]) + value(got_two[0, here, :])
+    right = value(part[at, half:]) + value(got_one[3, here, :]) + value(got_two[1, here, :])
+    return jnp.concatenate([left, right], axis=1)
+
+
+def forward_kernel(
+    n_blocks, n_dp,
+    tokens, small, ids, w_query, w_key, w_value, w_out, s_gate, s_up, s_down,
+    bias, cosine, sine,
+    attn_in, query, keys, values, attn, lse, hidden, moe_in,
+    heads_weight, out_weight, gate_weight, up_weight, down_weight, smalls, all_ids,
+    x_seq, partial, got_core, got_one, got_two, send, recv, local,
+):
+    place = Place(n_dp)
+    wire = Wire(send, recv)
+    inside = Local(local)
+    z, c, y = place.z, place.c, place.y
+    rows, width = tokens.shape
+    seq = x_seq.shape[0]
+    cols = query.shape[1]
+    head_dim = cosine.shape[1]
+    block = seq // n_blocks
+    scale = 1.0 / math.sqrt(head_dim)
+    n_ctx = 4
+    share = w_query.shape[0]
+    f32, low = jnp.float32, jnp.bfloat16
+
+    others = [(dz, dc) for dz in range(n_dp) for dc in range(n_ctx) if dz or dc]
+
+    def moved(dz, dc, y_to):
+        return (lax.bitwise_xor(z, jnp.int32(dz)), lax.bitwise_xor(c, jnp.int32(dc)), y_to)
+
+    barrier(
+        [moved(dz, dc, y) for dz, dc in others] + [moved(dz, 0, place.yn) for dz in range(n_dp)]
+    )
+
+    mine = z * n_ctx + c
+    my_rows = rows_of(mine, share)
+    exchanges = []
+    for dc in range(n_ctx):
+        to = lax.bitwise_xor(c, jnp.int32(dc))
+        lanes = pl.ds(pl.multiple_of(to * cols, cols), cols)
+        pairs = [
+            (weight.at[:, lanes], heads_weight.at[my_rows, pl.ds(index * cols, cols)])
+            for index, weight in enumerate((w_query, w_key, w_value))
+        ]
+        pairs.append((w_out.at[rows_of(to, cols), :], out_weight.at[:, my_rows]))
+        for src, dst in pairs:
+            if dc == 0:
+                exchanges.append(inside.start(src, dst))
+            else:
+                item = wire.copy(src, dst, moved(0, dc, y))
+                item.start()
+                exchanges.append(item)
+    own_rows = rows_of(place.block(c, y), rows)
+    here = inside.start(tokens, x_seq.at[own_rows, :])
+    here.wait()
+    tokens_in = plane_gather(wire, place, x_seq)
+    next(tokens_in)
+    small_copies = [inside.start(small, smalls.at[:, my_rows])]
+    for dz, dc in others:
+        item = wire.copy(small, smalls.at[:, my_rows], moved(dz, dc, y))
+        item.start()
+        small_copies.append(item)
+    group = z * 2 + y
+    small_copies.append(inside.start(ids, all_ids.at[group]))
+    for dz in range(n_dp):
+        for y_to in (y, place.yn):
+            if dz or y_to is not y:
+                item = wire.copy(ids, all_ids.at[group], moved(dz, 0, y_to))
+                item.start()
+                small_copies.append(item)
+    for item in exchanges:
+        item.wait_recv()
+
+    def attention_blocks(slot):
+        at = rows_of(slot, n_ctx * share)
+        return [heads_weight.at[at, :], out_weight.at[:, at]]
+
+    weights_in = chain_gather(wire, place, attention_blocks)
+    next(weights_in)
+    finish(tokens_in)
+    for item in small_copies:
+        item.wait_recv()
+
+    gain_one = smalls[9:10, :].astype(f32)
+    gain_two = smalls[10:11, :].astype(f32)
+
+    def norm_one(at):
+        x_float = x_seq[at, :].astype(f32)
+        rstd = lax.rsqrt(jnp.mean(x_float * x_float, axis=1, keepdims=True) + EPS)
+        attn_in[at, :] = (x_float * rstd * gain_one).astype(low)
+
+    by_rows(seq, 64, norm_one)
+    finish(weights_in)
+
+    shared_pieces = []
+    for dz in range(n_dp):
+        to = lax.bitwise_xor(z, jnp.int32(dz))
+        hidden_rows = rows_of(to, s_down.shape[0] // n_dp)
+        pairs = [
+            (s_gate.at[to], gate_weight.at[z, c]),
+            (s_up.at[to], up_weight.at[z, c]),
+            (s_down.at[hidden_rows, :], down_weight.at[:, my_rows]),
+        ]
+        for src, dst in pairs:
+            if dz == 0:
+                shared_pieces.append(inside.start(src, dst))
+            else:
+                item = wire.copy(src, dst, moved(dz, 0, y))
+                item.start()
+                shared_pieces.append(item)
+
+    def project(at):
+        pre = dot_f32(attn_in[at, :], heads_weight[...], 1, 0)
+        cos = cosine[at, :]
+        sin = sine[at, :]
+        for index, kept in enumerate((query, keys, values)):
+            for start in range(0, cols, head_dim):
+                from_lane = index * cols + start
+                part = pre[:, from_lane : from_lane + head_dim]
+                part = part + bias[index : index + 1, start : start + head_dim]
+                if index < 2:
+                    part = part * cos + pltpu.roll(part, head_dim // 2, 1) * sin
+                kept[at, start : start + head_dim] = part.astype(low)
+
+    by_rows(seq, block, project)
+    for start in range(0, cols, head_dim):
+        lanes = slice(start, start + head_dim)
+        for step in range(n_blocks):
+            at = slice(step * block, (step + 1) * block)
+            seen = slice(0, (step + 1) * block)
+            scores = dot_f32(query[at, lanes], keys[seen, lanes], 1, 1) * scale
+            top = jnp.max(scores, axis=1, keepdims=True)
+            expo = jnp.exp(scores - top)
+            total = jnp.sum(expo, axis=1, keepdims=True)
+            probs = (expo / total).astype(low)
+            attn[at, lanes] = dot_f32(probs, values[seen, lanes], 1, 0).astype(low)
+            lse[at, lanes] = jnp.broadcast_to(top + jnp.log(total), (block, head_dim))
+
+    def output(at):
+        partial[at, :] = dot_f32(attn[at, :], out_weight[...], 1, 0).astype(low)
+
+    by_rows(seq, block, output)
+    finish(plane_reduce(wire, place, partial, got_core, got_one, got_two))
+
+    def norm_two(at):
+        start = place.block(c, y) * rows + at.start
+        own = pl.ds(pl.multiple_of(start, at.size), at.size)
+        total = x_seq[own, :].astype(f32) + plane_sum(place, partial, got_one, got_two, at)
+        hidden[at, :] = total
+        rstd = lax.rsqrt(jnp.mean(total * total, axis=1, keepdims=True) + EPS)
+        got_core[0, at, :] = (total * rstd * gain_two).astype(low)
+
+    by_rows(rows, 16, norm_two)
+    at_group = rows_of(group, rows)
+    here = inside.start(got_core.at[0], moe_in.at[at_group, :])
+    here.wait()
+
+    y_recv = wire.take(n_dp)
+    y_send = wire.take_send(n_dp)
+
+    def to_y(slot):
+        at = rows_of(slot * 2 + y, rows)
+        return wire.copy_to(
+            moe_in.at[at, :], moe_in.at[at, :], place.over_y, y_recv + slot, y_send + slot
+        )
+
+    def from_y(slot):
+        at = rows_of(slot * 2 + place.yn, rows)
+        return wire.copy_to(
+            moe_in.at[at, :], moe_in.at[at, :], place.over_y, y_recv + slot, y_send + slot
+        )
+
+    rows_chain = chain_gather(
+        wire,
+        place,
+        lambda slot: [moe_in.at[rows_of(slot * 2 + y, rows), :]],
+        arrived=lambda slot: to_y(slot).start(),
+    )
+    next(rows_chain)
+    to_y(z).start()
+    for item in shared_pieces:
+        item.wait_recv()
+
+    def shared_set(context):
+        return [gate_weight.at[:, context], up_weight.at[:, context]] + [
+            down_weight.at[:, rows_of(dz * n_ctx + context, share)] for dz in range(n_dp)
+        ]
+
+    over = []
+    for ref in shared_set(c):
+        item = wire.copy(ref, ref, place.over_x)
+        item.start()
+        over.append(item)
+    close = []
+    for ref in shared_set(c):
+        item = wire.copy(ref, ref, place.core)
+        item.start()
+        close.append(item)
+    finish(rows_chain)
+    for item, ref in zip(over, shared_set(place.cx)):
+        item.wait_recv()
+        item = wire.copy(ref, ref, place.core)
+        item.start()
+        close.append(item)
+    for item in close:
+        item.wait_recv()
+    for slot in range(n_dp):
+        from_y(slot).wait_recv()
+        to_y(slot).wait_send()
+    wire.drain()
+
+
+def attention_backward(
+    n_blocks, d_out, w_out, heads_weight, query, keys, values, lse, cosine, sine,
+    d_query_pre, d_key_pre, d_value_pre, d_bias, partial,
+    d_attn, d_keys, d_values,
+):
+    rows, width = d_out.shape
+    cols = query.shape[1]
+    head_dim = cosine.shape[1]
+    block = rows // n_blocks
+    scale = 1.0 / math.sqrt(head_dim)
+
+    def project(step, carry):
+        here = pl.ds(pl.multiple_of(step * block, block), block)
+        d_attn[here, :] = dot_f32(d_out[here, :], w_out[...], 1, 1).astype(jnp.bfloat16)
+        return carry
+
+    lax.fori_loop(0, n_blocks, project, 0)
+
+    def back(part, here):
+        return part * cosine[here, :] - pltpu.roll(part, head_dim // 2, 1) * sine[here, :]
+
+    for start in range(0, cols, head_dim):
+        lanes = slice(start, start + head_dim)
+        d_keys[...] = jnp.zeros_like(d_keys)
+        d_values[...] = jnp.zeros_like(d_values)
+        for step in range(n_blocks):
+            here = slice(step * block, (step + 1) * block)
+            seen = slice(0, (step + 1) * block)
+            q_here = query[here, lanes]
+            k_seen = keys[seen, lanes]
+            grad = d_attn[here, lanes]
+            scores = dot_f32(q_here, k_seen, 1, 1) * scale
+            probs = jnp.exp(scores - lse[here, start : start + 1])
+            d_probs = dot_f32(grad, values[seen, lanes], 1, 1)
+            delta = jnp.sum(probs * d_probs, axis=1, keepdims=True)
+            d_scores = (probs * (d_probs - delta)).astype(jnp.bfloat16)
+            d_query = dot_f32(d_scores, k_seen, 1, 0) * scale
+            d_query_pre[here, lanes] = back(d_query, here).astype(jnp.bfloat16)
+            d_keys[seen, :] += dot_f32(d_scores, q_here, 0, 0) * scale
+            d_values[seen, :] += dot_f32(probs.astype(jnp.bfloat16), grad, 0, 0)
+        every = slice(0, rows)
+        d_key_pre[:, lanes] = back(d_keys[...], every).astype(jnp.bfloat16)
+        d_value_pre[:, lanes] = d_values[...].astype(jnp.bfloat16)
+    d_bias[...] = jnp.zeros_like(d_bias)
+    for index, kept in enumerate((d_query_pre, d_key_pre, d_value_pre)):
+        d_bias[index : index + 1, :] = jnp.sum(
+            kept[...].astype(jnp.float32), axis=0, keepdims=True
+        )
+
+    def output(step, carry):
+        here = pl.ds(pl.multiple_of(step * block, block), block)
+        total = 0.0
+        for index, kept in enumerate((d_query_pre, d_key_pre, d_value_pre)):
+            weight = heads_weight[:, index * cols : (index + 1) * cols]
+            total = total + dot_f32(kept[here, :], weight, 1, 1)
+        partial[here, :] = total.astype(jnp.bfloat16)
+        return carry
+
+    lax.fori_loop(0, n_blocks, output, 0)
+
+
+def tokens_plan(
+    tokens,
+    out_grad,
+    expert_ids,
+    norm1_gain,
+    w_query,
+    w_key,
+    w_value,
+    query_bias_heads,
+    bias_key,
+    bias_value,
+    w_out,
+    norm2_gain,
+    w_router,
+    shared_mix,
+    shared_in_gate,
+    shared_in_up,
+    shared_down,
+    expert_gate,
+    expert_up,
+    expert_down,
+):
+    low = jnp.bfloat16
+    f32 = jnp.float32
+    tok_rows, width = tokens.shape
+    n_dp, n_ctx, n_half = (lax.axis_size(name) for name in (DP, CONTEXT, EXPERT))
+    dp, ctx, half = (lax.axis_index(name) for name in (DP, CONTEXT, EXPERT))
+    half_heads, head_dim = query_bias_heads.shape
+    heads = half_heads // n_ctx
+    cols = heads * head_dim
+    seq_len = tok_rows * n_ctx * n_half
+    n_blocks = seq_len // BLOCK
+    n_experts = w_router.shape[1]
+    n_group = n_dp * n_half
+    my_expert = dp * n_half + half
+
+    def heads_out(grad):
+        mine = lax.psum_scatter(grad.astype(low), DP, scatter_dimension=0, tiled=True)
+        return lax.all_to_all(mine, CONTEXT, split_axis=0, concat_axis=1, tiled=True).astype(f32)
+
+    def heads_out_rows(grad):
+        mine = lax.psum_scatter(grad.astype(low), DP, scatter_dimension=1, tiled=True)
+        return lax.all_to_all(mine, CONTEXT, split_axis=1, concat_axis=0, tiled=True).astype(f32)
+
+    def hidden_out(grad):
+        split = grad.astype(low).reshape(n_dp, n_ctx, -1, grad.shape[1])
+        mine = lax.psum_scatter(split, CONTEXT, scatter_dimension=1, tiled=True)
+        mine = mine.reshape(width // n_ctx, -1)
+        return lax.all_to_all(mine, DP, split_axis=0, concat_axis=1, tiled=True).astype(f32)
+
+    def hidden_out_rows(grad):
+        split = grad.astype(low).reshape(grad.shape[0], n_dp, n_ctx, -1)
+        mine = lax.psum_scatter(split, CONTEXT, scatter_dimension=2, tiled=True)
+        mine = mine.reshape(grad.shape[0], -1)
+        return lax.all_to_all(mine, DP, split_axis=1, concat_axis=0, tiled=True).astype(f32)
+
+    def plane_in(rows):
+        return lax.all_gather(rows, (CONTEXT, EXPERT), axis=0, tiled=True)
+
+    def plane_out(rows):
+        return lax.psum_scatter(rows, (CONTEXT, EXPERT), scatter_dimension=0, tiled=True)
+
+    def group_in(rows):
+        return lax.all_gather(rows, (DP, EXPERT), axis=0, tiled=True)
+
+    def group_out(rows):
+        return lax.psum_scatter(rows, (DP, EXPERT), scatter_dimension=0, tiled=True)
+
+    small = jnp.concatenate(
+        [w_router.T, shared_mix[None], norm1_gain[None], norm2_gain[None]], axis=0
+    )
+    small = jnp.pad(small, ((0, 16 - small.shape[0]), (0, 0)))
+    ids = jnp.pad(expert_ids.T, ((0, 8 - expert_ids.shape[1]), (0, 0)), constant_values=-1)
+    hidden_units = shared_in_gate.shape[1] // n_dp
+
+    def by_dp(weight):
+        return weight.reshape(weight.shape[0], n_dp, hidden_units).transpose(1, 0, 2)
+
+    biases = jnp.stack([query_bias_heads, bias_key, bias_value]).astype(f32)
+    biases = lax.dynamic_slice_in_dim(biases, ctx * heads, heads, 1).reshape(3, cols)
+    cosine, sine = rope_tables(jnp.arange(seq_len), head_dim)
+    cosine = jnp.concatenate([cosine[:, 0], cosine[:, 0]], axis=1)
+    sine = jnp.concatenate([-sine[:, 0], sine[:, 0]], axis=1)
+    dy_group = group_in(out_grad)
+    vmem = pl.BlockSpec(memory_space=pltpu.VMEM)
+    anywhere = pl.BlockSpec(memory_space=pl.ANY)
+    share = w_query.shape[0]
+    half_width = width // 2
+    (
+        attn_in, query, keys, values, attn, lse, hidden_own, moe_in,
+        heads_weight, wo, sg, su, sd, small, ids_group,
+    ) = pl.pallas_call(
+        lambda *refs: forward_kernel(n_blocks, n_dp, *refs),
+        out_shape=[
+            like((seq_len, width), low),
+            like((seq_len, cols), low),
+            like((seq_len, cols), low),
+            like((seq_len, cols), low),
+            like((seq_len, cols), low),
+            like((seq_len, cols), f32),
+            like((tok_rows, width), f32),
+            like((n_group * tok_rows, width), low),
+            like((width, 3 * cols), low),
+            like((cols, width), low),
+            like((n_dp, n_ctx, share, hidden_units), low),
+            like((n_dp, n_ctx, share, hidden_units), low),
+            like((hidden_units, width), low),
+            like((16, width), low),
+            like((n_group, 8, tok_rows), jnp.int32),
+        ],
+        in_specs=[anywhere] * 10 + [vmem] * 3,
+        out_specs=[vmem] * 7 + [anywhere] + [vmem] * 2 + [anywhere] * 3 + [vmem, anywhere],
+        scratch_shapes=[
+            pltpu.VMEM((seq_len, width), low),
+            pltpu.VMEM((seq_len, width), low),
+            pltpu.VMEM((4, tok_rows, width), low),
+            pltpu.VMEM((4, tok_rows, half_width), low),
+            pltpu.VMEM((2, tok_rows, half_width), low),
+            pltpu.SemaphoreType.DMA((144,)),
+            pltpu.SemaphoreType.DMA((144,)),
+            pltpu.SemaphoreType.DMA((16,)),
+        ],
+        name="forward",
+        compiler_params=pltpu.CompilerParams(
+            collective_id=1, has_side_effects=True, vmem_limit_bytes=60 * 2**20
+        ),
+    )(
+        tokens, small, ids, w_query, w_key, w_value, w_out,
+        by_dp(shared_in_gate), by_dp(shared_in_up), shared_down, biases, cosine, sine,
+    )
+    sg, su = sg.reshape(width, hidden_units), su.reshape(width, hidden_units)
+    gain_one = small[n_experts + 1].astype(f32)
+    gain_two = small[n_experts + 2].astype(f32)
+    x_own = tokens.astype(f32)
+    dy_own = out_grad.astype(f32)
+    rstd_two = lax.rsqrt(jnp.mean(hidden_own * hidden_own, axis=1, keepdims=True) + EPS)
+    normed_two = hidden_own * rstd_two
+    moe_own = (normed_two * gain_two).astype(low)
+
+    logits = mat_right(moe_in, small)
+    router_probs = jax.nn.softmax(logits[:, :n_experts], axis=1)
+    mix = jax.nn.sigmoid(logits[:, n_experts])
+    hit = jnp.any(ids_group == my_expert, axis=1)
+    gate = jnp.sum(
+        jnp.where(jnp.arange(n_experts)[None, :] == my_expert, router_probs, 0.0), axis=1
+    )
+    place = jnp.cumsum(hit.astype(jnp.int32), axis=1) - 1
+    chosen = (hit[:, None, :] & (place[:, None, :] == jnp.arange(CAP)[None, :, None]))
+    pick = chosen.astype(low)
+    gate_rows = jnp.sum(jnp.where(chosen, gate.reshape(n_group, 1, tok_rows), 0.0), axis=2)
+
+    def to_rows(group):
+        return jnp.einsum(
+            "sct,std->scd", pick, group.reshape(n_group, tok_rows, -1), preferred_element_type=f32
+        ).astype(low).reshape(n_group * CAP, -1)
+
+    def to_tokens(rows):
+        return jnp.einsum(
+            "sct,scd->std", pick, rows.reshape(n_group, CAP, -1), preferred_element_type=f32
+        ).reshape(n_group * tok_rows, -1)
+
+    rows_in = to_rows(moe_in)
+    dy_rows = to_rows(dy_group)
+    grads_in = (gate_rows.reshape(-1, 1) * dy_rows.astype(f32)).astype(low)
+    gate_weight, up_weight, down_weight = expert_gate[0], expert_up[0], expert_down[0]
+    e_gate = jnp.dot(rows_in, gate_weight, preferred_element_type=f32)
+    e_up = jnp.dot(rows_in, up_weight, preferred_element_type=f32)
+    e_silu = jax.nn.silu(e_gate)
+    e_hidden = (e_silu * e_up).astype(low)
+    e_out = jnp.dot(e_hidden, down_weight, preferred_element_type=f32).astype(low)
+    d_hidden = mat_right(grads_in, down_weight)
+    d_gate = (d_hidden * e_up * silu_slope(e_gate)).astype(low)
+    d_up = (d_hidden * e_silu).astype(low)
+    d_in = (mat_right(d_gate, gate_weight) + mat_right(d_up, up_weight)).astype(low)
+
+    s_gate = jnp.dot(moe_in, sg, preferred_element_type=f32)
+    s_up = jnp.dot(moe_in, su, preferred_element_type=f32)
+    s_silu = jax.nn.silu(s_gate)
+    s_hidden = (s_silu * s_up).astype(low)
+    shared = jnp.dot(s_hidden, sd, preferred_element_type=f32)
+    dy_float = dy_group.astype(f32)
+    d_shared = (mix[:, None] * dy_float).astype(low)
+    d_shidden = mat_right(d_shared, sd)
+    d_sgate = (d_shidden * s_up * silu_slope(s_gate)).astype(low)
+    d_sup = (d_shidden * s_silu).astype(low)
+
+    moe_part = (gate[:, None] * to_tokens(e_out) + mix[:, None] * shared).astype(low)
+    d_in_part = (to_tokens(d_in) + mat_right(d_sgate, sg) + mat_right(d_sup, su)).astype(low)
+    d_gate_rows = jnp.sum(e_out.astype(f32) * dy_rows.astype(f32), axis=1).reshape(n_group, CAP)
+    d_gate_tok = jnp.sum(jnp.where(chosen, d_gate_rows[:, :, None], 0.0), axis=1).reshape(-1)
+    shared_dot = jnp.sum(shared * dy_float, axis=1)
+    scalars = jnp.concatenate(
+        [
+            jnp.where(jnp.arange(n_experts)[None, :] == my_expert, d_gate_tok[:, None], 0.0),
+            shared_dot[:, None],
+        ],
+        axis=1,
+    )
+    scalars = group_out(scalars)
+    d_in_own = group_out(d_in_part).astype(f32)
+    moe_sum = group_out(moe_part).astype(f32)
+    mixed = (hidden_own + moe_sum).astype(low)
+
+    own = my_expert * tok_rows
+    probs_own = lax.dynamic_slice_in_dim(router_probs, own, tok_rows, 0)
+    mix_own = lax.dynamic_slice_in_dim(mix, own, tok_rows, 0)
+    d_rprobs = scalars[:, :n_experts]
+    d_logits = probs_own * (d_rprobs - jnp.sum(probs_own * d_rprobs, axis=1, keepdims=True))
+    d_mixlogit = scalars[:, n_experts] * mix_own * (1.0 - mix_own)
+    d_side = jnp.concatenate([d_logits, d_mixlogit[:, None]], axis=1)
+    moe_own_float = moe_own.astype(f32)
+    side_grad = jnp.dot(d_side.T, moe_own_float, precision=HIGH)
+    d_moe_in = d_in_own + jnp.dot(
+        d_side, small[: n_experts + 1].astype(f32), precision=HIGH
+    )
+    gain_two_grad = jnp.sum(d_moe_in * normed_two, axis=0)
+    d_norm_two = d_moe_in * gain_two
+    d_hidden_own = dy_own + rstd_two * (
+        d_norm_two - normed_two * jnp.mean(d_norm_two * normed_two, axis=1, keepdims=True)
+    )
+    d_proj = plane_in(d_hidden_own.astype(low))
+
+    d_q_pre, d_k_pre, d_v_pre, d_bias, d_partial = pl.pallas_call(
+        lambda *refs: attention_backward(n_blocks, *refs),
+        out_shape=[
+            like((seq_len, cols), low),
+            like((seq_len, cols), low),
+            like((seq_len, cols), low),
+            like((8, cols), f32),
+            like((seq_len, width), low),
+        ],
+        in_specs=whole_vmem(9),
+        out_specs=whole_vmem(5),
+        scratch_shapes=[
+            pltpu.VMEM((seq_len, cols), low),
+            pltpu.VMEM((seq_len, head_dim), f32),
+            pltpu.VMEM((seq_len, head_dim), f32),
+        ],
+        name="attention_backward",
+        compiler_params=pltpu.CompilerParams(vmem_limit_bytes=56 * 2**20),
+    )(d_proj, wo, heads_weight, query, keys, values, lse, cosine, sine)
+    d_attn_in = plane_out(d_partial).astype(f32)
+    rstd_one = lax.rsqrt(jnp.mean(x_own * x_own, axis=1, keepdims=True) + EPS)
+    normed_one = x_own * rstd_one
+    d_norm_one = d_attn_in * gain_one
+    gain_one_grad = jnp.sum(d_attn_in * normed_one, axis=0)
+    input_grad = (
+        d_hidden_own
+        + rstd_one
+        * (d_norm_one - normed_one * jnp.mean(d_norm_one * normed_one, axis=1, keepdims=True))
+    ).astype(low)
+
+    routed = [
+        lax.psum_scatter(
+            grad[None].astype(low), CONTEXT, scatter_dimension=dim, tiled=True
+        ).astype(f32)
+        for grad, dim in (
+            (left_operand(rows_in, d_gate), 1),
+            (left_operand(rows_in, d_up), 1),
+            (left_operand(e_hidden, grads_in), 2),
+        )
+    ]
+    grad_sgate = hidden_out(left_operand(moe_in, d_sgate))
+    grad_sup = hidden_out(left_operand(moe_in, d_sup))
+    grad_sdown = hidden_out_rows(left_operand(s_hidden, d_shared))
+    grad_out = heads_out_rows(left_operand(attn, d_proj))
+    grad_query = heads_out(left_operand(attn_in, d_q_pre))
+    grad_key = heads_out(left_operand(attn_in, d_k_pre))
+    grad_value = heads_out(left_operand(attn_in, d_v_pre))
+
+    all_bias = jnp.zeros((n_half, 3, half_heads, head_dim), f32)
+    all_bias = lax.dynamic_update_slice(
+        all_bias, d_bias[:3].reshape(1, 3, heads, head_dim), (half, 0, ctx * heads, 0)
+    )
+    rest = jnp.concatenate(
+        [
+            side_grad,
+            gain_one_grad[None],
+            gain_two_grad[None],
+            all_bias.reshape(-1, width),
+        ],
+        axis=0,
+    )
+    rest = lax.psum(rest, (DP, CONTEXT, EXPERT))
+    share = width // (n_dp * n_ctx)
+    place = dp * n_ctx + ctx
+    mine = lax.dynamic_slice_in_dim(rest[: n_experts + 3], place * share, share, 1)
+    bias_sum = rest[n_experts + 3 :].reshape(n_half, 3, half_heads, head_dim)
+    bias_share = head_dim // (n_dp * n_ctx)
+    bias_sum = lax.dynamic_slice(
+        bias_sum, (half, 0, 0, place * bias_share), (1, 3, half_heads, bias_share)
+    )[0]
+    return (
+        mixed,
+        input_grad,
+        mine[n_experts + 1],
+        grad_query,
+        grad_key,
+        grad_value,
+        bias_sum[0],
+        bias_sum[1],
+        bias_sum[2],
+        grad_out,
+        mine[n_experts + 2],
+        mine[:n_experts].T,
+        mine[n_experts],
+        grad_sgate,
+        grad_sup,
+        grad_sdown,
+        routed[0],
+        routed[1],
+        routed[2],
+    )
+
+
+def on_device(*arrays):
+    sizes = [lax.axis_size(name) for name in (DP, CONTEXT, EXPERT)]
+    if sizes == [4, 4, 2] and arrays[7].shape[0] % sizes[1] == 0:
+        return tokens_plan(*arrays)
+    return weights_plan(*arrays)
+
+
 def solution(mesh):
     placed = (
-        P(("dp", "context", "expert"), None),
-        P(("dp", "context", "expert"), None),
-        P(("dp", "context", "expert"), None),
-        P(("dp", "context")),
-        P(("dp", "context"), "expert"),
-        P(("dp", "context"), "expert"),
-        P(("dp", "context"), "expert"),
-        P("expert", None),
-        P("expert", None),
-        P("expert", None),
-        P("expert", ("dp", "context")),
-        P(("dp", "context")),
-        P(("dp", "context"), None),
-        P(("dp", "context")),
-        P(("dp", "context"), "expert"),
-        P(("dp", "context"), "expert"),
-        P("expert", ("dp", "context")),
-        P(("dp", "expert"), None, None),
-        P(("dp", "expert"), None, None),
-        P(("dp", "expert"), None, None),
+        P((DP, CONTEXT, EXPERT), None),
+        P((DP, CONTEXT, EXPERT), None),
+        P((DP, CONTEXT, EXPERT), None),
+        P((DP, CONTEXT)),
+        P((DP, CONTEXT), EXPERT),
+        P((DP, CONTEXT), EXPERT),
+        P((DP, CONTEXT), EXPERT),
+        P(EXPERT, None),
+        P(EXPERT, None),
+        P(EXPERT, None),
+        P(EXPERT, (DP, CONTEXT)),
+        P((DP, CONTEXT)),
+        P((DP, CONTEXT), None),
+        P((DP, CONTEXT)),
+        P((DP, CONTEXT), EXPERT),
+        P((DP, CONTEXT), EXPERT),
+        P(EXPERT, (DP, CONTEXT)),
+        P((DP, EXPERT), None, None),
+        P((DP, EXPERT), None, None),
+        P((DP, EXPERT), None, None),
     )
     return jax.shard_map(
         on_device,
         mesh=mesh,
         in_specs=placed,
         out_specs=(
-            P(("dp", "context", "expert"), None),
-            P(("dp", "context", "expert"), None),
-            P(("dp", "context")),
-            P(("dp", "context"), "expert"),
-            P(("dp", "context"), "expert"),
-            P(("dp", "context"), "expert"),
-            P("expert", ("dp", "context")),
-            P("expert", ("dp", "context")),
-            P("expert", ("dp", "context")),
-            P("expert", ("dp", "context")),
-            P(("dp", "context")),
-            P(("dp", "context"), None),
-            P(("dp", "context")),
-            P(("dp", "context"), "expert"),
-            P(("dp", "context"), "expert"),
-            P("expert", ("dp", "context")),
-            P(("dp", "expert"), "context", None),
-            P(("dp", "expert"), "context", None),
-            P(("dp", "expert"), None, "context"),
+            P((DP, CONTEXT, EXPERT), None),
+            P((DP, CONTEXT, EXPERT), None),
+            P((DP, CONTEXT)),
+            P((DP, CONTEXT), EXPERT),
+            P((DP, CONTEXT), EXPERT),
+            P((DP, CONTEXT), EXPERT),
+            P(EXPERT, (DP, CONTEXT)),
+            P(EXPERT, (DP, CONTEXT)),
+            P(EXPERT, (DP, CONTEXT)),
+            P(EXPERT, (DP, CONTEXT)),
+            P((DP, CONTEXT)),
+            P((DP, CONTEXT), None),
+            P((DP, CONTEXT)),
+            P((DP, CONTEXT), EXPERT),
+            P((DP, CONTEXT), EXPERT),
+            P(EXPERT, (DP, CONTEXT)),
+            P((DP, EXPERT), CONTEXT, None),
+            P((DP, EXPERT), CONTEXT, None),
+            P((DP, EXPERT), None, CONTEXT),
         ),
         check_vma=False,
     )

time: 2550 us -> 1270 us (0.50)
  waiting for transfers between devices: 1870 us -> 675 us
  Pallas kernels: 0 us -> 255 us
  blocking collectives: 194 us -> 0 us
  matrix products: 271 us -> 167 us
  other arithmetic: 67 us -> 36.7 us
    reduce_scatter x14 -> x11, waiting for transfers between devices: 1260 us -> 423 us  [the longest x3 192 us: group_out(): return lax.psum_scatter(rows, (DP, EXPERT), scatter_dimension=0, tiled=True)]
    all_gather x11 -> x2, waiting for transfers between devices: 271 us -> 0.02 us  [the longest x1 0.02 us: plane_in(): return lax.all_gather(rows, (CONTEXT, EXPERT), axis=0, tiled=True)]
    pallas_call x0 -> x2, Pallas kernels: none -> 255 us  [the longest x1 236 us: tokens_plan(): pl.pallas_call(lambda *refs: forward_kernel(n_blocks, n_dp, *refs), out_s...]
    all_to_all x4 -> x7, waiting for transfers between devices: 205 us -> 36 us  [the longest x2 23.3 us: hidden_out(): lax.all_to_all(mine, DP, split_axis=0, concat_axis=1, tiled=True)]
    all_gather x4 -> x0, blocking collectives: 141 us -> none  [the longest x1 86.1 us: on_device(): lax.all_gather(shared_mix, ('dp', 'context'), axis=0, tiled=True)]
    unnamed x28 -> x16, waiting for transfers between devices: 6.51 us -> 93.5 us
    dot_general x43 -> x12, matrix products: 127 us -> 55.5 us  [the longest x1 12.5 us: tokens_plan(): shared = jnp.dot(s_hidden, sd, preferred_element_type=f32)]
    unnamed x1 -> x0, blocking collectives: 48.9 us -> none
  transfers between devices with their start and end apart: 32 -> 22, of which waited for: 24 -> 17; matrix products, arithmetic and copies ran while one was open for 14% -> 19% of each run, Pallas kernels for 0% -> 20%
where the time goes in v1:
time: 1270 us; the launch traced here: 1260 us
  waiting for transfers between devices  675 us (53%)
  Pallas kernels  255 us (20%)
  matrix products  167 us (13%)
  local copies, waits for them, and re-layouts  79 us (6%)
  starting transfers between devices  37.3 us (3%)
  other arithmetic  36.7 us (3%)
  between operations  15 us (1%)
    pallas_call x1, Pallas kernels, tokens_plan(): pl.pallas_call(lambda *refs: forward_kernel(n_blocks, n_dp, *refs), out_s...  236 us
    reduce_scatter x3, waiting for transfers between devices, group_out(): return lax.psum_scatter(rows, (DP, EXPERT), scatter_dimension=0, tiled=True)  192 us
    psum x1, waiting for transfers between devices, tokens_plan(): rest = lax.psum(rest, (DP, CONTEXT, EXPERT))  123 us
    reduce_scatter x3, waiting for transfers between devices, tokens_plan(): lax.psum_scatter(grad[None].astype(low), CONTEXT, scatter_dimension=dim,...  98 us
    unnamed x16, waiting for transfers between devices  93.5 us
    reduce_scatter x3, waiting for transfers between devices, heads_out(): lax.psum_scatter(grad.astype(low), DP, scatter_dimension=0, tiled=True)  73.3 us
    dot_general x10, matrix products, left_operand(): return jnp.dot(left.T, right, preferred_element_type=jnp.float32)  57.1 us
    dot_general x7, matrix products, mat_right(): return jnp.dot(left, right.T, preferred_element_type=jnp.float32)  54.6 us
  transfers between devices with their start and end apart: 22, of which 17 were waited for; matrix products, arithmetic and copies ran while one was open for 19% of the time, Pallas kernels for 20%

profile of v1, /device:TPU:9, one launch (start us, length us, event | category | flops | bytes accessed | tf_op | source)
XLA Modules:
  0.0 1264.9 jit_solution(18365126176442754605)
XLA Ops:
  18.0 235.7 %forward.1 = (bf16[1024,2048]{1,0:T(8,128)(2,1)}, bf16[1024,256]{1,0:T(8,128)(2,1)}, bf16[1024,256]{1,0:T(8,128)(2,1)}, bf16[1024,256]{1,0:T(8,128)(2,1)}, bf16[...) custom-call(bf16[128,2048]{1,0:T(8,128)(2,1)} %refs_0_.1, ...), custom_call_target="tpu_custom_call" | custom-call | tf_op jit(solution)/shard_map/forward/pallas_call | solution.py:1123
  259.5 8.9 fusion.22
  268.5 7.2 multiply_convert_fusion.2
  275.7 5.2 fusion.25
  281.0 4.7 fusion.50
  286.0 4.9 fusion.83
  290.8 4.9 fusion.84
  295.7 10.5 multiply_convert_fusion.3
  306.2 6.0 fusion.85
  314.1 12.5 fusion.1
  328.0 10.8 multiply_convert_fusion.1
  338.8 5.1 fusion.16
  343.9 8.4 add_convert_fusion
  353.6 10.3 fusion.3
  365.5 11.9 reduce-scatter.25.cloned.1.call-done
  379.5 91.1 %reduce-scatter.23.cloned.1.call-done = bf16[128,2048]{1,0:T(8,128)(2,1)} async-done(((bf16[1024,2048]{1,0:T(8,128)(2,1)}), bf16[128,2048]{1,0:T(8,128)(2,1)}) %reduce-scatter.23.cloned.1.call-update) | async-done | bytes 524304 | tf_op jit(solution)/shard_map/reduce_scatter | solution.py:1098
  476.9 7.4 convolution_convert_fusion.5
  484.2 18.5 %reshape.234 = bf16[4,4,128,704]{2,1,0,3:T(4,128)(2,1)} reshape(bf16[2048,704]{0,1:T(8,128)(2,1)} %convolution_convert_fusion.5) | data formatting | bytes 5767168 | tf_op jit(solution)/shard_map/reshape | solution.py:1077
  502.7 4.4 copy.68
  507.1 4.4 convolution_convert_fusion.6
  511.5 7.1 reshape.233
  522.9 4.6 convolution_convert_fusion.7
  527.5 7.1 reshape.235
  540.5 6.6 fusion.8
  549.0 8.5 fusion.6
  557.5 8.5 fusion.7
  566.1 19.1 %attention_backward.1 = (bf16[1024,256]{1,0:T(8,128)(2,1)}, bf16[1024,256]{1,0:T(8,128)(2,1)}, bf16[1024,256]{1,0:T(8,128)(2,1)}, f32[8,256]{1,0:T(8,128)}, bf16[1024,2048]{1,0:T(8,128)(2,1)}) custom-call(bf16[1024,2048]{1,0:T(8,128)(2,1)} %all-gather.5.cloned.1.call-done.refs_0_, bf16[256,2048]{1,0:T(8,128)(2,1)} %get-tuple-element.46.refs_1_, ...), custom_call_target="tpu_custom_call" | custom-call | tf_op jit(solution)/shard_map/attention_backward/pallas_call | solution.py:1254
  588.7 4.5 convolution_convert_fusion.8
  593.3 4.7 convolution_convert_fusion.9
  598.1 4.5 convolution_convert_fusion.10
  604.6 91.7 %all-reduce.11.cloned.1.call-done = (bf16[4,4,128,704]{2,3,1,0:T(8,128)(2,1)}, bf16[4,4,128,704]{2,3,1,0:T(8,128)(2,1)}, bf16[704,4,4,128]{3,0,2,1:T(8,128)(2,1)}) async-done(((bf16[4,4,128,704]{2,3,1,0:T(8,128)(2,1)}, bf16[4,4,128,704]{2,3,1,0:T(8,128)(2,1)}, bf16[704,4,4,128]{3,0,2,1:T(8,128)(2,1)}), (bf16[4,4,128,704]{2,3,1,0:T(8,128)(2,1)}, bf16[4,4,128,704]{2,3,1,0:T(8,128)(2,1)}, ...) | async-done | bytes 8650768
  699.0 4.6 all-to-all-start.4
  706.5 11.7 all-to-all-done.4
  718.2 7.0 all-to-all-start.5
  727.9 11.6 all-to-all-done.5
  739.5 8.0 all-to-all-start.6
  756.9 5.0 all-to-all-done.6
  768.0 43.5 %reduce-scatter.37.cloned.1.call-done = bf16[1,512,1408]{2,1,0:T(8,128)(2,1)} async-done(((bf16[1,2048,1408]{2,1,0:T(8,128)(2,1)}), bf16[1,512,1408]{2,1,0:T(8,128)(2,1)}) %reduce-scatter.37.cloned.1.call-update) | async-done | bytes 1441808 | tf_op jit(solution)/shard_map/reduce_scatter | solution.py:1285
  814.6 54.4 %reduce-scatter.39.cloned.1.call-done = bf16[1,512,1408]{2,1,0:T(8,128)(2,1)} async-done(((bf16[1,2048,1408]{2,1,0:T(8,128)(2,1)}), bf16[1,512,1408]{2,1,0:T(8,128)(2,1)}) %reduce-scatter.39.cloned.1.call-update) | async-done | bytes 1441808 | tf_op jit(solution)/shard_map/reduce_scatter | solution.py:1285
  872.9 23.7 %reduce-scatter.29.cloned.1.call-done = bf16[512,256]{1,0:T(8,128)(2,1)} async-done(((bf16[2048,256]{1,0:T(8,128)(2,1)}), bf16[512,256]{1,0:T(8,128)(2,1)}) %reduce-scatter.29.cloned.1.call-update) | async-done | bytes 262160 | tf_op jit(solution)/shard_map/reduce_scatter | solution.py:1069
  900.6 24.1 %reduce-scatter.35.cloned.1.call-done = bf16[256,512]{1,0:T(8,128)(2,1)} async-done(((bf16[256,2048]{1,0:T(8,128)(2,1)}), bf16[256,512]{1,0:T(8,128)(2,1)}) %reduce-scatter.35.cloned.1.call-update) | async-done | bytes 262160 | tf_op jit(solution)/shard_map/reduce_scatter | solution.py:1073
  926.3 26.4 %reduce-scatter.33.cloned.1.call-done = bf16[512,256]{1,0:T(8,128)(2,1)} async-done(((bf16[2048,256]{1,0:T(8,128)(2,1)}), bf16[512,256]{1,0:T(8,128)(2,1)}) %reduce-scatter.33.cloned.1.call-update) | async-done | bytes 262160 | tf_op jit(solution)/shard_map/reduce_scatter | solution.py:1069
  957.6 23.2 %reduce-scatter.31.cloned.1.call-done = bf16[512,256]{1,0:T(8,128)(2,1)} async-done(((bf16[2048,256]{1,0:T(8,128)(2,1)}), bf16[512,256]{1,0:T(8,128)(2,1)}) %reduce-scatter.31.cloned.1.call-update) | async-done | bytes 262160 | tf_op jit(solution)/shard_map/reduce_scatter | solution.py:1069
  980.9 4.6 all-to-all-start.1
  986.4 4.4 all-to-all-done.1
  1001.0 35.2 %reduce-scatter.27.cloned.1.call-done = bf16[128,2048]{1,0:T(8,128)(2,1)} async-done(((bf16[1024,2048]{1,0:T(8,128)(2,1)}), bf16[128,2048]{1,0:T(8,128)(2,1)}) %reduce-scatter.27.cloned.1.call-update) | async-done | bytes 524304 | tf_op jit(solution)/shard_map/reduce_scatter | solution.py:1092
  1039.2 89.0 %reduce-scatter.21.cloned.1.call-done = bf16[128,2048]{1,0:T(8,128)(2,1)} async-done(((bf16[1024,2048]{1,0:T(8,128)(2,1)}), bf16[128,2048]{1,0:T(8,128)(2,1)}) %reduce-scatter.21.cloned.1.call-update) | async-done | bytes 524304 | tf_op jit(solution)/shard_map/reduce_scatter | solution.py:1098
  1130.9 122.8 %all-reduce.9.cloned.1.call-done = f32[14,2048]{1,0:T(8,128)} async-done(((f32[14,2048]{1,0:T(8,128)}), f32[14,2048]{1,0:T(8,128)}) %all-reduce.9.cloned.1.call-update) | async-done | bytes 114704 | tf_op jit(solution)/shard_map/psum | solution.py:1315
  (213 shorter events, 111.0 us)
Async XLA Ops:
  7.2 6.4 copy-start.19
  7.2 288.5 %all-gather.3.cloned.1.call-start = ((), (), s32[]{:S(2)}) async-start(), calls=%async_computation.19 | async-start | bytes 4718592 | tf_op jit(solution)/shard_map/all_gather | solution.py:1095
  7.9 369.5 %reduce-scatter.25.cloned.1.call-start = ((), (), s32[]{:S(2)}) async-start(), calls=%async_computation.21 | async-start | bytes 73728 | tf_op jit(solution)/shard_map/reduce_scatter | solution.py:1098
  12.3 5.0 copy-start.20
  12.4 5.0 copy-start.21
  12.4 5.0 copy-start.22
  258.5 10.0 slice-start.2
  259.5 8.9 copy-start.12
  259.5 9.0 slice-start.3
  259.5 16.2 %slice-start = ((s8[5767168]{0:T(1024)(128)(4,1)}), s8[4194304]{0:T(1024)(128)(4,1)S(1)}, s32[]{:S(2)}) async-start(s8[5767168]{0:T(1024)(128)(4,1)} %bitcast.255), calls=%async_computation.33 | async-start | bytes 8388608
  268.5 7.3 copy-start.34
  268.5 7.3 slice-start.1
  275.7 5.3 copy-start.35
  306.2 6.0 copy-start.31
  306.2 6.0 copy-start.5
  306.2 6.0 copy-start.10
  327.3 143.2 %reduce-scatter.23.cloned.1.call-start = ((), (), s32[]{:S(2)}) async-start(), calls=%async_computation.20 | async-start | bytes 4718592 | tf_op jit(solution)/shard_map/reduce_scatter | solution.py:1098
  327.3 11.4 slice-start.4
  327.9 10.9 slice-start.5
  338.8 5.1 copy-start.38
  338.8 5.1 copy-start.37
  364.0 202.1 %all-gather.5.cloned.1.call-start = ((), (), s32[]{:S(2)}) async-start(), calls=%async_computation.22 | async-start | bytes 4718592 | tf_op jit(solution)/shard_map/all_gather | solution.py:1089
  365.4 382.8 %copy-start.16 = (f32[128]{0:T(128)}, f32[128]{0:T(128)S(1)}, u32[]{:S(2)}) copy-start(f32[128]{0:T(128)S(1)} %add_rsqrt_fusion.1) | copy-start | bytes 1540
  473.6 10.7 copy-start.17
  476.8 219.5 %all-reduce.11.cloned.1.call-start = ((), (), s32[]{:S(2)}) async-start(), calls=%async_computation.32 | async-start | bytes 17301504
  538.8 225.6 %reduce-scatter.41.cloned.1.call-start = ((), (), s32[]{:S(2)}) async-start(), calls=%async_computation.31 | async-start | bytes 7208960 | tf_op jit(solution)/shard_map/reduce_scatter | solution.py:1285
  547.1 264.4 %reduce-scatter.37.cloned.1.call-start = ((), (), s32[]{:S(2)}) async-start(), calls=%async_computation.29 | async-start | bytes 7208960 | tf_op jit(solution)/shard_map/reduce_scatter | solution.py:1285
  557.5 311.6 %reduce-scatter.39.cloned.1.call-start = ((), (), s32[]{:S(2)}) async-start(), calls=%async_computation.30 | async-start | bytes 7208960 | tf_op jit(solution)/shard_map/reduce_scatter | solution.py:1285
  566.0 330.5 %reduce-scatter.29.cloned.1.call-start = ((), (), s32[]{:S(2)}) async-start(), calls=%async_computation.25 | async-start | bytes 1310720 | tf_op jit(solution)/shard_map/reduce_scatter | solution.py:1069
  566.1 19.1 %copy-start.24 = (bf16[1024,2048]{1,0:T(8,128)(2,1)S(1)}, bf16[1024,2048]{1,0:T(8,128)(2,1)}, u32[]{:S(2)}) copy-start(bf16[1024,2048]{1,0:T(8,128)(2,1)} %get-tuple-element.54) | copy-start | bytes 12582916
  588.7 336.0 %reduce-scatter.35.cloned.1.call-start = ((), (), s32[]{:S(2)}) async-start(), calls=%async_computation.28 | async-start | bytes 1310720 | tf_op jit(solution)/shard_map/reduce_scatter | solution.py:1073
  593.3 359.5 %reduce-scatter.33.cloned.1.call-start = ((), (), s32[]{:S(2)}) async-start(), calls=%async_computation.27 | async-start | bytes 1310720 | tf_op jit(solution)/shard_map/reduce_scatter | solution.py:1069
  598.0 382.8 %reduce-scatter.31.cloned.1.call-start = ((), (), s32[]{:S(2)}) async-start(), calls=%async_computation.26 | async-start | bytes 1310720 | tf_op jit(solution)/shard_map/reduce_scatter | solution.py:1069
  602.6 433.6 %reduce-scatter.27.cloned.1.call-start = ((), (), s32[]{:S(2)}) async-start(), calls=%async_computation.23 | async-start | bytes 4718592 | tf_op jit(solution)/shard_map/reduce_scatter | solution.py:1092
  603.4 524.7 %reduce-scatter.21.cloned.1.call-start = ((), (), s32[]{:S(2)}) async-start(), calls=%async_computation.18 | async-start | bytes 4718592 | tf_op jit(solution)/shard_map/reduce_scatter | solution.py:1098
  699.0 19.2 %all-to-all-start.4 = ((bf16[4,128,704]{1,2,0:T(8,128)(2,1)}), bf16[4,128,704]{1,2,0:T(8,128)(2,1)S(1)}, u32[]{:S(2)}, u32[]{:S(2)}) async-start(bf16[4,128,704]{1,2,0:T(8,128)(2,1)} %dynamic-slice_bitcast_fusion.2), calls=%async_computation.12 | async-start | bytes 1441792 | tf_op jit(solution)/shard_map/all_to_all | solution.py:1080
  703.6 44.0 %copy-start.8 = (bf16[128,2048]{1,0:T(8,128)(2,1)S(1)}, bf16[128,2048]{1,0:T(8,128)(2,1)}, u32[]{:S(2)}) copy-start(bf16[128,2048]{1,0:T(8,128)(2,1)} %refs_0_.1) | copy-start | bytes 1572868
  703.6 44.7 %copy-start.1 = (f32[128,2048]{1,0:T(8,128)S(1)}, f32[128,2048]{1,0:T(8,128)}, u32[]{:S(2)}) copy-start(f32[128,2048]{1,0:T(8,128)} %get-tuple-element.39) | copy-start | bytes 3145732
  718.2 21.3 %all-to-all-start.5 = ((bf16[4,128,704]{1,2,0:T(8,128)(2,1)}), bf16[4,128,704]{1,2,0:T(8,128)(2,1)S(1)}, u32[]{:S(2)}, u32[]{:S(2)}) async-start(bf16[4,128,704]{1,2,0:T(8,128)(2,1)} %dynamic-slice_bitcast_fusion.1), calls=%async_computation.13 | async-start | bytes 1441792 | tf_op jit(solution)/shard_map/all_to_all | solution.py:1080
  739.5 22.3 %all-to-all-start.6 = ((bf16[704,4,128]{2,0,1:T(8,128)(2,1)}), bf16[704,4,128]{2,0,1:T(8,128)(2,1)}, u32[]{:S(2)}, u32[]{:S(2)}) async-start(bf16[704,4,128]{2,0,1:T(8,128)(2,1)} %dynamic-slice_bitcast_fusion), calls=%async_computation.14 | async-start | bytes 1441792 | tf_op jit(solution)/shard_map/all_to_all | solution.py:1086
  814.6 57.6 %copy-start.18 = (f32[8,256]{1,0:T(8,128)S(1)}, f32[8,256]{1,0:T(8,128)}, u32[]{:S(2)}) copy-start(f32[8,256]{1,0:T(8,128)} %get-tuple-element.53) | copy-start | bytes 24580
  896.6 56.2 %all-to-all-start = ((bf16[4,128,256]{2,1,0:T(8,128)(2,1)}), bf16[4,128,256]{2,1,0:T(8,128)(2,1)S(1)}, u32[]{:S(2)}, u32[]{:S(2)}) async-start(bf16[4,128,256]{2,1,0:T(8,128)(2,1)} %bitcast.227), calls=%async_computation.5 | async-start | bytes 524288 | tf_op jit(solution)/shard_map/all_to_all | solution.py:1070
  952.8 28.1 %all-to-all-start.2 = ((bf16[4,128,256]{2,1,0:T(8,128)(2,1)}), bf16[4,128,256]{2,1,0:T(8,128)(2,1)S(1)}, u32[]{:S(2)}, u32[]{:S(2)}) async-start(bf16[4,128,256]{2,1,0:T(8,128)(2,1)} %bitcast.229), calls=%async_computation.9 | async-start | bytes 524288 | tf_op jit(solution)/shard_map/all_to_all | solution.py:1070
  980.9 9.9 all-to-all-start.1
  985.5 142.6 %copy-start.7 = (f32[128,2048]{1,0:T(8,128)S(1)}, f32[128,2048]{1,0:T(8,128)}, u32[]{:S(2)}) copy-start(f32[128,2048]{1,0:T(8,128)} %copy-done.6) | copy-start | bytes 3145732
  985.5 142.7 %copy-start.9 = (bf16[128,2048]{1,0:T(8,128)(2,1)S(1)}, bf16[128,2048]{1,0:T(8,128)(2,1)}, u32[]{:S(2)}) copy-start(bf16[128,2048]{1,0:T(8,128)(2,1)} %param.21) | copy-start | bytes 1572868
  990.8 9.4 all-to-all-start.3
  995.0 258.7 %all-reduce.9.cloned.1.call-start = ((), (), s32[]{:S(2)}) async-start(), calls=%async_computation.24 | async-start | bytes 262144 | tf_op jit(solution)/shard_map/psum | solution.py:1315
  (19 other events, 69.2 us)
Sparse Core Ops, SparseCore 0:
  10.2 92.5 all-gather.2
  327.4 49.9 reduce-scatter.24
  381.0 89.4 reduce-scatter.22
  476.9 36.8 all-gather.4
  538.9 157.3 all-reduce.10
  698.9 55.1 reduce-scatter.40
  756.6 54.8 reduce-scatter.36
  814.2 54.8 reduce-scatter.38
  871.4 25.1 reduce-scatter.28
  898.8 25.7 reduce-scatter.34
  926.9 25.7 reduce-scatter.32
  955.0 25.7 reduce-scatter.30
  984.2 51.9 reduce-scatter.26
  1040.2 87.9 reduce-scatter.20
  1133.5 120.1 all-reduce.8

commit v2 on v1

--- a/solution.py
+++ b/solution.py
@@ -523,10 +523,11 @@
             device_id_type=MESH_ID,
         )
 
-    def drain(self):
-        for item in self.own:
+    def drain(self, some=None):
+        for item in self.own if some is None else some:
             item.wait_send()
-        self.own = []
+        done = {id(item) for item in some} if some is not None else None
+        self.own = [] if done is None else [item for item in self.own if id(item) not in done]
 
 
 class Local:
@@ -968,65 +969,506 @@
     wire.drain()
 
 
-def attention_backward(
-    n_blocks, d_out, w_out, heads_weight, query, keys, values, lse, cosine, sine,
-    d_query_pre, d_key_pre, d_value_pre, d_bias, partial,
-    d_attn, d_keys, d_values,
+def chain_reduce(wire, place, parts):
+    n = place.n_dp
+    z = place.z
+    count = len(parts)
+    recv = wire.take(2 * n * count)
+    send = wire.take_send(2 * n * count)
+
+    def copies(target, up):
+        out = []
+        for index, (block, below, above) in enumerate(parts):
+            slot = (2 * target + (0 if up else 1)) * count + index
+            landing = below if up else above
+            out.append(
+                wire.copy_to(
+                    block(target),
+                    landing.at[target],
+                    place.up if up else place.down,
+                    recv + slot,
+                    send + slot,
+                )
+            )
+        return out
+
+    def collect(target, up):
+        for item, (block, below, above) in zip(copies(target, up), parts):
+            item.wait_recv()
+            add_block(block(target), (below if up else above).at[target])
+
+    def pass_on(target, up):
+        more = (z > 0) if up else (z < n - 1)
+        pl.when(more)(lambda: collect(target, up))
+        for item in copies(target, up):
+            item.start()
+
+    for step in range(n - 1):
+        high, low = n - 1 - step, step
+
+        @pl.when(z < n // 2)
+        def _():
+            pl.when(z < high)(lambda: pass_on(high, True))
+            pl.when(z > low)(lambda: pass_on(low, False))
+
+        @pl.when(z >= n // 2)
+        def _():
+            pl.when(z > low)(lambda: pass_on(low, False))
+            pl.when(z < high)(lambda: pass_on(high, True))
+
+        yield
+    pl.when(z > 0)(lambda: collect(z, True))
+    pl.when(z < n - 1)(lambda: collect(z, False))
+    for target in range(n):
+
+        @pl.when(z < target)
+        def _():
+            for item in copies(target, True):
+                item.wait_send()
+
+        @pl.when(z > target)
+        def _():
+            for item in copies(target, False):
+                item.wait_send()
+
+
+def add_block(target, extra):
+    step = 16
+
+    def one(index, carry):
+        here = rows_of(index, step)
+        total = target[here, :].astype(jnp.float32) + extra[here, :].astype(jnp.float32)
+        target[here, :] = total.astype(target.dtype)
+        return carry
+
+    lax.fori_loop(0, extra.shape[0] // step, one, 0)
+
+
+class Adder:
+    def __init__(self, sems):
+        self.sems = sems
+
+    def run(self, buf, chunks):
+        def load(index):
+            first, second, _ = chunks[index]
+            slot = index % 2
+            items = [
+                pltpu.make_async_copy(first, buf.at[0, slot], self.sems.at[3 * slot]),
+                pltpu.make_async_copy(second, buf.at[1, slot], self.sems.at[3 * slot + 1]),
+            ]
+            for item in items:
+                item.start()
+            return items
+
+        stores = [None, None]
+        loads = load(0)
+        for index, (_, _, target) in enumerate(chunks):
+            slot = index % 2
+            after = load(index + 1) if index + 1 < len(chunks) else None
+            for item in loads:
+                item.wait()
+            loads = after
+            if stores[slot] is not None:
+                stores[slot].wait()
+            total, first, second = buf.at[2, slot], buf.at[0, slot], buf.at[1, slot]
+
+            def one(step, carry):
+                here = rows_of(step, 16)
+                value = first[here, :].astype(jnp.float32) + second[here, :].astype(jnp.float32)
+                total[here, :] = value.astype(total.dtype)
+                return carry
+
+            lax.fori_loop(0, total.shape[0] // 16, one, 0)
+            stores[slot] = pltpu.make_async_copy(total, target, self.sems.at[3 * slot + 2])
+            stores[slot].start()
+        for item in stores:
+            if item is not None:
+                item.wait()
+
+
+def backward_kernel(
+    n_blocks, n_dp,
+    d_in_part, scalars, g_sgate, g_sup, g_sdown, g_egate, g_eup, g_edown,
+    hidden, out_grad, tokens, smalls, probs, mix,
+    heads_weight, w_out, query, keys, values, attn, lse, attn_in, cosine, sine,
+    input_grad, heads_grad, out_weight_grad, small_grad, bias_grad,
+    t_sgate, t_sup, t_sdown, r_egate, r_eup, r_edown, x_egate, x_eup, x_edown,
+    k_sgate, k_sup, k_sdown, r_sgate, r_sup, r_sdown, x_sgate, x_sup, x_sdown,
+    s_sgate, s_sup, s_sdown, k_egate, k_eup, k_edown,
+    partial, got_y, got_z, got_scalars, d_hidden, side, moe_own, terms, acc,
+    proj, d_attn, d_qkv, d_keys, d_values, got_core, got_one, got_two,
+    g_heads, g_out, heads_below, heads_above, out_below, out_above, out_block,
+    stage, landed, over_y, wide_buf, tall_buf, gate_buf, down_buf, send, recv, local, adds,
 ):
-    rows, width = d_out.shape
+    place = Place(n_dp)
+    wire = Wire(send, recv)
+    inside = Local(local)
+    adder = Adder(adds)
+    z, c, y = place.z, place.c, place.y
+    rows, width = tokens.shape
+    seq = proj.shape[0]
     cols = query.shape[1]
     head_dim = cosine.shape[1]
-    block = rows // n_blocks
+    block = seq // n_blocks
     scale = 1.0 / math.sqrt(head_dim)
-
-    def project(step, carry):
-        here = pl.ds(pl.multiple_of(step * block, block), block)
-        d_attn[here, :] = dot_f32(d_out[here, :], w_out[...], 1, 1).astype(jnp.bfloat16)
-        return carry
-
-    lax.fori_loop(0, n_blocks, project, 0)
-
-    def back(part, here):
-        return part * cosine[here, :] - pltpu.roll(part, head_dim // 2, 1) * sine[here, :]
-
+    n_ctx = 4
+    share = width // (n_dp * n_ctx)
+    n_experts = probs.shape[0]
+    f32, low = jnp.float32, jnp.bfloat16
+    core = lax.rem(c, 2)
+    others = [(dz, dc) for dz in range(n_dp) for dc in range(n_ctx) if dz or dc]
+
+    def moved(dz, dc, y_to):
+        return (lax.bitwise_xor(z, jnp.int32(dz)), lax.bitwise_xor(c, jnp.int32(dc)), y_to)
+
+    fill = inside.start(d_in_part, partial)
+    barrier(
+        [moved(dz, dc, y) for dz, dc in others] + [moved(dz, 0, place.yn) for dz in range(n_dp)]
+    )
+    fill.wait()
+
+    def group_rows(dz, y_of):
+        return rows_of(lax.bitwise_xor(z, jnp.int32(dz)) * 2 + y_of, rows)
+
+    order = (2, 3, 1, 0)
+    y_swaps = {}
+    for dz in order:
+        item = wire.copy(partial.at[group_rows(dz, place.yn), :], got_y.at[dz], place.over_y)
+        item.start()
+        y_swaps[dz] = item
+    group = z * 2 + y
+    scalar_items = []
+    for dz in range(n_dp):
+        for y_to in (y, place.yn):
+            target = lax.bitwise_xor(z, jnp.int32(dz)) * 2 + y_to
+            if dz == 0 and y_to is y:
+                item = inside.start(scalars.at[target], got_scalars.at[group])
+            else:
+                item = wire.copy(
+                    scalars.at[target], got_scalars.at[group], moved(dz, 0, y_to)
+                )
+                item.start()
+            scalar_items.append(item)
+
+    def piece(dx, sibling):
+        side_of = lax.bitwise_xor(lax.div(c, 2), jnp.int32(dx))
+        return side_of * 2 + (1 - core if sibling else core)
+
+    piece_cols = g_edown.shape[1] // n_ctx
+
+    def shared_blocks(dx, dz, sibling):
+        index = dz * n_ctx + piece(dx, sibling)
+        return [g_sgate.at[index], g_sup.at[index], g_sdown.at[:, rows_of(index, share)]]
+
+    def routed_pieces(dx, sibling):
+        index = piece(dx, sibling)
+        return [g_egate.at[index], g_eup.at[index], g_edown.at[:, rows_of(index, piece_cols)]]
+
+    shared_core = []
+    for dx in (1, 0):
+        for dz in range(n_dp):
+            for src, dst in zip(shared_blocks(dx, dz, True), (k_sgate, k_sup, k_sdown)):
+                item = wire.copy(src, dst.at[dx, dz], place.core)
+                item.start()
+                shared_core.append(item)
+    routed_core = []
+    for index, dst in enumerate((k_egate, k_eup, k_edown)):
+        for dx in (1, 0):
+            item = wire.copy(routed_pieces(dx, True)[index], dst.at[dx], place.core)
+            item.start()
+            routed_core.append(item)
+
+    for item in shared_core:
+        item.wait_recv()
+    shared_over = []
+    for index, (buf, kept, total, got) in enumerate(
+        (
+            (gate_buf, k_sgate, r_sgate, x_sgate),
+            (gate_buf, k_sup, r_sup, x_sup),
+            (down_buf, k_sdown, r_sdown, x_sdown),
+        )
+    ):
+        adder.run(
+            buf,
+            [
+                (shared_blocks(dx, dz, False)[index], kept.at[dx, dz], total.at[dx, dz])
+                for dx in (1, 0)
+                for dz in range(n_dp)
+            ],
+        )
+        item = wire.copy(total.at[1], got, place.over_x)
+        item.start()
+        shared_over.append(item)
+
+    z_swaps = []
+
+    def over_dp(dz):
+        y_swaps[dz].wait_recv()
+        target = lax.bitwise_xor(z, jnp.int32(dz)) * 2 + y
+        add_into(partial, pl.ds(0, width), target * rows, got_y.at[dz])
+        if dz:
+            item = wire.copy(
+                partial.at[rows_of(target, rows), :], got_z.at[dz - 1], moved(dz, 0, y)
+            )
+            item.start()
+            z_swaps.append(item)
+
+    def routed_sum(index):
+        for item in routed_core[2 * index : 2 * index + 2]:
+            item.wait_recv()
+        kept = (k_egate, k_eup, k_edown)[index]
+        total = (r_egate, r_eup, r_edown)[index]
+        buf = tall_buf if index == 2 else wide_buf
+        step = buf.shape[2]
+        chunks = []
+        for dx in (1, 0):
+            mine = routed_pieces(dx, False)[index]
+            for start in range(0, mine.shape[0], step):
+                at = pl.ds(start, step)
+                chunks.append((mine.at[at, :], kept.at[dx, at, :], total.at[dx, at, :]))
+        adder.run(buf, chunks)
+
+    over_dp(2)
+    routed_sum(0)
+    over_dp(3)
+    routed_sum(1)
+    over_dp(1)
+    routed_sum(2)
+    over_dp(0)
+
+    for item in scalar_items:
+        item.wait_recv()
+    d_rprobs = got_scalars[:, 0, :]
+    probs_own = probs[...]
+    d_logits = probs_own * (d_rprobs - jnp.sum(probs_own * d_rprobs, axis=0, keepdims=True))
+    shared_dot = jnp.sum(got_scalars[:, 1, :], axis=0, keepdims=True)
+    d_mix = shared_dot * mix[...] * (1.0 - mix[...])
+    d_side = jnp.concatenate(
+        [d_logits, jnp.broadcast_to(d_mix, (16 - n_experts, rows))], axis=0
+    )
+    row_of = lax.broadcasted_iota(jnp.int32, d_side.shape, 0)
+    d_side = jnp.where(row_of <= n_experts, d_side, 0.0)
+    first = d_side.astype(low)
+    rest = d_side - first.astype(f32)
+    second = rest.astype(low)
+    third = (rest - second.astype(f32)).astype(low)
+    terms[...] = jnp.concatenate([first, second, third], axis=0)
+    side[...] = dot_f32(terms[...], jnp.concatenate([smalls[...]] * 3, axis=0), 0, 0)
+    gain_one = smalls[n_experts + 1 : n_experts + 2, :].astype(f32)
+    gain_two = smalls[n_experts + 2 : n_experts + 3, :].astype(f32)
+    acc[...] = jnp.zeros_like(acc)
+    for item in z_swaps:
+        item.wait_recv()
+    own_plane = place.block(c, y) * rows
+
+    def norm_two(at):
+        mine = pl.ds(pl.multiple_of(group * rows + at.start, at.size), at.size)
+        d_moe = side[at, :] + partial[mine, :].astype(f32)
+        for dz in range(n_dp - 1):
+            d_moe = d_moe + got_z[dz, at, :].astype(f32)
+        total = hidden[at, :]
+        rstd = lax.rsqrt(jnp.mean(total * total, axis=1, keepdims=True) + EPS)
+        normed = total * rstd
+        acc[0] += d_moe * normed
+        d_norm = d_moe * gain_two
+        back = out_grad[at, :].astype(f32) + rstd * (
+            d_norm - normed * jnp.mean(d_norm * normed, axis=1, keepdims=True)
+        )
+        d_hidden[at, :] = back
+        moe_own[at, :] = (normed * gain_two).astype(low)
+        proj[pl.ds(pl.multiple_of(own_plane + at.start, at.size), at.size), :] = back.astype(low)
+
+    by_rows(rows, 16, norm_two)
+    proj_in = plane_gather(wire, place, proj)
+    next(proj_in)
+    side[0:48, :] = dot_f32(terms[...], moe_own[...], 1, 0)
+    next(proj_in)
+    next(proj_in)
+
+    shared_last = []
+    for index, (buf, total, got, ready, target) in enumerate(
+        (
+            (gate_buf, r_sgate, x_sgate, s_sgate, t_sgate),
+            (gate_buf, r_sup, x_sup, s_sup, t_sup),
+            (down_buf, r_sdown, x_sdown, s_sdown, t_sdown),
+        )
+    ):
+        shared_over[index].wait_recv()
+        adder.run(buf, [(total.at[0, dz], got.at[dz], ready.at[dz]) for dz in range(n_dp)])
+        for dz in (2, 3, 1, 0):
+            to = lax.bitwise_xor(z, jnp.int32(dz))
+            if dz:
+                item = wire.copy(ready.at[to], target.at[z], moved(dz, 0, y))
+                item.start()
+            else:
+                item = inside.start(ready.at[to], target.at[z])
+            shared_last.append(item)
+        if index == 0:
+            finish(proj_in)
+
+    def go_over_x(index):
+        total = (r_egate, r_eup, r_edown)[index]
+        got = (x_egate, x_eup, x_edown)[index]
+        item = wire.copy(total.at[1], got, place.over_x)
+        item.start()
+        return item
+
+    routed_over = [go_over_x(0)]
+    by_share = n_ctx * share
+
+    def out_weight(target):
+        at = rows_of(target, by_share)
+        g_out[:, at] = dot_f32(attn[...], proj[:, at], 0, 0).astype(low)
+
+    def each(count, body):
+        def one(index, carry):
+            body(index)
+            return carry
+
+        lax.fori_loop(0, count, one, 0)
+
+    each(n_dp, out_weight)
+    out_chain = chain_reduce(
+        wire, place, [(lambda t: g_out.at[:, rows_of(t, by_share)], out_below, out_above)]
+    )
+    next(out_chain)
+
+    def project(at):
+        d_attn[at, :] = dot_f32(proj[at, :], w_out[...], 1, 1).astype(low)
+
+    by_rows(seq, block, project)
+
+    def turn(part, at):
+        return part * cosine[at, :] - pltpu.roll(part, head_dim // 2, 1) * sine[at, :]
+
+    every = slice(0, seq)
     for start in range(0, cols, head_dim):
         lanes = slice(start, start + head_dim)
         d_keys[...] = jnp.zeros_like(d_keys)
         d_values[...] = jnp.zeros_like(d_values)
         for step in range(n_blocks):
-            here = slice(step * block, (step + 1) * block)
+            at = slice(step * block, (step + 1) * block)
             seen = slice(0, (step + 1) * block)
-            q_here = query[here, lanes]
+            q_here = query[at, lanes]
             k_seen = keys[seen, lanes]
-            grad = d_attn[here, lanes]
+            grad = d_attn[at, lanes]
             scores = dot_f32(q_here, k_seen, 1, 1) * scale
-            probs = jnp.exp(scores - lse[here, start : start + 1])
+            weights = jnp.exp(scores - lse[at, start : start + 1])
             d_probs = dot_f32(grad, values[seen, lanes], 1, 1)
-            delta = jnp.sum(probs * d_probs, axis=1, keepdims=True)
-            d_scores = (probs * (d_probs - delta)).astype(jnp.bfloat16)
+            delta = jnp.sum(weights * d_probs, axis=1, keepdims=True)
+            d_scores = (weights * (d_probs - delta)).astype(low)
             d_query = dot_f32(d_scores, k_seen, 1, 0) * scale
-            d_query_pre[here, lanes] = back(d_query, here).astype(jnp.bfloat16)
+            d_qkv[at, lanes] = turn(d_query, at).astype(low)
             d_keys[seen, :] += dot_f32(d_scores, q_here, 0, 0) * scale
-            d_values[seen, :] += dot_f32(probs.astype(jnp.bfloat16), grad, 0, 0)
-        every = slice(0, rows)
-        d_key_pre[:, lanes] = back(d_keys[...], every).astype(jnp.bfloat16)
-        d_value_pre[:, lanes] = d_values[...].astype(jnp.bfloat16)
-    d_bias[...] = jnp.zeros_like(d_bias)
-    for index, kept in enumerate((d_query_pre, d_key_pre, d_value_pre)):
-        d_bias[index : index + 1, :] = jnp.sum(
-            kept[...].astype(jnp.float32), axis=0, keepdims=True
-        )
-
-    def output(step, carry):
-        here = pl.ds(pl.multiple_of(step * block, block), block)
-        total = 0.0
-        for index, kept in enumerate((d_query_pre, d_key_pre, d_value_pre)):
-            weight = heads_weight[:, index * cols : (index + 1) * cols]
-            total = total + dot_f32(kept[here, :], weight, 1, 1)
-        partial[here, :] = total.astype(jnp.bfloat16)
-        return carry
-
-    lax.fori_loop(0, n_blocks, output, 0)
+            d_values[seen, :] += dot_f32(weights.astype(low), grad, 0, 0)
+        d_qkv[:, cols + start : cols + start + head_dim] = turn(d_keys[...], every).astype(low)
+        d_qkv[:, 2 * cols + start : 2 * cols + start + head_dim] = d_values[...].astype(low)
+
+    wire.drain(list(y_swaps.values()) + z_swaps)
+
+    def output(at):
+        partial[at, :] = dot_f32(d_qkv[at, :], heads_weight[...], 1, 1).astype(low)
+
+    by_rows(seq, block, output)
+    reduce = plane_reduce(wire, place, partial, got_core, got_one, got_two)
+    next(reduce)
+
+    def heads_weights(target):
+        at = rows_of(target, by_share)
+        g_heads[at, :] = dot_f32(attn_in[:, at], d_qkv[...], 0, 0).astype(low)
+
+    each(n_dp // 2, heads_weights)
+    next(reduce)
+    each(n_dp // 2, lambda index: heads_weights(index + n_dp // 2))
+    heads_chain = chain_reduce(
+        wire,
+        place,
+        [(lambda t: g_heads.at[rows_of(t, by_share), :], heads_below, heads_above)],
+    )
+    next(heads_chain)
+    finish(reduce)
+    routed_over += [go_over_x(1), go_over_x(2)]
+
+    def norm_one(at):
+        d_attn_in = plane_sum(place, partial, got_one, got_two, at)
+        x_float = tokens[at, :].astype(f32)
+        rstd = lax.rsqrt(jnp.mean(x_float * x_float, axis=1, keepdims=True) + EPS)
+        normed = x_float * rstd
+        acc[1] += d_attn_in * normed
+        d_norm = d_attn_in * gain_one
+        input_grad[at, :] = (
+            d_hidden[at, :]
+            + rstd * (d_norm - normed * jnp.mean(d_norm * normed, axis=1, keepdims=True))
+        ).astype(low)
+
+    by_rows(rows, 16, norm_one)
+
+    side_grad = side[0:16, :] + side[16:32, :] + side[32:48, :]
+    row_of = lax.broadcasted_iota(jnp.int32, side_grad.shape, 0)
+    gain_one_grad = jnp.sum(acc[1], axis=0, keepdims=True)
+    gain_two_grad = jnp.sum(acc[0], axis=0, keepdims=True)
+    small_rows = jnp.where(
+        row_of == n_experts + 1,
+        gain_one_grad,
+        jnp.where(row_of == n_experts + 2, gain_two_grad, side_grad),
+    )
+    bias_sums = jnp.sum(d_qkv[...].astype(f32), axis=0, keepdims=True)
+    bias_rows = [
+        bias_sums[:, start : start + head_dim] for start in range(0, 3 * cols, head_dim)
+    ]
+    bias_rows += [jnp.zeros((8 - len(bias_rows), head_dim), f32)]
+    bias_rows = jnp.concatenate(bias_rows, axis=0)
+    for target in range(n_dp * n_ctx):
+        stage[target, 0:16, :] = small_rows[:, target * share : (target + 1) * share]
+        stage[target, 16:24, :] = bias_rows
+    mine = z * n_ctx + c
+    small_items = [inside.start(stage.at[mine], landed.at[mine])]
+    for dz, dc in others:
+        target = lax.bitwise_xor(z, jnp.int32(dz)) * n_ctx + lax.bitwise_xor(c, jnp.int32(dc))
+        item = wire.copy(stage.at[target], landed.at[mine], moved(dz, dc, y))
+        item.start()
+        small_items.append(item)
+    next(out_chain)
+    next(heads_chain)
+    for item in small_items:
+        item.wait_recv()
+    total = landed[0, 0:16, :]
+    for source in range(1, n_dp * n_ctx):
+        total = total + landed[source, 0:16, :]
+    over_y[0] = total
+    swap = wire.copy(over_y.at[0], over_y.at[1], place.over_y)
+    swap.start()
+    for context in range(n_ctx):
+        sums = landed[context, 16:24, :]
+        for source in range(1, n_dp):
+            sums = sums + landed[source * n_ctx + context, 16:24, :]
+        bias_grad[context] = sums
+    finish(out_chain)
+    finish(heads_chain)
+
+    out_block[...] = g_out[:, rows_of(z, by_share)]
+    last = []
+    for dc in range(n_ctx):
+        to = lax.bitwise_xor(c, jnp.int32(dc))
+        pairs = [
+            (
+                g_heads.at[pl.ds(pl.multiple_of(z * by_share + to * share, share), share), :],
+                heads_grad.at[c],
+            ),
+            (out_block.at[:, rows_of(to, share)], out_weight_grad.at[c]),
+        ]
+        for src, dst in pairs:
+            if dc:
+                item = wire.copy(src, dst, moved(0, dc, y))
+                item.start()
+            else:
+                item = inside.start(src, dst)
+            last.append(item)
+    swap.wait_recv()
+    small_grad[...] = over_y[0] + over_y[1]
+    for item in last + shared_last + routed_over:
+        item.wait_recv()
+    wire.drain()
 
 
 def tokens_plan(
@@ -1064,32 +1506,6 @@
     n_experts = w_router.shape[1]
     n_group = n_dp * n_half
     my_expert = dp * n_half + half
-
-    def heads_out(grad):
-        mine = lax.psum_scatter(grad.astype(low), DP, scatter_dimension=0, tiled=True)
-        return lax.all_to_all(mine, CONTEXT, split_axis=0, concat_axis=1, tiled=True).astype(f32)
-
-    def heads_out_rows(grad):
-        mine = lax.psum_scatter(grad.astype(low), DP, scatter_dimension=1, tiled=True)
-        return lax.all_to_all(mine, CONTEXT, split_axis=1, concat_axis=0, tiled=True).astype(f32)
-
-    def hidden_out(grad):
-        split = grad.astype(low).reshape(n_dp, n_ctx, -1, grad.shape[1])
-        mine = lax.psum_scatter(split, CONTEXT, scatter_dimension=1, tiled=True)
-        mine = mine.reshape(width // n_ctx, -1)
-        return lax.all_to_all(mine, DP, split_axis=0, concat_axis=1, tiled=True).astype(f32)
-
-    def hidden_out_rows(grad):
-        split = grad.astype(low).reshape(grad.shape[0], n_dp, n_ctx, -1)
-        mine = lax.psum_scatter(split, CONTEXT, scatter_dimension=2, tiled=True)
-        mine = mine.reshape(grad.shape[0], -1)
-        return lax.all_to_all(mine, DP, split_axis=1, concat_axis=0, tiled=True).astype(f32)
-
-    def plane_in(rows):
-        return lax.all_gather(rows, (CONTEXT, EXPERT), axis=0, tiled=True)
-
-    def plane_out(rows):
-        return lax.psum_scatter(rows, (CONTEXT, EXPERT), scatter_dimension=0, tiled=True)
 
     def group_in(rows):
         return lax.all_gather(rows, (DP, EXPERT), axis=0, tiled=True)
@@ -1220,121 +1636,123 @@
     d_gate_rows = jnp.sum(e_out.astype(f32) * dy_rows.astype(f32), axis=1).reshape(n_group, CAP)
     d_gate_tok = jnp.sum(jnp.where(chosen, d_gate_rows[:, :, None], 0.0), axis=1).reshape(-1)
     shared_dot = jnp.sum(shared * dy_float, axis=1)
-    scalars = jnp.concatenate(
-        [
-            jnp.where(jnp.arange(n_experts)[None, :] == my_expert, d_gate_tok[:, None], 0.0),
-            shared_dot[:, None],
-        ],
-        axis=1,
-    )
-    scalars = group_out(scalars)
-    d_in_own = group_out(d_in_part).astype(f32)
+    scalars = jnp.stack([d_gate_tok, shared_dot]).reshape(2, n_group, tok_rows).transpose(1, 0, 2)
+    scalars = jnp.pad(scalars, ((0, 0), (0, 6), (0, 0)))
     moe_sum = group_out(moe_part).astype(f32)
     mixed = (hidden_own + moe_sum).astype(low)
 
     own = my_expert * tok_rows
-    probs_own = lax.dynamic_slice_in_dim(router_probs, own, tok_rows, 0)
-    mix_own = lax.dynamic_slice_in_dim(mix, own, tok_rows, 0)
-    d_rprobs = scalars[:, :n_experts]
-    d_logits = probs_own * (d_rprobs - jnp.sum(probs_own * d_rprobs, axis=1, keepdims=True))
-    d_mixlogit = scalars[:, n_experts] * mix_own * (1.0 - mix_own)
-    d_side = jnp.concatenate([d_logits, d_mixlogit[:, None]], axis=1)
-    moe_own_float = moe_own.astype(f32)
-    side_grad = jnp.dot(d_side.T, moe_own_float, precision=HIGH)
-    d_moe_in = d_in_own + jnp.dot(
-        d_side, small[: n_experts + 1].astype(f32), precision=HIGH
-    )
-    gain_two_grad = jnp.sum(d_moe_in * normed_two, axis=0)
-    d_norm_two = d_moe_in * gain_two
-    d_hidden_own = dy_own + rstd_two * (
-        d_norm_two - normed_two * jnp.mean(d_norm_two * normed_two, axis=1, keepdims=True)
-    )
-    d_proj = plane_in(d_hidden_own.astype(low))
-
-    d_q_pre, d_k_pre, d_v_pre, d_bias, d_partial = pl.pallas_call(
-        lambda *refs: attention_backward(n_blocks, *refs),
+    probs_own = lax.dynamic_slice_in_dim(router_probs, own, tok_rows, 0).T
+    mix_own = lax.dynamic_slice_in_dim(mix, own, tok_rows, 0)[None]
+    g_sgate = left_operand(moe_in, d_sgate).astype(low).reshape(-1, share, hidden_units)
+    g_sup = left_operand(moe_in, d_sup).astype(low).reshape(-1, share, hidden_units)
+    g_sdown = left_operand(s_hidden, d_shared).astype(low)
+    g_egate = left_operand(rows_in, d_gate).astype(low).reshape(n_ctx, width // n_ctx, -1)
+    g_eup = left_operand(rows_in, d_up).astype(low).reshape(n_ctx, width // n_ctx, -1)
+    g_edown = left_operand(e_hidden, grads_in).astype(low)
+    units = g_edown.shape[0]
+    by_share = n_ctx * share
+    e_wide = (width // n_ctx, units)
+    e_tall = (units, width // n_ctx)
+    s_wide = (share, hidden_units)
+    s_tall = (hidden_units, share)
+    s_kinds = (s_wide, s_wide, s_tall)
+    e_kinds = (e_wide, e_wide, e_tall)
+    results = pl.pallas_call(
+        lambda *refs: backward_kernel(n_blocks, n_dp, *refs),
         out_shape=[
-            like((seq_len, cols), low),
-            like((seq_len, cols), low),
-            like((seq_len, cols), low),
-            like((8, cols), f32),
-            like((seq_len, width), low),
-        ],
-        in_specs=whole_vmem(9),
-        out_specs=whole_vmem(5),
+            like((tok_rows, width), low),
+            like((n_ctx, share, 3 * cols), low),
+            like((n_ctx, cols, share), low),
+            like((16, share), f32),
+            like((n_ctx, 8, head_dim), f32),
+        ]
+        + [like((n_dp, *kind), low) for kind in s_kinds]
+        + [like((2, *kind), low) for kind in e_kinds]
+        + [like(kind, low) for kind in e_kinds]
+        + [like((2, n_dp, *kind), low) for kind in s_kinds]
+        + [like((2, n_dp, *kind), low) for kind in s_kinds]
+        + [like((n_dp, *kind), low) for kind in s_kinds]
+        + [like((n_dp, *kind), low) for kind in s_kinds]
+        + [like((2, *kind), low) for kind in e_kinds],
+        in_specs=[anywhere] * 8 + [vmem] * 16,
+        out_specs=[vmem] + [anywhere] * 2 + [vmem] * 2 + [anywhere] * 24,
         scratch_shapes=[
+            pltpu.VMEM((seq_len, width), low),
+            pltpu.VMEM((n_dp, tok_rows, width), low),
+            pltpu.VMEM((n_dp - 1, tok_rows, width), low),
+            pltpu.VMEM((n_group, 8, tok_rows), f32),
+            pltpu.VMEM((tok_rows, width), f32),
+            pltpu.VMEM((tok_rows, width), f32),
+            pltpu.VMEM((tok_rows, width), low),
+            pltpu.VMEM((48, tok_rows), low),
+            pltpu.VMEM((2, 16, width), f32),
+            pltpu.VMEM((seq_len, width), low),
             pltpu.VMEM((seq_len, cols), low),
+            pltpu.VMEM((seq_len, 3 * cols), low),
             pltpu.VMEM((seq_len, head_dim), f32),
             pltpu.VMEM((seq_len, head_dim), f32),
+            pltpu.VMEM((4, tok_rows, width), low),
+            pltpu.VMEM((4, tok_rows, half_width), low),
+            pltpu.VMEM((2, tok_rows, half_width), low),
+            pltpu.VMEM((width, 3 * cols), low),
+            pltpu.VMEM((cols, width), low),
+            pltpu.VMEM((n_dp, by_share, 3 * cols), low),
+            pltpu.VMEM((n_dp, by_share, 3 * cols), low),
+            pltpu.VMEM((n_dp, cols, by_share), low),
+            pltpu.VMEM((n_dp, cols, by_share), low),
+            pltpu.VMEM((cols, by_share), low),
+            pltpu.VMEM((n_dp * n_ctx, 24, share), f32),
+            pltpu.VMEM((n_dp * n_ctx, 24, share), f32),
+            pltpu.VMEM((2, 16, share), f32),
+            pltpu.VMEM((3, 2, 128, units), low),
+            pltpu.VMEM((3, 2, units // 4, width // n_ctx), low),
+            pltpu.VMEM((3, 2, *s_wide), low),
+            pltpu.VMEM((3, 2, *s_tall), low),
+            pltpu.SemaphoreType.DMA((160,)),
+            pltpu.SemaphoreType.DMA((160,)),
+            pltpu.SemaphoreType.DMA((16,)),
+            pltpu.SemaphoreType.DMA((6,)),
         ],
-        name="attention_backward",
-        compiler_params=pltpu.CompilerParams(vmem_limit_bytes=56 * 2**20),
-    )(d_proj, wo, heads_weight, query, keys, values, lse, cosine, sine)
-    d_attn_in = plane_out(d_partial).astype(f32)
-    rstd_one = lax.rsqrt(jnp.mean(x_own * x_own, axis=1, keepdims=True) + EPS)
-    normed_one = x_own * rstd_one
-    d_norm_one = d_attn_in * gain_one
-    gain_one_grad = jnp.sum(d_attn_in * normed_one, axis=0)
-    input_grad = (
-        d_hidden_own
-        + rstd_one
-        * (d_norm_one - normed_one * jnp.mean(d_norm_one * normed_one, axis=1, keepdims=True))
-    ).astype(low)
-
+        name="backward",
+        compiler_params=pltpu.CompilerParams(
+            collective_id=2, has_side_effects=True, vmem_limit_bytes=63 * 2**20
+        ),
+    )(
+        d_in_part, scalars, g_sgate, g_sup, g_sdown, g_egate, g_eup, g_edown,
+        hidden_own, out_grad, tokens, small, probs_own, mix_own,
+        heads_weight, wo, query, keys, values, attn, lse, attn_in, cosine, sine,
+    )
+    input_grad, heads_grad, out_weight_grad, small_grad, bias_grad = results[:5]
+    s_done, e_own, e_other = results[5:8], results[8:11], results[11:14]
+    grad_sgate, grad_sup = (
+        grad.transpose(1, 0, 2).reshape(share, -1).astype(f32) for grad in s_done[:2]
+    )
+    grad_sdown = s_done[2].reshape(-1, share).astype(f32)
     routed = [
-        lax.psum_scatter(
-            grad[None].astype(low), CONTEXT, scatter_dimension=dim, tiled=True
-        ).astype(f32)
-        for grad, dim in (
-            (left_operand(rows_in, d_gate), 1),
-            (left_operand(rows_in, d_up), 1),
-            (left_operand(e_hidden, grads_in), 2),
-        )
+        (mine[0].astype(f32) + other.astype(f32))[None] for mine, other in zip(e_own, e_other)
     ]
-    grad_sgate = hidden_out(left_operand(moe_in, d_sgate))
-    grad_sup = hidden_out(left_operand(moe_in, d_sup))
-    grad_sdown = hidden_out_rows(left_operand(s_hidden, d_shared))
-    grad_out = heads_out_rows(left_operand(attn, d_proj))
-    grad_query = heads_out(left_operand(attn_in, d_q_pre))
-    grad_key = heads_out(left_operand(attn_in, d_k_pre))
-    grad_value = heads_out(left_operand(attn_in, d_v_pre))
-
-    all_bias = jnp.zeros((n_half, 3, half_heads, head_dim), f32)
-    all_bias = lax.dynamic_update_slice(
-        all_bias, d_bias[:3].reshape(1, 3, heads, head_dim), (half, 0, ctx * heads, 0)
-    )
-    rest = jnp.concatenate(
-        [
-            side_grad,
-            gain_one_grad[None],
-            gain_two_grad[None],
-            all_bias.reshape(-1, width),
-        ],
-        axis=0,
-    )
-    rest = lax.psum(rest, (DP, CONTEXT, EXPERT))
-    share = width // (n_dp * n_ctx)
-    place = dp * n_ctx + ctx
-    mine = lax.dynamic_slice_in_dim(rest[: n_experts + 3], place * share, share, 1)
-    bias_sum = rest[n_experts + 3 :].reshape(n_half, 3, half_heads, head_dim)
+    heads_grad = heads_grad.reshape(n_ctx, share, 3, cols).transpose(2, 1, 0, 3)
+    heads_grad = heads_grad.reshape(3, share, -1).astype(f32)
+    grad_out = out_weight_grad.reshape(-1, share).astype(f32)
+    bias_sum = bias_grad[:, : 3 * heads].reshape(n_ctx, 3, heads, head_dim)
+    bias_sum = bias_sum.transpose(1, 0, 2, 3).reshape(3, half_heads, head_dim)
     bias_share = head_dim // (n_dp * n_ctx)
-    bias_sum = lax.dynamic_slice(
-        bias_sum, (half, 0, 0, place * bias_share), (1, 3, half_heads, bias_share)
-    )[0]
+    bias_sum = lax.dynamic_slice_in_dim(bias_sum, (dp * n_ctx + ctx) * bias_share, bias_share, 2)
     return (
         mixed,
         input_grad,
-        mine[n_experts + 1],
-        grad_query,
-        grad_key,
-        grad_value,
+        small_grad[n_experts + 1],
+        heads_grad[0],
+        heads_grad[1],
+        heads_grad[2],
         bias_sum[0],
         bias_sum[1],
         bias_sum[2],
         grad_out,
-        mine[n_experts + 2],
-        mine[:n_experts].T,
-        mine[n_experts],
+        small_grad[n_experts + 2],
+        small_grad[:n_experts].T,
+        small_grad[n_experts],
         grad_sgate,
         grad_sup,
         grad_sdown,

time: 1270 us -> 734 us (0.58)
  waiting for transfers between devices: 675 us -> 0.7 us
  Pallas kernels: 255 us -> 519 us
  local copies, waits for them, and re-layouts: 79 us -> 29.5 us
  starting transfers between devices: 37.3 us -> 0.08 us
  matrix products: 167 us -> 144 us
  other arithmetic: 36.7 us -> 20.5 us
    pallas_call x1, Pallas kernels: 19.1 us -> 283 us  [tokens_plan(): pl.pallas_call(lambda *refs: backward_kernel(n_blocks, n_dp, *refs), out_...]
    reduce_scatter x8 -> x0, waiting for transfers between devices: 231 us -> none  [the longest x3 98 us: tokens_plan(): lax.psum_scatter(grad[None].astype(low), CONTEXT, scatter_dimension=dim,...]
    reduce_scatter x3 -> x1, waiting for transfers between devices: 192 us -> 0.01 us  [group_out(): return lax.psum_scatter(rows, (DP, EXPERT), scatter_dimension=0, tiled=True)]
    psum x1 -> x0, waiting for transfers between devices: 123 us -> none  [tokens_plan(): rest = lax.psum(rest, (DP, CONTEXT, EXPERT))]
    unnamed x16 -> x2, waiting for transfers between devices: 93.5 us -> 0.7 us
    reshape x9 -> x0, local copies, waits for them, and re-layouts: 46.1 us -> none  [the longest x4 34.2 us: hidden_out(): split = grad.astype(low).reshape(n_dp, n_ctx, -1, grad.shape[1])]
    all_to_all x7 -> x0, starting transfers between devices: 36.5 us -> none  [the longest x3 12.6 us: heads_out(): lax.all_to_all(mine, CONTEXT, split_axis=0, concat_axis=1, tiled=True)]
    all_to_all x7 -> x0, waiting for transfers between devices: 36 us -> none  [the longest x2 23.3 us: hidden_out(): lax.all_to_all(mine, DP, split_axis=0, concat_axis=1, tiled=True)]
  transfers between devices with their start and end apart: 22 -> 2, of which waited for: 17 -> 0; matrix products, arithmetic and copies ran while one was open for 19% -> 22% of each run, Pallas kernels for 20% -> 71%
where the time goes in v2:
time: 734 us; the launch traced here: 729 us
  Pallas kernels  519 us (71%)
  matrix products  144 us (20%)
  local copies, waits for them, and re-layouts  29.5 us (4%)
  other arithmetic  20.5 us (3%)
  between operations  14.9 us (2%)
    pallas_call x1, Pallas kernels, tokens_plan(): pl.pallas_call(lambda *refs: backward_kernel(n_blocks, n_dp, *refs), out_...  283 us
    pallas_call x1, Pallas kernels, tokens_plan(): pl.pallas_call(lambda *refs: forward_kernel(n_blocks, n_dp, *refs), out_s...  236 us
    dot_general x7, matrix products, mat_right(): return jnp.dot(left, right.T, preferred_element_type=jnp.float32)  51.2 us
    dot_general x6, matrix products, left_operand(): return jnp.dot(left.T, right, preferred_element_type=jnp.float32)  37.2 us
  transfers between devices with their start and end apart: 2, of which 0 were waited for; matrix products, arithmetic and copies ran while one was open for 22% of the time, Pallas kernels for 71%

profile of v2, /device:TPU:9, one launch (start us, length us, event | category | flops | bytes accessed | tf_op | source)
XLA Modules:
  0.0 729.0 jit_solution(11267017928461397858)
XLA Ops:
  8.1 1.5 copy.60
  9.5 1.2 copy.61
  11.1 1.2 copy.63
  13.5 1.9 fusion.49
  15.4 1.3 pad_maximum_fusion
  17.3 236.3 %forward.1 = (bf16[1024,2048]{1,0:T(8,128)(2,1)}, bf16[1024,256]{1,0:T(8,128)(2,1)}, bf16[1024,256]{1,0:T(8,128)(2,1)}, bf16[1024,256]{1,0:T(8,128)(2,1)}, bf16[...) custom-call(bf16[128,2048]{1,0:T(8,128)(2,1)} %refs_10_.1, ...), custom_call_target="tpu_custom_call" | custom-call | tf_op jit(solution)/shard_map/forward/pallas_call | solution.py:1539
  253.6 3.4 fusion.67
  258.6 3.3 convolution_convert_fusion.4
  262.0 8.7 %fusion.19 = f32[768,1408]{1,0:T(8,128)S(1)} fusion(bf16[768,2048]{1,0:T(8,128)(2,1)S(1)} %bitcast.181, bf16[1,2048,1408]{2,1,0:T(8,128)(2,1)} %param.37), kind=kOutput, calls=%fused_computation.30 | convolution fusion | flops 4429185024 | bytes 13238272 | tf_op jit(solution)/shard_map/dot_general | solution.py:1613
  270.7 7.0 multiply_convert_fusion.2
  277.7 5.2 fusion.22
  283.0 5.6 fusion.38
  288.8 1.5 copy-done.34
  290.3 4.9 fusion.68
  295.2 4.9 fusion.69
  300.1 10.1 %multiply_convert_fusion.3 = (bf16[1024,704]{0,1:T(8,128)(2,1)}, bf16[1024,704]{0,1:T(8,128)(2,1)S(1)}, bf16[1024,704]{0,1:T(8,128)(2,1)S(1)}) fusion(f32[1024,704]{0,1:T(8,128)} %fusion.68, f32[1024,704]{0,1:T(8,128)} %fusion.69, bf16[704,2048]{1,0:T(8,128)(2,1)} %get-tuple-element.54, bf16[1024,2048]{1,0:T(8,128)(2,1)} %all-gather.2.cloned.1.call-done, ...), kind=kOutput, calls=%fused_computation.49 | convolution fusion | flops 2969894912 | bytes 17174528 | tf_op jit(solution)/shard_map/dot_general | solution.py:63
  310.2 6.1 fusion.70
  316.3 4.5 convolution_convert_fusion.6
  320.8 7.1 fusion.1
  327.9 4.4 fusion.7
  333.5 12.0 %multiply_convert_fusion.1 = (bf16[768,1408]{1,0:T(8,128)(2,1)S(1)}, bf16[768,1408]{1,0:T(8,128)(2,1)}) fusion(f32[768,1408]{1,0:T(8,128)} %copy-done.39, f32[768,1408]{1,0:T(8,128)} %get-tuple-element.139, bf16[768,2048]{1,0:T(8,128)(2,1)S(1)} %bitcast.185, bf16[1,1408,2048]{2,1,0:T(8,128)(2,1)} %param.39), kind=kOutput, calls=%fused_computation.33 | convolution fusion | flops 4443242496 | bytes 21889024 | tf_op jit(solution)/shard_map/dot_general | solution.py:63
  345.6 6.8 fusion.13
  352.4 7.0 convolution_convert_fusion.2
  359.4 5.3 add_convert_fusion
  364.8 4.7 fusion.35
  369.5 4.5 convolution_convert_fusion.5
  373.9 2.2 fusion.8
  376.1 4.8 copy.64
  380.9 3.0 copy.65
  384.5 7.7 %convolution_convert_fusion.7.refs_4_ = bf16[704,2048]{1,0:T(8,128)(2,1)} fusion(bf16[1024,704]{0,1:T(8,128)(2,1)} %copy-done.38, bf16[1024,2048]{1,0:T(8,128)(2,1)} %all-gather.2.cloned.1.call-done, f32[1024]{0:T(1024)S(1)} %bitcast.202), kind=kOutput, calls=%fused_computation.42 | convolution fusion | flops 2960523264 | bytes 8523776 | tf_op jit(solution)/shard_map/dot_general | solution.py:59
  392.2 7.0 convolution_convert_fusion.1
  399.2 6.6 convolution_convert_fusion.refs_7_
  405.8 7.4 %fusion.3.refs_0_ = bf16[1024,2048]{1,0:T(8,128)(2,1)} fusion(f32[1024,2048]{1,0:T(8,128)} %fusion.70, f32[8,128,2048]{2,1,0:T(8,128)S(1)} %bitcast.172, bf16[1024,704]{0,1:T(8,128)(2,1)S(1)} %copy-done.37, bf16[2048,704]{1,0:T(8,128)(2,1)S(1)} %bitcast.221), kind=kOutput, calls=%fused_computation.6 | convolution fusion | flops 2959081472 | bytes 25296896 | tf_op jit(solution)/shard_map/dot_general | solution.py:63
  413.3 282.9 %backward.1 = (bf16[128,2048]{1,0:T(8,128)(2,1)}, bf16[4,128,768]{2,1,0:T(8,128)(2,1)}, bf16[4,256,128]{2,1,0:T(8,128)(2,1)}, f32[16,128]{1,0:T(8,128)}, f32[4,8...) custom-call(bf16[1024,2048]{1,0:T(8,128)(2,1)} %fusion.3.refs_0_, ...), custom_call_target="tpu_custom_call" | custom-call | tf_op jit(solution)/shard_map/backward/pallas_call | solution.py:1661
  696.2 1.4 copy.66
  697.7 1.0 copy.71
  698.7 1.0 copy.72
  699.7 1.0 copy.73
  701.4 1.5 copy.74
  702.9 1.3 convert_bitcast_fusion
  704.7 1.5 copy.75
  708.0 0.8 bitcast_convert_fusion.1
  708.9 3.8 fusion.29
  712.7 1.9 fusion.28
  714.6 1.4 copy-done.17
  716.0 2.0 fusion.27
  718.0 1.2 bitcast_convert_fusion
  719.2 1.9 add_convert_fusion.1
  (154 shorter events, 10.5 us)
Async XLA Ops:
  7.2 3.5 copy-start.15
  7.2 5.0 copy-start.24
  7.2 5.0 copy-start.25
  7.2 5.0 copy-start.26
  7.2 5.6 copy-start.27
  7.2 292.8 %all-gather.2.cloned.1.call-start = ((), (), s32[]{:S(2)}) async-start(), calls=%async_computation.2 | async-start | bytes 4718592 | tf_op jit(solution)/shard_map/all_gather | solution.py:1511
  8.0 711.3 %reduce-scatter.2.cloned.1.call-start = ((), (), s32[]{:S(2)}) async-start(), calls=%async_computation.1 | async-start | bytes 4718592 | tf_op jit(solution)/shard_map/reduce_scatter | solution.py:1514
  11.0 5.6 copy-start.28
  11.0 5.6 copy-start.29
  11.1 5.6 copy-start.30
  11.1 5.6 copy-start.31
  258.6 12.0 %slice-start.6 = ((s8[5767168]{0:T(1024)(128)(4,1)}), s8[4194304]{0:T(1024)(128)(4,1)S(1)}, s32[]{:S(2)}) async-start(s8[5767168]{0:T(1024)(128)(4,1)} %bitcast.214), calls=%async_computation.9 | async-start | bytes 8388608
  261.9 8.7 %copy-start.6 = (bf16[8,96,2048]{2,1,0:T(8,128)(2,1)}, bf16[8,96,2048]{2,1,0:T(8,128)(2,1)S(1)}, u32[]{:S(2)}) copy-start(bf16[8,96,2048]{2,1,0:T(8,128)(2,1)S(1)} %convolution_convert_fusion.4) | copy-start | bytes 9437188
  261.9 8.7 %slice-start.7 = ((s8[5767168]{0:T(1024)(128)(4,1)}), s8[1572864]{0:T(1024)(128)(4,1)S(1)}, s32[]{:S(2)}) async-start(s8[5767168]{0:T(1024)(128)(4,1)} %bitcast.214), calls=%async_computation.10 | async-start | bytes 3145728
  262.0 15.8 %slice-start.4 = ((s8[5767168]{0:T(1024)(128)(4,1)}), s8[4194304]{0:T(1024)(128)(4,1)S(1)}, s32[]{:S(2)}) async-start(s8[5767168]{0:T(1024)(128)(4,1)} %bitcast.212), calls=%async_computation.7 | async-start | bytes 8388608
  270.7 7.0 copy-start.39
  270.7 7.0 slice-start.5
  277.7 5.3 copy-start.40
  283.0 5.8 copy-start.3
  283.0 5.8 copy-start
  283.0 7.3 %copy-start.34 = (bf16[4,4,128,704]{3,2,1,0:T(8,128)(2,1)S(1)}, bf16[4,4,128,704]{3,2,1,0:T(8,128)(2,1)}, u32[]{:S(2)}) copy-start(bf16[4,4,128,704]{3,2,1,0:T(8,128)(2,1)} %get-tuple-element.52) | copy-start | bytes 8650756
  290.3 4.9 copy-start.32
  300.1 20.7 %slice-start.2 = ((s8[8388608]{0:T(1024)(128)(4,1)}), s8[4194304]{0:T(1024)(128)(4,1)S(1)}, s32[]{:S(2)}) async-start(s8[8388608]{0:T(1024)(128)(4,1)} %bitcast.173), calls=%async_computation.5 | async-start | bytes 8388608
  310.2 10.6 %copy-start.38 = (bf16[1024,704]{0,1:T(8,128)(2,1)}, bf16[1024,704]{0,1:T(8,128)(2,1)S(1)}, u32[]{:S(2)}) copy-start(bf16[1024,704]{0,1:T(8,128)(2,1)S(1)} %get-tuple-element.125) | copy-start | bytes 4325380
  310.2 6.1 copy-start.1
  310.2 10.6 %slice-start.3 = ((s8[8388608]{0:T(1024)(128)(4,1)}), s8[4194304]{0:T(1024)(128)(4,1)S(1)}, s32[]{:S(2)}) async-start(s8[8388608]{0:T(1024)(128)(4,1)} %bitcast.173), calls=%async_computation.6 | async-start | bytes 8388608
  316.3 4.5 copy-start.5
  316.3 4.5 copy-start.35
  332.9 12.6 %slice-start.8 = ((s8[5767168]{0:T(1024)(128)(4,1)}), s8[4194304]{0:T(1024)(128)(4,1)S(1)}, s32[]{:S(2)}) async-start(s8[5767168]{0:T(1024)(128)(4,1)} %bitcast.216), calls=%async_computation.11 | async-start | bytes 8388608
  333.5 12.0 %slice-start.9 = ((s8[5767168]{0:T(1024)(128)(4,1)}), s8[1572864]{0:T(1024)(128)(4,1)S(1)}, s32[]{:S(2)}) async-start(s8[5767168]{0:T(1024)(128)(4,1)} %bitcast.216), calls=%async_computation.12 | async-start | bytes 3145728
  333.5 25.9 %slice-start.10 = ((s8[5767168]{0:T(1024)(128)(4,1)}), s8[4194304]{0:T(1024)(128)(4,1)S(1)}, s32[]{:S(2)}) async-start(s8[5767168]{0:T(1024)(128)(4,1)} %bitcast.218), calls=%async_computation.13 | async-start | bytes 8388608
  345.5 6.9 copy-start.7
  345.6 13.9 %slice-start.11 = ((s8[5767168]{0:T(1024)(128)(4,1)}), s8[1572864]{0:T(1024)(128)(4,1)S(1)}, s32[]{:S(2)}) async-start(s8[5767168]{0:T(1024)(128)(4,1)} %bitcast.218), calls=%async_computation.14 | async-start | bytes 3145728
  364.8 4.7 copy-start.2
  364.8 4.7 copy-start.36
  376.1 4.8 copy-start.10
  384.5 7.7 %copy-start.8 = (bf16[8,96,2048]{2,1,0:T(8,128)(2,1)S(1)}, bf16[8,96,2048]{2,1,0:T(8,128)(2,1)}, u32[]{:S(2)}) copy-start(bf16[8,96,2048]{2,1,0:T(8,128)(2,1)} %copy-done.6) | copy-start | bytes 9437188
  384.5 7.7 %copy-start.42 = (bf16[768,1408]{1,0:T(8,128)(2,1)S(1)}, bf16[768,1408]{1,0:T(8,128)(2,1)}, u32[]{:S(2)}) copy-start(bf16[768,1408]{1,0:T(8,128)(2,1)} %get-tuple-element.120) | copy-start | bytes 6488068
  384.5 21.3 %slice-start = ((s8[8388608]{0:T(1024)(128)(4,1)}), s8[4194304]{0:T(1024)(128)(4,1)S(1)}, s32[]{:S(2)}) async-start(s8[8388608]{0:T(1024)(128)(4,1)} %bitcast.171), calls=%async_computation.3 | async-start | bytes 8388608
  392.2 7.0 copy-start.9
  392.2 7.0 copy-start.41
  392.2 13.6 %slice-start.1 = ((s8[8388608]{0:T(1024)(128)(4,1)}), s8[4194304]{0:T(1024)(128)(4,1)S(1)}, s32[]{:S(2)}) async-start(s8[8388608]{0:T(1024)(128)(4,1)} %bitcast.171), calls=%async_computation.4 | async-start | bytes 8388608
  399.2 6.6 copy-start.33
  399.2 6.6 copy-start.37
  704.2 3.8 copy-start.20
  704.7 4.2 copy-start.13
  708.0 4.7 copy-start.12
  708.0 4.7 copy-start.18
  (9 other events, 27.3 us)
Sparse Core Ops, SparseCore 0:
  10.2 95.3 all-gather.1
  328.1 86.8 reduce-scatter.1

commit v3 on v2

--- a/solution.py
+++ b/solution.py
@@ -2,6 +2,7 @@
 
 import jax
 import jax.numpy as jnp
+import numpy as np
 from jax import lax
 from jax.experimental import pallas as pl
 from jax.experimental.pallas import tpu as pltpu
@@ -543,6 +544,18 @@
         return item
 
 
+class Phases:
+    def __init__(self):
+        self.scope = None
+
+    def go(self, name):
+        if self.scope is not None:
+            self.scope.__exit__(None, None, None)
+        self.scope = jax.named_scope(name) if name else None
+        if name:
+            self.scope.__enter__()
+
+
 class Place:
     def __init__(self, n_dp):
         self.n_dp = n_dp
@@ -582,7 +595,7 @@
     lax.fori_loop(0, total // step, one, 0)
 
 
-def chain_gather(wire, place, refs, arrived=None):
+def chain_gather(wire, place, refs, arrived=None, own=None):
     n = place.n_dp
     z = place.z
     width = len(refs(z))
@@ -592,7 +605,7 @@
     def copies(slot, up, dist):
         return [
             wire.copy_to(
-                ref,
+                own[index] if own is not None and dist == 0 else ref,
                 ref,
                 place.up if up else place.down,
                 recv + slot * width + index,
@@ -764,9 +777,10 @@
     n_blocks, n_dp,
     tokens, small, ids, w_query, w_key, w_value, w_out, s_gate, s_up, s_down,
     bias, cosine, sine,
-    attn_in, query, keys, values, attn, lse, hidden, moe_in,
-    heads_weight, out_weight, gate_weight, up_weight, down_weight, smalls, all_ids,
-    x_seq, partial, got_core, got_one, got_two, send, recv, local,
+    attn_in_to, query_to, keys_to, values_to, attn_to, lse_to, hidden_to, moe_in,
+    heads_weight_to, out_weight_to, gate_weight, up_weight, down_weight, smalls, all_ids,
+    x_seq, partial, got_core, got_one, got_two,
+    attn_in, query, keys, values, attn, lse, hidden, heads_weight, out_weight, send, recv, local,
 ):
     place = Place(n_dp)
     wire = Wire(send, recv)
@@ -783,6 +797,8 @@
     f32, low = jnp.float32, jnp.bfloat16
 
     others = [(dz, dc) for dz in range(n_dp) for dc in range(n_ctx) if dz or dc]
+    phases = Phases()
+    phases.go("entry")
 
     def moved(dz, dc, y_to):
         return (lax.bitwise_xor(z, jnp.int32(dz)), lax.bitwise_xor(c, jnp.int32(dc)), y_to)
@@ -793,6 +809,27 @@
 
     mine = z * n_ctx + c
     my_rows = rows_of(mine, share)
+    group = z * 2 + y
+    shared_pieces = [[], [], []]
+
+    def shared_along_dp(index):
+        for dz in (2, 3, 1, 0):
+            to = lax.bitwise_xor(z, jnp.int32(dz))
+            if index == 2:
+                src = s_down.at[rows_of(to, s_down.shape[0] // n_dp), :]
+                dst = down_weight.at[:, my_rows]
+            else:
+                src = (s_gate, s_up)[index].at[to]
+                dst = (gate_weight, up_weight)[index].at[z, c]
+            if dz == 0:
+                item = inside.start(src, dst)
+            else:
+                item = wire.copy(src, dst, moved(dz, 0, y))
+                item.start()
+            shared_pieces[index].append(item)
+
+    shared_along_dp(0)
+
     exchanges = []
     for dc in range(n_ctx):
         to = lax.bitwise_xor(c, jnp.int32(dc))
@@ -812,14 +849,11 @@
     own_rows = rows_of(place.block(c, y), rows)
     here = inside.start(tokens, x_seq.at[own_rows, :])
     here.wait()
-    tokens_in = plane_gather(wire, place, x_seq)
-    next(tokens_in)
     small_copies = [inside.start(small, smalls.at[:, my_rows])]
     for dz, dc in others:
         item = wire.copy(small, smalls.at[:, my_rows], moved(dz, dc, y))
         item.start()
         small_copies.append(item)
-    group = z * 2 + y
     small_copies.append(inside.start(ids, all_ids.at[group]))
     for dz in range(n_dp):
         for y_to in (y, place.yn):
@@ -827,16 +861,19 @@
                 item = wire.copy(ids, all_ids.at[group], moved(dz, 0, y_to))
                 item.start()
                 small_copies.append(item)
+    phases.go("exchanges")
     for item in exchanges:
         item.wait_recv()
 
-    def attention_blocks(slot):
-        at = rows_of(slot, n_ctx * share)
-        return [heads_weight.at[at, :], out_weight.at[:, at]]
-
-    weights_in = chain_gather(wire, place, attention_blocks)
+    def from_place(slot):
+        return rows_of(slot, n_ctx * share)
+
+    weights_in = chain_gather(wire, place, lambda slot: [heads_weight.at[from_place(slot), :]])
     next(weights_in)
+    phases.go("tokens")
+    tokens_in = plane_gather(wire, place, x_seq)
     finish(tokens_in)
+    next(weights_in)
     for item in small_copies:
         item.wait_recv()
 
@@ -849,24 +886,41 @@
         attn_in[at, :] = (x_float * rstd * gain_one).astype(low)
 
     by_rows(seq, 64, norm_one)
+    def shared_set(index, context):
+        if index < 2:
+            return [(gate_weight, up_weight)[index].at[:, context]]
+        return [
+            down_weight.at[:, rows_of(dz * n_ctx + context, share)] for dz in range(n_dp)
+        ]
+
+    over = [[], [], []]
+    close = []
+
+    def shared_over_x(index):
+        for item in shared_pieces[index]:
+            item.wait_recv()
+        for ref in shared_set(index, c):
+            item = wire.copy(ref, ref, place.over_x)
+            item.start()
+            over[index].append(item)
+        for ref in shared_set(index, c):
+            item = wire.copy(ref, ref, place.core)
+            item.start()
+            close.append(item)
+
+    def shared_close(index):
+        for item, ref in zip(over[index], shared_set(index, place.cx)):
+            item.wait_recv()
+            item = wire.copy(ref, ref, place.core)
+            item.start()
+            close.append(item)
+
+    shared_over_x(0)
+    phases.go("heads_weights")
     finish(weights_in)
-
-    shared_pieces = []
-    for dz in range(n_dp):
-        to = lax.bitwise_xor(z, jnp.int32(dz))
-        hidden_rows = rows_of(to, s_down.shape[0] // n_dp)
-        pairs = [
-            (s_gate.at[to], gate_weight.at[z, c]),
-            (s_up.at[to], up_weight.at[z, c]),
-            (s_down.at[hidden_rows, :], down_weight.at[:, my_rows]),
-        ]
-        for src, dst in pairs:
-            if dz == 0:
-                shared_pieces.append(inside.start(src, dst))
-            else:
-                item = wire.copy(src, dst, moved(dz, 0, y))
-                item.start()
-                shared_pieces.append(item)
+    phases.go("attention")
+    out_in = chain_gather(wire, place, lambda slot: [out_weight.at[:, from_place(slot)]])
+    next(out_in)
 
     def project(at):
         pre = dot_f32(attn_in[at, :], heads_weight[...], 1, 0)
@@ -882,6 +936,7 @@
                 kept[at, start : start + head_dim] = part.astype(low)
 
     by_rows(seq, block, project)
+    next(out_in)
     for start in range(0, cols, head_dim):
         lanes = slice(start, start + head_dim)
         for step in range(n_blocks):
@@ -894,12 +949,33 @@
             probs = (expo / total).astype(low)
             attn[at, lanes] = dot_f32(probs, values[seen, lanes], 1, 0).astype(low)
             lse[at, lanes] = jnp.broadcast_to(top + jnp.log(total), (block, head_dim))
+        if start == 0:
+            next(out_in)
+    phases.go("out_weights")
+    finish(out_in)
+    shared_along_dp(1)
+    shared_along_dp(2)
+    phases.go("attention_out")
 
     def output(at):
         partial[at, :] = dot_f32(attn[at, :], out_weight[...], 1, 0).astype(low)
 
     by_rows(seq, block, output)
-    finish(plane_reduce(wire, place, partial, got_core, got_one, got_two))
+    stores = [
+        inside.start(src, dst)
+        for src, dst in (
+            (attn_in, attn_in_to), (query, query_to), (keys, keys_to), (values, values_to),
+            (attn, attn_to), (lse, lse_to), (heads_weight, heads_weight_to),
+            (out_weight, out_weight_to),
+        )
+    ]
+    phases.go("sum_in_plane")
+    reduce = plane_reduce(wire, place, partial, got_core, got_one, got_two)
+    next(reduce)
+
+    next(reduce)
+    finish(reduce)
+    phases.go("norm_two")
 
     def norm_two(at):
         start = place.block(c, y) * rows + at.start
@@ -910,6 +986,7 @@
         got_core[0, at, :] = (total * rstd * gain_two).astype(low)
 
     by_rows(rows, 16, norm_two)
+    stores.append(inside.start(hidden, hidden_to))
     at_group = rows_of(group, rows)
     here = inside.start(got_core.at[0], moe_in.at[at_group, :])
     here.wait()
@@ -937,36 +1014,29 @@
     )
     next(rows_chain)
     to_y(z).start()
-    for item in shared_pieces:
-        item.wait_recv()
-
-    def shared_set(context):
-        return [gate_weight.at[:, context], up_weight.at[:, context]] + [
-            down_weight.at[:, rows_of(dz * n_ctx + context, share)] for dz in range(n_dp)
-        ]
-
-    over = []
-    for ref in shared_set(c):
-        item = wire.copy(ref, ref, place.over_x)
-        item.start()
-        over.append(item)
-    close = []
-    for ref in shared_set(c):
-        item = wire.copy(ref, ref, place.core)
-        item.start()
-        close.append(item)
+    phases.go("rows_one")
+    next(rows_chain)
+    phases.go("shared_one")
+    shared_over_x(1)
+    phases.go("rows_two")
+    next(rows_chain)
+    phases.go("shared_two")
+    shared_over_x(2)
+    phases.go("rows_three")
     finish(rows_chain)
-    for item, ref in zip(over, shared_set(place.cx)):
-        item.wait_recv()
-        item = wire.copy(ref, ref, place.core)
-        item.start()
-        close.append(item)
+    phases.go("shared_close")
+    for index in range(3):
+        shared_close(index)
     for item in close:
         item.wait_recv()
+    phases.go("rows_over_y")
     for slot in range(n_dp):
         from_y(slot).wait_recv()
         to_y(slot).wait_send()
+    for item in stores:
+        item.wait()
     wire.drain()
+    phases.go(None)
 
 
 def chain_reduce(wire, place, parts):
@@ -998,20 +1068,34 @@
             add_block(block(target), (below if up else above).at[target])
 
     def pass_on(target, up):
-        more = (z > 0) if up else (z < n - 1)
-        pl.when(more)(lambda: collect(target, up))
+        collect(target, up)
         for item in copies(target, up):
             item.start()
 
+    def first(target, up):
+        for item in copies(target, up):
+            item.start()
+
+    @pl.when(z == 0)
+    def _():
+        for target in range(n - 1, 0, -1):
+            first(target, True)
+
+    @pl.when(z == n - 1)
+    def _():
+        for target in range(n - 1):
+            first(target, False)
+
+    yield
     for step in range(n - 1):
         high, low = n - 1 - step, step
 
-        @pl.when(z < n // 2)
+        @pl.when((z > 0) & (z < n // 2))
         def _():
             pl.when(z < high)(lambda: pass_on(high, True))
             pl.when(z > low)(lambda: pass_on(low, False))
 
-        @pl.when(z >= n // 2)
+        @pl.when((z >= n // 2) & (z < n - 1))
         def _():
             pl.when(z > low)(lambda: pass_on(low, False))
             pl.when(z < high)(lambda: pass_on(high, True))
@@ -1088,17 +1172,19 @@
 
 def backward_kernel(
     n_blocks, n_dp,
-    d_in_part, scalars, g_sgate, g_sup, g_sdown, g_egate, g_eup, g_edown,
-    hidden, out_grad, tokens, smalls, probs, mix,
-    heads_weight, w_out, query, keys, values, attn, lse, attn_in, cosine, sine,
+    d_in_part, scalars, k_sgate, k_sup, k_sdown, x_sgate, x_sup, x_sdown, g_egate, g_eup, g_edown,
+    hidden_in, out_grad_in, tokens_in, smalls, probs, mix,
+    heads_weight_in, w_out_in, query_in, keys_in, values_in, attn_from, lse_in, attn_in_from,
+    cosine_in, sine_in,
     input_grad, heads_grad, out_weight_grad, small_grad, bias_grad,
     t_sgate, t_sup, t_sdown, r_egate, r_eup, r_edown, x_egate, x_eup, x_edown,
-    k_sgate, k_sup, k_sdown, r_sgate, r_sup, r_sdown, x_sgate, x_sup, x_sdown,
     s_sgate, s_sup, s_sdown, k_egate, k_eup, k_edown,
     partial, got_y, got_z, got_scalars, d_hidden, side, moe_own, terms, acc,
     proj, d_attn, d_qkv, d_keys, d_values, got_core, got_one, got_two,
     g_heads, g_out, heads_below, heads_above, out_below, out_above, out_block,
-    stage, landed, over_y, wide_buf, tall_buf, gate_buf, down_buf, send, recv, local, adds,
+    stage, landed, over_y, wide_buf, tall_buf, gate_buf, down_buf,
+    hidden, out_grad, tokens, heads_weight, w_out, query, keys, values, attn, lse, attn_in,
+    cosine, sine, send, recv, local, adds,
 ):
     place = Place(n_dp)
     wire = Wire(send, recv)
@@ -1121,6 +1207,8 @@
     def moved(dz, dc, y_to):
         return (lax.bitwise_xor(z, jnp.int32(dz)), lax.bitwise_xor(c, jnp.int32(dc)), y_to)
 
+    phases = Phases()
+    phases.go("entry")
     fill = inside.start(d_in_part, partial)
     barrier(
         [moved(dz, dc, y) for dz, dc in others] + [moved(dz, 0, place.yn) for dz in range(n_dp)]
@@ -1156,49 +1244,16 @@
 
     piece_cols = g_edown.shape[1] // n_ctx
 
-    def shared_blocks(dx, dz, sibling):
-        index = dz * n_ctx + piece(dx, sibling)
-        return [g_sgate.at[index], g_sup.at[index], g_sdown.at[:, rows_of(index, share)]]
-
     def routed_pieces(dx, sibling):
         index = piece(dx, sibling)
         return [g_egate.at[index], g_eup.at[index], g_edown.at[:, rows_of(index, piece_cols)]]
 
-    shared_core = []
-    for dx in (1, 0):
-        for dz in range(n_dp):
-            for src, dst in zip(shared_blocks(dx, dz, True), (k_sgate, k_sup, k_sdown)):
-                item = wire.copy(src, dst.at[dx, dz], place.core)
-                item.start()
-                shared_core.append(item)
     routed_core = []
     for index, dst in enumerate((k_egate, k_eup, k_edown)):
         for dx in (1, 0):
             item = wire.copy(routed_pieces(dx, True)[index], dst.at[dx], place.core)
             item.start()
             routed_core.append(item)
-
-    for item in shared_core:
-        item.wait_recv()
-    shared_over = []
-    for index, (buf, kept, total, got) in enumerate(
-        (
-            (gate_buf, k_sgate, r_sgate, x_sgate),
-            (gate_buf, k_sup, r_sup, x_sup),
-            (down_buf, k_sdown, r_sdown, x_sdown),
-        )
-    ):
-        adder.run(
-            buf,
-            [
-                (shared_blocks(dx, dz, False)[index], kept.at[dx, dz], total.at[dx, dz])
-                for dx in (1, 0)
-                for dz in range(n_dp)
-            ],
-        )
-        item = wire.copy(total.at[1], got, place.over_x)
-        item.start()
-        shared_over.append(item)
 
     z_swaps = []
 
@@ -1228,14 +1283,72 @@
                 chunks.append((mine.at[at, :], kept.at[dx, at, :], total.at[dx, at, :]))
         adder.run(buf, chunks)
 
+    def go_over_x(index, part=0, parts=1):
+        total = (r_egate, r_eup, r_edown)[index]
+        got = (x_egate, x_eup, x_edown)[index]
+        count = got.shape[0] // parts
+        at = pl.ds(part * count, count)
+        item = wire.copy(total.at[1, at, :], got.at[at, :], place.over_x)
+        item.start()
+        return item
+
+    def part_of(ref, dz):
+        size = ref.shape[0] // n_dp
+        return ref.at[pl.ds(dz * size, size), :]
+
+    def shared_ready(index):
+        buf = down_buf if index == 2 else gate_buf
+        kept = (k_sgate, k_sup, k_sdown)[index]
+        got = (x_sgate, x_sup, x_sdown)[index]
+        ready = (s_sgate, s_sup, s_sdown)[index]
+        adder.run(buf, [(part_of(kept, dz), part_of(got, dz), ready.at[dz]) for dz in range(n_dp)])
+
+    shared_last = []
+
+    def shared_along_dp(index):
+        ready = (s_sgate, s_sup, s_sdown)[index]
+        target = (t_sgate, t_sup, t_sdown)[index]
+        for dz in (2, 3, 1, 0):
+            to = lax.bitwise_xor(z, jnp.int32(dz))
+            if dz:
+                item = wire.copy(ready.at[to], target.at[z], moved(dz, 0, y))
+                item.start()
+            else:
+                item = inside.start(ready.at[to], target.at[z])
+            shared_last.append(item)
+
+    loads = [
+        inside.start(src, dst)
+        for src, dst in (
+            (hidden_in, hidden), (out_grad_in, out_grad), (tokens_in, tokens), (attn_from, attn),
+            (w_out_in, w_out), (query_in, query), (keys_in, keys), (values_in, values),
+            (lse_in, lse), (cosine_in, cosine), (sine_in, sine), (heads_weight_in, heads_weight),
+            (attn_in_from, attn_in),
+        )
+    ]
+    phases.go("routed_gate")
+    routed_sum(0)
+    routed_over = [go_over_x(0)]
+    phases.go("over_dp_two")
     over_dp(2)
-    routed_sum(0)
+    phases.go("routed_up")
+    routed_sum(1)
+    routed_over.append(go_over_x(1, 0, 2))
+    phases.go("over_dp_three")
     over_dp(3)
-    routed_sum(1)
+    phases.go("routed_down")
+    routed_sum(2)
+    phases.go("over_dp_one")
     over_dp(1)
-    routed_sum(2)
+    phases.go("shared_ready")
+    shared_ready(0)
+    shared_ready(1)
+    phases.go("over_dp_own")
     over_dp(0)
-
+    phases.go("shared_ready_last")
+    shared_ready(2)
+
+    phases.go("router")
     for item in scalar_items:
         item.wait_recv()
     d_rprobs = got_scalars[:, 0, :]
@@ -1257,6 +1370,7 @@
     gain_one = smalls[n_experts + 1 : n_experts + 2, :].astype(f32)
     gain_two = smalls[n_experts + 2 : n_experts + 3, :].astype(f32)
     acc[...] = jnp.zeros_like(acc)
+    phases.go("wait_sums")
     for item in z_swaps:
         item.wait_recv()
     own_plane = place.block(c, y) * rows
@@ -1278,42 +1392,26 @@
         moe_own[at, :] = (normed * gain_two).astype(low)
         proj[pl.ds(pl.multiple_of(own_plane + at.start, at.size), at.size), :] = back.astype(low)
 
+    phases.go("norm_two")
+    for item in loads:
+        item.wait()
     by_rows(rows, 16, norm_two)
+    phases.go("gather_in_plane")
     proj_in = plane_gather(wire, place, proj)
     next(proj_in)
     side[0:48, :] = dot_f32(terms[...], moe_own[...], 1, 0)
+
+    for index in range(3):
+        shared_along_dp(index)
+    phases.go("gather_relay")
     next(proj_in)
+    phases.go("gather_close")
     next(proj_in)
-
-    shared_last = []
-    for index, (buf, total, got, ready, target) in enumerate(
-        (
-            (gate_buf, r_sgate, x_sgate, s_sgate, t_sgate),
-            (gate_buf, r_sup, x_sup, s_sup, t_sup),
-            (down_buf, r_sdown, x_sdown, s_sdown, t_sdown),
-        )
-    ):
-        shared_over[index].wait_recv()
-        adder.run(buf, [(total.at[0, dz], got.at[dz], ready.at[dz]) for dz in range(n_dp)])
-        for dz in (2, 3, 1, 0):
-            to = lax.bitwise_xor(z, jnp.int32(dz))
-            if dz:
-                item = wire.copy(ready.at[to], target.at[z], moved(dz, 0, y))
-                item.start()
-            else:
-                item = inside.start(ready.at[to], target.at[z])
-            shared_last.append(item)
-        if index == 0:
-            finish(proj_in)
-
-    def go_over_x(index):
-        total = (r_egate, r_eup, r_edown)[index]
-        got = (x_egate, x_eup, x_edown)[index]
-        item = wire.copy(total.at[1], got, place.over_x)
-        item.start()
-        return item
-
-    routed_over = [go_over_x(0)]
+    phases.go("gather_end")
+    finish(proj_in)
+
+    phases.go("attention")
+    routed_over.append(go_over_x(1, 1, 2))
     by_share = n_ctx * share
 
     def out_weight(target):
@@ -1364,12 +1462,14 @@
         d_qkv[:, cols + start : cols + start + head_dim] = turn(d_keys[...], every).astype(low)
         d_qkv[:, 2 * cols + start : 2 * cols + start + head_dim] = d_values[...].astype(low)
 
+    phases.go("attention_in_grad")
     wire.drain(list(y_swaps.values()) + z_swaps)
 
     def output(at):
         partial[at, :] = dot_f32(d_qkv[at, :], heads_weight[...], 1, 1).astype(low)
 
     by_rows(seq, block, output)
+    phases.go("sum_in_plane")
     reduce = plane_reduce(wire, place, partial, got_core, got_one, got_two)
     next(reduce)
 
@@ -1379,6 +1479,7 @@
 
     each(n_dp // 2, heads_weights)
     next(reduce)
+    next(out_chain)
     each(n_dp // 2, lambda index: heads_weights(index + n_dp // 2))
     heads_chain = chain_reduce(
         wire,
@@ -1386,8 +1487,9 @@
         [(lambda t: g_heads.at[rows_of(t, by_share), :], heads_below, heads_above)],
     )
     next(heads_chain)
+    phases.go("sum_in_plane_end")
     finish(reduce)
-    routed_over += [go_over_x(1), go_over_x(2)]
+    routed_over.append(go_over_x(2))
 
     def norm_one(at):
         d_attn_in = plane_sum(place, partial, got_one, got_two, at)
@@ -1401,6 +1503,7 @@
             + rstd * (d_norm - normed * jnp.mean(d_norm * normed, axis=1, keepdims=True))
         ).astype(low)
 
+    phases.go("norm_one")
     by_rows(rows, 16, norm_one)
 
     side_grad = side[0:16, :] + side[16:32, :] + side[32:48, :]
@@ -1428,23 +1531,11 @@
         item = wire.copy(stage.at[target], landed.at[mine], moved(dz, dc, y))
         item.start()
         small_items.append(item)
-    next(out_chain)
-    next(heads_chain)
-    for item in small_items:
-        item.wait_recv()
-    total = landed[0, 0:16, :]
-    for source in range(1, n_dp * n_ctx):
-        total = total + landed[source, 0:16, :]
-    over_y[0] = total
-    swap = wire.copy(over_y.at[0], over_y.at[1], place.over_y)
-    swap.start()
-    for context in range(n_ctx):
-        sums = landed[context, 16:24, :]
-        for source in range(1, n_dp):
-            sums = sums + landed[source * n_ctx + context, 16:24, :]
-        bias_grad[context] = sums
+    phases.go("chains")
     finish(out_chain)
+    phases.go("heads_chain")
     finish(heads_chain)
+    phases.go("last")
 
     out_block[...] = g_out[:, rows_of(z, by_share)]
     last = []
@@ -1464,11 +1555,474 @@
             else:
                 item = inside.start(src, dst)
             last.append(item)
+
+    phases.go("small")
+    for item in small_items:
+        item.wait_recv()
+    total = landed[0, 0:16, :]
+    for source in range(1, n_dp * n_ctx):
+        total = total + landed[source, 0:16, :]
+    over_y[0] = total
+    swap = wire.copy(over_y.at[0], over_y.at[1], place.over_y)
+    swap.start()
+    for context in range(n_ctx):
+        sums = landed[context, 16:24, :]
+        for source in range(1, n_dp):
+            sums = sums + landed[source * n_ctx + context, 16:24, :]
+        bias_grad[context] = sums
     swap.wait_recv()
     small_grad[...] = over_y[0] + over_y[1]
+    phases.go("wait_all")
     for item in last + shared_last + routed_over:
         item.wait_recv()
     wire.drain()
+    phases.go(None)
+
+
+def moe_forward(
+    n_dp, out_grad, moe_in, smalls, ids, s_gate_in, s_up_in, s_down_in, e_gate, e_up, e_down,
+    cols, pick, s_slope, s_silu, s_hidden, e_slope, e_silu, e_hidden, rows_in, part, e_out, shared,
+    dy_group,
+    x, wg, wu, wd, v_slope, v_silu, v_hidden, r_slope, r_silu, r_hidden, rows, out, sh,
+    s_gate, s_up, s_down, send, recv, local,
+):
+    place_here = Place(n_dp)
+    wire = Wire(send, recv)
+    z, c, y = place_here.z, place_here.c, place_here.y
+    f32, low = jnp.float32, jnp.bfloat16
+    inside = Local(local)
+    n_experts = ids.shape[0]
+    tok_rows = ids.shape[2]
+    phases = Phases()
+    phases.go("entry")
+    mine = z * 2 + y
+
+    def block_of(slot):
+        return dy_group.at[rows_of(slot * 2 + y, tok_rows), :]
+
+    y_recv = wire.take(n_dp)
+    y_send = wire.take_send(n_dp)
+
+    def over_y(slot):
+        ref = block_of(slot)
+        return wire.copy_to(ref, ref, place_here.over_y, y_recv + slot, y_send + slot)
+
+    loads = [
+        inside.start(src, dst)
+        for src, dst in ((moe_in, x), (s_gate_in, s_gate), (s_up_in, s_up), (s_down_in, s_down))
+    ]
+    near = [(lax.bitwise_xor(z, jnp.int32(dz)), c, y) for dz in range(1, n_dp)]
+    barrier(near + [place_here.over_y])
+    dy_chain = chain_gather(
+        wire,
+        place_here,
+        lambda slot: [block_of(slot)],
+        arrived=lambda slot: over_y(slot).start(),
+        own=[out_grad],
+    )
+    next(dy_chain)
+
+    def own_over_y():
+        return wire.copy_to(
+            out_grad, block_of(z), place_here.over_y, y_recv + z, y_send + z
+        )
+
+    own_over_y().start()
+    own = inside.start(out_grad, block_of(z))
+    loads += [inside.start(src, dst) for src, dst in ((e_gate, wg), (e_up, wu), (e_down, wd))]
+    hit = jnp.concatenate(
+        [jnp.any(ids[s] == mine, axis=0, keepdims=True).astype(f32) for s in range(n_experts)], axis=0
+    )
+    upto = (
+        lax.broadcasted_iota(jnp.int32, (tok_rows, tok_rows), 0)
+        <= lax.broadcasted_iota(jnp.int32, (tok_rows, tok_rows), 1)
+    ).astype(low)
+    place = dot_f32(hit.astype(low), upto, 1, 0) - 1.0
+    slots = lax.broadcasted_iota(jnp.int32, (CAP, tok_rows), 0).astype(f32)
+    for s in range(n_experts):
+        chosen = (hit[s : s + 1] > 0.5) & (place[s : s + 1] == slots)
+        pick[s] = jnp.where(chosen, 1.0, 0.0).astype(low)
+    phases.go("x_wait")
+    for item in loads[:4]:
+        item.wait()
+
+    def gated(g, u):
+        sigma = 1.0 / (1.0 + jnp.exp(-g))
+        silu = g * sigma
+        return u * (sigma * (1.0 + g * (1.0 - sigma))), silu, silu * u
+
+    def shared_tile(at):
+        here = x[at, :]
+        logits = dot_f32(here, smalls[...], 1, 1)
+        lane = lax.broadcasted_iota(jnp.int32, logits.shape, 1)
+        routed = lane < n_experts
+        top = jnp.max(jnp.where(routed, logits, -jnp.inf), axis=1, keepdims=True)
+        expo = jnp.where(routed, jnp.exp(jnp.where(routed, logits, top) - top), 0.0)
+        probs = expo / jnp.sum(expo, axis=1, keepdims=True)
+        mix = jnp.sum(jnp.where(lane == n_experts, logits, 0.0), axis=1, keepdims=True)
+        mix = 1.0 / (1.0 + jnp.exp(-mix))
+        gate = jnp.sum(jnp.where(lane == mine, probs, 0.0), axis=1, keepdims=True)
+        cols[at, 0:16] = jnp.where(
+            routed, probs, jnp.where(lane == n_experts, mix, jnp.where(lane == n_experts + 1, gate, 0.0))
+        )
+        slope, silu, hidden = gated(dot_f32(here, s_gate[...], 1, 0), dot_f32(here, s_up[...], 1, 0))
+        v_slope[at, :] = slope.astype(low)
+        v_silu[at, :] = silu.astype(low)
+        v_hidden[at, :] = hidden.astype(low)
+        sh[at, :] = dot_f32(v_hidden[at, :], s_down[...], 1, 0).astype(low)
+
+    phases.go("shared")
+    by_rows(x.shape[0], 512, shared_tile)
+    next(dy_chain)
+    stores = [
+        inside.start(src, dst)
+        for src, dst in ((v_slope, s_slope), (v_silu, s_silu), (v_hidden, s_hidden), (sh, shared))
+    ]
+
+    def gather(s, carry):
+        block = x[rows_of(s, tok_rows), :]
+        rows[rows_of(s, CAP), :] = dot_f32(pick[s], block, 1, 0).astype(low)
+        return carry
+
+    phases.go("gather")
+    lax.fori_loop(0, n_experts, gather, 0)
+    stores.append(inside.start(rows, rows_in))
+    phases.go("w_wait")
+    for item in loads[4:]:
+        item.wait()
+
+    def routed_tile(at):
+        here = rows[at, :]
+        slope, silu, hidden = gated(dot_f32(here, wg[...], 1, 0), dot_f32(here, wu[...], 1, 0))
+        r_slope[at, :] = slope.astype(low)
+        r_silu[at, :] = silu.astype(low)
+        r_hidden[at, :] = hidden.astype(low)
+        out[at, :] = dot_f32(r_hidden[at, :], wd[...], 1, 0).astype(low)
+
+    phases.go("routed")
+    routed_tile(pl.ds(0, 384))
+    phases.go("dy_two")
+    next(dy_chain)
+    phases.go("routed_end")
+    routed_tile(pl.ds(384, 384))
+    phases.go("dy_three")
+    next(dy_chain)
+    stores.append(inside.start(out, e_out))
+    stores += [
+        inside.start(src, dst)
+        for src, dst in ((r_slope, e_slope), (r_silu, e_silu), (r_hidden, e_hidden))
+    ]
+
+    def scatter(s, carry):
+        at = rows_of(s, tok_rows)
+        back = dot_f32(pick[s], out[rows_of(s, CAP), :], 0, 0)
+        mix = cols[at, n_experts : n_experts + 1]
+        gate = cols[at, n_experts + 1 : n_experts + 2]
+        x[at, :] = (gate * back + mix * sh[at, :].astype(f32)).astype(low)
+        return carry
+
+    phases.go("scatter")
+    lax.fori_loop(0, n_experts, scatter, 0)
+    phases.go("stores")
+    stores.append(inside.start(x, part))
+    for item in stores:
+        item.wait()
+    phases.go("over_y")
+    finish(dy_chain)
+    for slot in range(n_dp):
+        over_y(slot).wait_recv()
+        over_y(slot).wait_send()
+    own.wait()
+    phases.go(None)
+
+
+def shared_backward(
+    n_dp, dy_group, cols, pick, s_gate_in, s_up_in, s_down_in, s_slope_in, s_silu_in,
+    s_hidden, e_out, shared, moe_in,
+    grads_in, part, scalars, keep_gate, keep_up, keep_down, give_gate, give_up, give_down,
+    dy, out, sh, tok, d_sh, rows, grads, total, x, hidden,
+    g_gate, g_up, g_down, got_gate, got_up, got_down,
+    s_gate, s_up, s_down, s_slope, s_silu, sums, send, recv, local, slots,
+):
+    f32, low = jnp.float32, jnp.bfloat16
+    inside = Local(local)
+    wire = Wire(send, recv)
+    place = Place(n_dp)
+    n_experts = pick.shape[0]
+    tok_rows = pick.shape[2]
+    units = s_gate.shape[1]
+    lanes = grads.shape[1] // 2
+    share = g_gate.shape[1]
+    n_ctx = 4
+    core = lax.rem(place.c, 2)
+    chip = lax.div(place.c, 2)
+    phases = Phases()
+    phases.go("entry")
+
+    depth = dy.shape[0]
+
+    def fetch(index):
+        slot = index % depth
+        at = pl.ds(index * tok_rows, tok_rows)
+        items = [
+            pltpu.make_async_copy(src, dst.at[slot], slots.at[3 * slot + k])
+            for k, (src, dst) in enumerate(
+                (
+                    (dy_group.at[at, :], dy),
+                    (e_out.at[pl.ds(index * CAP, CAP), :], out),
+                    (shared.at[at, :], sh),
+                )
+            )
+        ]
+        for item in items:
+            item.start()
+        return items
+
+    coming = [fetch(index) for index in range(depth - 1)]
+    loads = [
+        inside.start(src, dst)
+        for src, dst in (
+            (s_down_in, s_down), (s_slope_in, s_slope), (s_silu_in, s_silu),
+            (s_gate_in, s_gate), (s_up_in, s_up), (moe_in, x), (s_hidden, hidden),
+        )
+    ]
+    barrier([place.core])
+    grads[...] = jnp.zeros_like(grads)
+    sums[...] = jnp.zeros_like(sums)
+    for index in range(n_experts):
+        slot = index % depth
+        if index + depth - 1 < n_experts:
+            coming.append(fetch(index + depth - 1))
+        for item in coming[index]:
+            item.wait()
+        tok[...] = dot_f32(pick[index], out[slot], 0, 0)
+
+        def chunk(at):
+            here = pl.ds(pl.multiple_of(index * tok_rows + at.start, at.size), at.size)
+            grad = dy[slot, at, :].astype(f32)
+            mix = cols[here, n_experts : n_experts + 1]
+            gate = cols[here, n_experts + 1 : n_experts + 2]
+            d_sh[here, :] = (mix * grad).astype(low)
+            sums[at, 0:1] = jnp.sum(tok[at, :] * grad, axis=1, keepdims=True)
+            sums[at, 1:2] = jnp.sum(sh[slot, at, :].astype(f32) * grad, axis=1, keepdims=True)
+            dy[slot, at, :] = (gate * grad).astype(low)
+
+        by_rows(tok_rows, 32, chunk)
+        scalars[index] = jnp.transpose(sums[...])[0:8, :]
+        rows[pl.ds(index * CAP, CAP), :] = dot_f32(pick[index], dy[slot], 1, 0).astype(low)
+    stores = [inside.start(rows, grads_in)]
+
+    def shared_tile(at):
+        d_hidden = dot_f32(d_sh[at, :], s_down[...], 1, 1)
+        d_gate = (d_hidden * s_slope[at, :].astype(f32)).astype(low)
+        d_up = (d_hidden * s_silu[at, :].astype(f32)).astype(low)
+        grads[at, 0:units] = d_gate
+        grads[at, lanes : lanes + units] = d_up
+        total[at, :] = (dot_f32(d_gate, s_gate[...], 1, 1) + dot_f32(d_up, s_up[...], 1, 1)).astype(low)
+
+    for item in loads[:5]:
+        item.wait()
+    phases.go("shared")
+    by_rows(d_sh.shape[0], 512, shared_tile)
+    stores.append(inside.start(total, part))
+    for item in loads[5:]:
+        item.wait()
+    phases.go("in_grads")
+
+    def block_index(dx, dz, sibling):
+        side = lax.bitwise_xor(chip, jnp.int32(dx)) * 2
+        return dz * n_ctx + side + (1 - core if sibling else core)
+
+    sent = {}
+
+    def to_sibling(dz, mats):
+        for dx in (1, 0):
+            for grad, got in mats:
+                item = wire.copy(grad.at[block_index(dx, dz, True)], got.at[dx, dz], place.core)
+                item.start()
+                sent.setdefault(dz, []).append(item)
+
+    step = n_ctx * share
+    for dz in range(n_dp):
+        product = dot_f32(x[:, dz * step : (dz + 1) * step], grads[...], 0, 0)
+        for k in range(n_ctx):
+            here = slice(k * share, (k + 1) * share)
+            g_gate[dz * n_ctx + k] = product[here, 0:units].astype(low)
+            g_up[dz * n_ctx + k] = product[here, lanes : lanes + units].astype(low)
+        to_sibling(dz, ((g_gate, got_gate), (g_up, got_up)))
+    phases.go("down_grads")
+    down = {}
+    for dz in range(n_dp):
+        product = dot_f32(hidden[...], d_sh[:, dz * step : (dz + 1) * step], 0, 0)
+        for k in range(n_ctx):
+            g_down[dz * n_ctx + k] = product[:, k * share : (k + 1) * share].astype(low)
+        for dx in (1, 0):
+            item = wire.copy(g_down.at[block_index(dx, dz, True)], got_down.at[dx, dz], place.core)
+            item.start()
+            down.setdefault(dz, []).append(item)
+    phases.go("sums")
+
+    def collect(dx, dz, grad, got, out_ref):
+        mine = block_index(dx, dz, False)
+        add_block(grad.at[mine], got.at[dx, dz])
+        size = grad.shape[1]
+        stores.append(inside.start(grad.at[mine], out_ref.at[pl.ds(dz * size, size), :]))
+
+    for dz in range(n_dp):
+        for item in sent[dz]:
+            item.wait_recv()
+        for dx, outs in ((1, (give_gate, give_up)), (0, (keep_gate, keep_up))):
+            for grad, got, out_ref in zip((g_gate, g_up), (got_gate, got_up), outs):
+                collect(dx, dz, grad, got, out_ref)
+    for dz in range(n_dp):
+        for item in down[dz]:
+            item.wait_recv()
+        for dx, out_ref in ((1, give_down), (0, keep_down)):
+            collect(dx, dz, g_down, got_down, out_ref)
+    phases.go("stores")
+    for item in stores:
+        item.wait()
+    wire.drain()
+    phases.go(None)
+
+
+def routed_backward(
+    grads_in, rows_in, e_gate, e_up, e_down, slope_in, silu_in, hidden_in, pick, shared_part,
+    part, o_gate, o_up, o_down,
+    wg, wu, wd, grads, rows, slope, silu, hidden, d_hid, d_in, total, buf_gate, buf_up, buf_down,
+    local, stores,
+):
+    f32, low = jnp.float32, jnp.bfloat16
+    inside = Local(local)
+    n_experts = pick.shape[0]
+    tok_rows = pick.shape[2]
+    units = wg.shape[1]
+    phases = Phases()
+    phases.go("entry")
+    loads = [
+        inside.start(src, dst)
+        for src, dst in (
+            (grads_in, grads), (e_down, wd), (slope_in, slope), (silu_in, silu),
+            (e_gate, wg), (e_up, wu), (shared_part, total), (rows_in, rows), (hidden_in, hidden),
+        )
+    ]
+    for item in loads[:4]:
+        item.wait()
+    phases.go("routed")
+    half = grads.shape[0] // 2
+
+    def routed_tile(at, wait):
+        d_hidden = dot_f32(grads[at, :], wd[...], 1, 1)
+        d_gate = (d_hidden * slope[at, :].astype(f32)).astype(low)
+        d_up = (d_hidden * silu[at, :].astype(f32)).astype(low)
+        d_hid[at, 0:units] = d_gate
+        d_hid[at, units : 2 * units] = d_up
+        for item in wait:
+            item.wait()
+        d_in[at, :] = (dot_f32(d_gate, wg[...], 1, 1) + dot_f32(d_up, wu[...], 1, 1)).astype(low)
+
+    routed_tile(pl.ds(0, half), loads[4:6])
+    routed_tile(pl.ds(half, half), [])
+    for item in loads[6:]:
+        item.wait()
+    phases.go("to_tokens")
+
+    def to_tokens(s, carry):
+        at = rows_of(s, tok_rows)
+        back = dot_f32(pick[s], d_in[rows_of(s, CAP), :], 0, 0)
+        total[at, :] = (back + total[at, :].astype(f32)).astype(low)
+        return carry
+
+    lax.fori_loop(0, n_experts, to_tokens, 0)
+    done = inside.start(total, part)
+    phases.go("in_grads")
+
+    def products(first, steps, size, outs, product):
+        def copy(index, k):
+            slot = lax.rem(index, 2)
+            buf, target = outs[k]
+            return pltpu.make_async_copy(buf.at[slot], target(index), stores.at[slot, first + k])
+
+        def one(index, carry):
+            for k in range(len(outs)):
+
+                @pl.when(index >= 2)
+                def _():
+                    copy(index - 2, k).wait()
+
+            value = product(rows_of(index, size))
+            for k, (buf, _) in enumerate(outs):
+                width = buf.shape[2]
+                buf[lax.rem(index, 2)] = value[:, k * width : (k + 1) * width].astype(low)
+                copy(index, k).start()
+            return carry
+
+        lax.fori_loop(0, steps, one, 0)
+        for k in range(len(outs)):
+            for last in (steps - 2, steps - 1):
+                copy(jnp.int32(last), k).wait()
+
+    tall = buf_gate.shape[1]
+    products(
+        0,
+        rows.shape[1] // tall,
+        tall,
+        [
+            (buf_gate, lambda index: o_gate.at[rows_of(index, tall), :]),
+            (buf_up, lambda index: o_up.at[rows_of(index, tall), :]),
+        ],
+        lambda at: dot_f32(rows[:, at], d_hid[...], 0, 0),
+    )
+    phases.go("down_grads")
+    wide = buf_down.shape[2]
+    products(
+        2,
+        grads.shape[1] // wide,
+        wide,
+        [(buf_down, lambda index: o_down.at[:, rows_of(index, wide)])],
+        lambda at: dot_f32(hidden[...], grads[:, at], 0, 0),
+    )
+    phases.go("stores")
+    done.wait()
+    phases.go(None)
+
+
+def finish_grads(n_ctx, *refs):
+    (
+        t_gate, t_up, t_down, own_gate, own_up, own_down, far_gate, far_up, far_down, heads, out_weight,
+        o_sgate, o_sup, o_sdown, o_egate, o_eup, o_edown, o_query, o_key, o_value, o_out,
+    ) = refs
+    f32 = jnp.float32
+    n_dp, share, units = t_gate.shape
+    for source, target in ((t_gate, o_sgate), (t_up, o_sup)):
+        target[...] = jnp.concatenate([source[k].astype(f32) for k in range(n_dp)], axis=1)
+    for k in range(n_dp):
+        o_sdown[k * units : (k + 1) * units, :] = t_down[k].astype(f32)
+    for own, far, target in (
+        (own_gate, far_gate, o_egate), (own_up, far_up, o_eup), (own_down, far_down, o_edown),
+    ):
+
+        def add(at):
+            target[at, :] = own[at, :].astype(f32) + far[at, :].astype(f32)
+
+        by_rows(target.shape[0], 32, add)
+    cols = heads.shape[2] // 3
+    for k, target in enumerate((o_query, o_key, o_value)):
+        for c in range(n_ctx):
+            target[:, c * cols : (c + 1) * cols] = heads[c, :, k * cols : (k + 1) * cols].astype(f32)
+    for c in range(n_ctx):
+        o_out[c * cols : (c + 1) * cols, :] = out_weight[c].astype(f32)
+
+
+def whole_tables(seq_len, head_dim):
+    half = head_dim // 2
+    freq = np.float32(THETA) ** (-(2.0 * np.arange(half, dtype=np.float32)) / np.float32(head_dim))
+    angle = np.arange(seq_len, dtype=np.float32)[:, None] * freq.astype(np.float32)[None, :]
+    cosine, sine = np.cos(angle), np.sin(angle)
+    return (
+        jnp.asarray(np.concatenate([cosine, cosine], axis=1), jnp.float32),
+        jnp.asarray(np.concatenate([-sine, sine], axis=1), jnp.float32),
+    )
 
 
 def tokens_plan(
@@ -1507,9 +2061,6 @@
     n_group = n_dp * n_half
     my_expert = dp * n_half + half
 
-    def group_in(rows):
-        return lax.all_gather(rows, (DP, EXPERT), axis=0, tiled=True)
-
     def group_out(rows):
         return lax.psum_scatter(rows, (DP, EXPERT), scatter_dimension=0, tiled=True)
 
@@ -1525,10 +2076,7 @@
 
     biases = jnp.stack([query_bias_heads, bias_key, bias_value]).astype(f32)
     biases = lax.dynamic_slice_in_dim(biases, ctx * heads, heads, 1).reshape(3, cols)
-    cosine, sine = rope_tables(jnp.arange(seq_len), head_dim)
-    cosine = jnp.concatenate([cosine[:, 0], cosine[:, 0]], axis=1)
-    sine = jnp.concatenate([-sine[:, 0], sine[:, 0]], axis=1)
-    dy_group = group_in(out_grad)
+    cosine, sine = whole_tables(seq_len, head_dim)
     vmem = pl.BlockSpec(memory_space=pltpu.VMEM)
     anywhere = pl.BlockSpec(memory_space=pl.ANY)
     share = w_query.shape[0]
@@ -1556,16 +2104,25 @@
             like((n_group, 8, tok_rows), jnp.int32),
         ],
         in_specs=[anywhere] * 10 + [vmem] * 3,
-        out_specs=[vmem] * 7 + [anywhere] + [vmem] * 2 + [anywhere] * 3 + [vmem, anywhere],
+        out_specs=[anywhere] * 13 + [vmem, anywhere],
         scratch_shapes=[
             pltpu.VMEM((seq_len, width), low),
             pltpu.VMEM((seq_len, width), low),
             pltpu.VMEM((4, tok_rows, width), low),
             pltpu.VMEM((4, tok_rows, half_width), low),
             pltpu.VMEM((2, tok_rows, half_width), low),
+            pltpu.VMEM((seq_len, width), low),
+            pltpu.VMEM((seq_len, cols), low),
+            pltpu.VMEM((seq_len, cols), low),
+            pltpu.VMEM((seq_len, cols), low),
+            pltpu.VMEM((seq_len, cols), low),
+            pltpu.VMEM((seq_len, cols), f32),
+            pltpu.VMEM((tok_rows, width), f32),
+            pltpu.VMEM((width, 3 * cols), low),
+            pltpu.VMEM((cols, width), low),
             pltpu.SemaphoreType.DMA((144,)),
             pltpu.SemaphoreType.DMA((144,)),
-            pltpu.SemaphoreType.DMA((16,)),
+            pltpu.SemaphoreType.DMA((32,)),
         ],
         name="forward",
         compiler_params=pltpu.CompilerParams(
@@ -1576,81 +2133,154 @@
         by_dp(shared_in_gate), by_dp(shared_in_up), shared_down, biases, cosine, sine,
     )
     sg, su = sg.reshape(width, hidden_units), su.reshape(width, hidden_units)
-    gain_one = small[n_experts + 1].astype(f32)
-    gain_two = small[n_experts + 2].astype(f32)
-    x_own = tokens.astype(f32)
-    dy_own = out_grad.astype(f32)
-    rstd_two = lax.rsqrt(jnp.mean(hidden_own * hidden_own, axis=1, keepdims=True) + EPS)
-    normed_two = hidden_own * rstd_two
-    moe_own = (normed_two * gain_two).astype(low)
-
-    logits = mat_right(moe_in, small)
-    router_probs = jax.nn.softmax(logits[:, :n_experts], axis=1)
-    mix = jax.nn.sigmoid(logits[:, n_experts])
-    hit = jnp.any(ids_group == my_expert, axis=1)
-    gate = jnp.sum(
-        jnp.where(jnp.arange(n_experts)[None, :] == my_expert, router_probs, 0.0), axis=1
-    )
-    place = jnp.cumsum(hit.astype(jnp.int32), axis=1) - 1
-    chosen = (hit[:, None, :] & (place[:, None, :] == jnp.arange(CAP)[None, :, None]))
-    pick = chosen.astype(low)
-    gate_rows = jnp.sum(jnp.where(chosen, gate.reshape(n_group, 1, tok_rows), 0.0), axis=2)
-
-    def to_rows(group):
-        return jnp.einsum(
-            "sct,std->scd", pick, group.reshape(n_group, tok_rows, -1), preferred_element_type=f32
-        ).astype(low).reshape(n_group * CAP, -1)
-
-    def to_tokens(rows):
-        return jnp.einsum(
-            "sct,scd->std", pick, rows.reshape(n_group, CAP, -1), preferred_element_type=f32
-        ).reshape(n_group * tok_rows, -1)
-
-    rows_in = to_rows(moe_in)
-    dy_rows = to_rows(dy_group)
-    grads_in = (gate_rows.reshape(-1, 1) * dy_rows.astype(f32)).astype(low)
+    units = expert_gate.shape[2]
+    s_weights = [
+        pltpu.VMEM((width, hidden_units), low),
+        pltpu.VMEM((width, hidden_units), low),
+        pltpu.VMEM((hidden_units, width), low),
+    ]
     gate_weight, up_weight, down_weight = expert_gate[0], expert_up[0], expert_down[0]
-    e_gate = jnp.dot(rows_in, gate_weight, preferred_element_type=f32)
-    e_up = jnp.dot(rows_in, up_weight, preferred_element_type=f32)
-    e_silu = jax.nn.silu(e_gate)
-    e_hidden = (e_silu * e_up).astype(low)
-    e_out = jnp.dot(e_hidden, down_weight, preferred_element_type=f32).astype(low)
-    d_hidden = mat_right(grads_in, down_weight)
-    d_gate = (d_hidden * e_up * silu_slope(e_gate)).astype(low)
-    d_up = (d_hidden * e_silu).astype(low)
-    d_in = (mat_right(d_gate, gate_weight) + mat_right(d_up, up_weight)).astype(low)
-
-    s_gate = jnp.dot(moe_in, sg, preferred_element_type=f32)
-    s_up = jnp.dot(moe_in, su, preferred_element_type=f32)
-    s_silu = jax.nn.silu(s_gate)
-    s_hidden = (s_silu * s_up).astype(low)
-    shared = jnp.dot(s_hidden, sd, preferred_element_type=f32)
-    dy_float = dy_group.astype(f32)
-    d_shared = (mix[:, None] * dy_float).astype(low)
-    d_shidden = mat_right(d_shared, sd)
-    d_sgate = (d_shidden * s_up * silu_slope(s_gate)).astype(low)
-    d_sup = (d_shidden * s_silu).astype(low)
-
-    moe_part = (gate[:, None] * to_tokens(e_out) + mix[:, None] * shared).astype(low)
-    d_in_part = (to_tokens(d_in) + mat_right(d_sgate, sg) + mat_right(d_sup, su)).astype(low)
-    d_gate_rows = jnp.sum(e_out.astype(f32) * dy_rows.astype(f32), axis=1).reshape(n_group, CAP)
-    d_gate_tok = jnp.sum(jnp.where(chosen, d_gate_rows[:, :, None], 0.0), axis=1).reshape(-1)
-    shared_dot = jnp.sum(shared * dy_float, axis=1)
-    scalars = jnp.stack([d_gate_tok, shared_dot]).reshape(2, n_group, tok_rows).transpose(1, 0, 2)
-    scalars = jnp.pad(scalars, ((0, 0), (0, 6), (0, 0)))
+    slots = n_group * CAP
+    group_rows = n_group * tok_rows
+    (
+        token_cols, pick, s_slope, s_silu, s_hidden, e_slope, e_silu, e_hidden, rows_in,
+        moe_part, e_out, shared, dy_group,
+    ) = pl.pallas_call(
+        lambda *refs: moe_forward(n_dp, *refs),
+        out_shape=[
+            like((group_rows, 128), f32),
+            like((n_group, CAP, tok_rows), low),
+        ]
+        + [like((group_rows, hidden_units), low)] * 3
+        + [like((slots, units), low)] * 3
+        + [
+            like((slots, width), low),
+            like((group_rows, width), low),
+            like((slots, width), low),
+            like((group_rows, width), low),
+            like((group_rows, width), low),
+        ],
+        in_specs=[anywhere] * 2 + [vmem] * 2 + [anywhere] * 6,
+        out_specs=[vmem] * 2 + [anywhere] * 11,
+        scratch_shapes=[
+            pltpu.VMEM((group_rows, width), low),
+            pltpu.VMEM((width, units), low),
+            pltpu.VMEM((width, units), low),
+            pltpu.VMEM((units, width), low),
+        ]
+        + [pltpu.VMEM((group_rows, hidden_units), low)] * 3
+        + [pltpu.VMEM((slots, units), low)] * 3
+        + [pltpu.VMEM((slots, width), low)] * 2
+        + [pltpu.VMEM((group_rows, width), low)]
+        + s_weights
+        + [pltpu.SemaphoreType.DMA((16,))] * 2
+        + [pltpu.SemaphoreType.DMA((24,))],
+        name="moe_forward",
+        compiler_params=pltpu.CompilerParams(
+            collective_id=3, has_side_effects=True, vmem_limit_bytes=63 * 2**20
+        ),
+        cost_estimate=pl.CostEstimate(
+            flops=6 * width * (group_rows * hidden_units + slots * units),
+            bytes_accessed=2 * (9 * width * units + 4 * group_rows * width),
+            transcendentals=0,
+        ),
+    )(out_grad, moe_in, small, ids_group, sg, su, sd, gate_weight, up_weight, down_weight)
+    lanes = -(-hidden_units // 128) * 128
+    block_kinds = [(n_dp, share, hidden_units)] * 2 + [(n_dp, hidden_units, share)]
+    shared_all = [(n_dp * n_ctx, share, hidden_units)] * 2 + [(n_dp * n_ctx, hidden_units, share)]
+    results = pl.pallas_call(
+        lambda *refs: shared_backward(n_dp, *refs),
+        out_shape=[
+            like((slots, width), low),
+            like((group_rows, width), low),
+            like((n_group, 8, tok_rows), f32),
+        ]
+        + [like((kind[0] * kind[1], kind[2]), low) for kind in block_kinds] * 2,
+        in_specs=[anywhere] + [vmem] * 2 + [anywhere] * 9,
+        out_specs=[anywhere] * 2 + [vmem] + [anywhere] * 6,
+        scratch_shapes=[
+            pltpu.VMEM((4, tok_rows, width), low),
+            pltpu.VMEM((4, CAP, width), low),
+            pltpu.VMEM((4, tok_rows, width), low),
+            pltpu.VMEM((tok_rows, width), f32),
+            pltpu.VMEM((group_rows, width), low),
+            pltpu.VMEM((slots, width), low),
+            pltpu.VMEM((group_rows, 2 * lanes), low),
+            pltpu.VMEM((group_rows, width), low),
+            pltpu.VMEM((group_rows, width), low),
+            pltpu.VMEM((group_rows, hidden_units), low),
+        ]
+        + [pltpu.VMEM(kind, low) for kind in shared_all]
+        + [pltpu.VMEM((2, *kind), low) for kind in block_kinds]
+        + s_weights
+        + [pltpu.VMEM((group_rows, hidden_units), low)] * 2
+        + [pltpu.VMEM((tok_rows, 128), f32)]
+        + [pltpu.SemaphoreType.DMA((32,))] * 2
+        + [pltpu.SemaphoreType.DMA((48,)), pltpu.SemaphoreType.DMA((12,))],
+        name="shared_backward",
+        compiler_params=pltpu.CompilerParams(
+            collective_id=4, has_side_effects=True, vmem_limit_bytes=63 * 2**20
+        ),
+        cost_estimate=pl.CostEstimate(
+            flops=12 * width * group_rows * hidden_units,
+            bytes_accessed=2 * (9 * width * hidden_units + 8 * group_rows * width),
+            transcendentals=0,
+        ),
+    )(
+        dy_group, token_cols, pick, sg, su, sd, s_slope, s_silu, s_hidden, e_out, shared, moe_in,
+    )
+    grads_in, shared_part, scalars = results[:3]
+    keep = results[3:6]
+    over_x = [(index, index ^ 2) for index in range(n_ctx)]
+    got = [lax.ppermute(item, CONTEXT, over_x) for item in results[6:9]]
+    quarter = width // n_ctx
+    d_in_part, g_egate, g_eup, g_edown = pl.pallas_call(
+        routed_backward,
+        out_shape=[
+            like((group_rows, width), low),
+            like((width, units), low),
+            like((width, units), low),
+            like((units, width), low),
+        ],
+        in_specs=[anywhere] * 8 + [vmem] + [anywhere],
+        out_specs=[anywhere] * 4,
+        scratch_shapes=[
+            pltpu.VMEM((width, units), low),
+            pltpu.VMEM((width, units), low),
+            pltpu.VMEM((units, width), low),
+            pltpu.VMEM((slots, width), low),
+            pltpu.VMEM((slots, width), low),
+            pltpu.VMEM((slots, units), low),
+            pltpu.VMEM((slots, units), low),
+            pltpu.VMEM((slots, units), low),
+            pltpu.VMEM((slots, 2 * units), low),
+            pltpu.VMEM((slots, width), low),
+            pltpu.VMEM((group_rows, width), low),
+            pltpu.VMEM((2, quarter // 2, units), low),
+            pltpu.VMEM((2, quarter // 2, units), low),
+            pltpu.VMEM((2, units, quarter), low),
+            pltpu.SemaphoreType.DMA((16,)),
+            pltpu.SemaphoreType.DMA((2, 3)),
+        ],
+        name="routed_backward",
+        compiler_params=pltpu.CompilerParams(vmem_limit_bytes=63 * 2**20),
+        cost_estimate=pl.CostEstimate(
+            flops=12 * width * slots * units,
+            bytes_accessed=2 * (12 * width * units + 4 * group_rows * width),
+            transcendentals=0,
+        ),
+    )(
+        grads_in, rows_in, gate_weight, up_weight, down_weight, e_slope, e_silu, e_hidden, pick,
+        shared_part,
+    )
+    g_egate = g_egate.reshape(n_ctx, quarter, units)
+    g_eup = g_eup.reshape(n_ctx, quarter, units)
     moe_sum = group_out(moe_part).astype(f32)
     mixed = (hidden_own + moe_sum).astype(low)
 
-    own = my_expert * tok_rows
-    probs_own = lax.dynamic_slice_in_dim(router_probs, own, tok_rows, 0).T
-    mix_own = lax.dynamic_slice_in_dim(mix, own, tok_rows, 0)[None]
-    g_sgate = left_operand(moe_in, d_sgate).astype(low).reshape(-1, share, hidden_units)
-    g_sup = left_operand(moe_in, d_sup).astype(low).reshape(-1, share, hidden_units)
-    g_sdown = left_operand(s_hidden, d_shared).astype(low)
-    g_egate = left_operand(rows_in, d_gate).astype(low).reshape(n_ctx, width // n_ctx, -1)
-    g_eup = left_operand(rows_in, d_up).astype(low).reshape(n_ctx, width // n_ctx, -1)
-    g_edown = left_operand(e_hidden, grads_in).astype(low)
-    units = g_edown.shape[0]
+    own_cols = lax.dynamic_slice_in_dim(token_cols, my_expert * tok_rows, tok_rows, 0)
+    probs_own = own_cols[:, :n_experts].T
+    mix_own = own_cols[:, n_experts][None]
     by_share = n_ctx * share
     e_wide = (width // n_ctx, units)
     e_tall = (units, width // n_ctx)
@@ -1670,13 +2300,10 @@
         + [like((n_dp, *kind), low) for kind in s_kinds]
         + [like((2, *kind), low) for kind in e_kinds]
         + [like(kind, low) for kind in e_kinds]
-        + [like((2, n_dp, *kind), low) for kind in s_kinds]
-        + [like((2, n_dp, *kind), low) for kind in s_kinds]
-        + [like((n_dp, *kind), low) for kind in s_kinds]
         + [like((n_dp, *kind), low) for kind in s_kinds]
         + [like((2, *kind), low) for kind in e_kinds],
-        in_specs=[anywhere] * 8 + [vmem] * 16,
-        out_specs=[vmem] + [anywhere] * 2 + [vmem] * 2 + [anywhere] * 24,
+        in_specs=[anywhere] * 14 + [vmem] * 3 + [anywhere] * 10,
+        out_specs=[vmem] + [anywhere] * 2 + [vmem] * 2 + [anywhere] * 15,
         scratch_shapes=[
             pltpu.VMEM((seq_len, width), low),
             pltpu.VMEM((n_dp, tok_rows, width), low),
@@ -1709,9 +2336,22 @@
             pltpu.VMEM((3, 2, units // 4, width // n_ctx), low),
             pltpu.VMEM((3, 2, *s_wide), low),
             pltpu.VMEM((3, 2, *s_tall), low),
+            pltpu.VMEM((tok_rows, width), f32),
+            pltpu.VMEM((tok_rows, width), low),
+            pltpu.VMEM((tok_rows, width), low),
+            pltpu.VMEM((width, 3 * cols), low),
+            pltpu.VMEM((cols, width), low),
+            pltpu.VMEM((seq_len, cols), low),
+            pltpu.VMEM((seq_len, cols), low),
+            pltpu.VMEM((seq_len, cols), low),
+            pltpu.VMEM((seq_len, cols), low),
+            pltpu.VMEM((seq_len, cols), f32),
+            pltpu.VMEM((seq_len, width), low),
+            pltpu.VMEM((seq_len, head_dim), f32),
+            pltpu.VMEM((seq_len, head_dim), f32),
             pltpu.SemaphoreType.DMA((160,)),
             pltpu.SemaphoreType.DMA((160,)),
-            pltpu.SemaphoreType.DMA((16,)),
+            pltpu.SemaphoreType.DMA((32,)),
             pltpu.SemaphoreType.DMA((6,)),
         ],
         name="backward",
@@ -1719,22 +2359,53 @@
             collective_id=2, has_side_effects=True, vmem_limit_bytes=63 * 2**20
         ),
     )(
-        d_in_part, scalars, g_sgate, g_sup, g_sdown, g_egate, g_eup, g_edown,
+        d_in_part, scalars, *keep, *got, g_egate, g_eup, g_edown,
         hidden_own, out_grad, tokens, small, probs_own, mix_own,
         heads_weight, wo, query, keys, values, attn, lse, attn_in, cosine, sine,
     )
     input_grad, heads_grad, out_weight_grad, small_grad, bias_grad = results[:5]
     s_done, e_own, e_other = results[5:8], results[8:11], results[11:14]
-    grad_sgate, grad_sup = (
-        grad.transpose(1, 0, 2).reshape(share, -1).astype(f32) for grad in s_done[:2]
-    )
-    grad_sdown = s_done[2].reshape(-1, share).astype(f32)
-    routed = [
-        (mine[0].astype(f32) + other.astype(f32))[None] for mine, other in zip(e_own, e_other)
-    ]
-    heads_grad = heads_grad.reshape(n_ctx, share, 3, cols).transpose(2, 1, 0, 3)
-    heads_grad = heads_grad.reshape(3, share, -1).astype(f32)
-    grad_out = out_weight_grad.reshape(-1, share).astype(f32)
+    finished = pl.pallas_call(
+        lambda *refs: finish_grads(n_ctx, *refs),
+        out_shape=[
+            like((share, n_dp * hidden_units), f32),
+            like((share, n_dp * hidden_units), f32),
+            like((n_dp * hidden_units, share), f32),
+            like(e_wide, f32),
+            like(e_wide, f32),
+            like(e_tall, f32),
+            like((share, n_ctx * cols), f32),
+            like((share, n_ctx * cols), f32),
+            like((share, n_ctx * cols), f32),
+            like((n_ctx * cols, share), f32),
+        ],
+        grid=(1,),
+        in_specs=[pl.BlockSpec((n_dp, *kind), lambda i: (0, 0, 0)) for kind in s_kinds]
+        + [pl.BlockSpec((None, *kind), lambda i: (0, 0, 0)) for kind in e_kinds]
+        + [pl.BlockSpec(kind, lambda i: (0, 0)) for kind in e_kinds]
+        + [
+            pl.BlockSpec(heads_grad.shape, lambda i: (0, 0, 0)),
+            pl.BlockSpec(out_weight_grad.shape, lambda i: (0, 0, 0)),
+        ],
+        out_specs=[
+            pl.BlockSpec((share, n_dp * hidden_units), lambda i: (0, 0)),
+            pl.BlockSpec((share, n_dp * hidden_units), lambda i: (0, 0)),
+            pl.BlockSpec((n_dp * hidden_units, share), lambda i: (0, 0)),
+            pl.BlockSpec(e_wide, lambda i: (0, 0)),
+            pl.BlockSpec(e_wide, lambda i: (0, 0)),
+            pl.BlockSpec(e_tall, lambda i: (0, 0)),
+            pl.BlockSpec((share, n_ctx * cols), lambda i: (0, 0)),
+            pl.BlockSpec((share, n_ctx * cols), lambda i: (0, 0)),
+            pl.BlockSpec((share, n_ctx * cols), lambda i: (0, 0)),
+            pl.BlockSpec((n_ctx * cols, share), lambda i: (0, 0)),
+        ],
+        name="finish_grads",
+        compiler_params=pltpu.CompilerParams(vmem_limit_bytes=63 * 2**20),
+    )(*s_done, *e_own, *e_other, heads_grad, out_weight_grad)
+    grad_sgate, grad_sup, grad_sdown = finished[:3]
+    routed = [item[None] for item in finished[3:6]]
+    heads_grad = finished[6:9]
+    grad_out = finished[9]
     bias_sum = bias_grad[:, : 3 * heads].reshape(n_ctx, 3, heads, head_dim)
     bias_sum = bias_sum.transpose(1, 0, 2, 3).reshape(3, half_heads, head_dim)
     bias_share = head_dim // (n_dp * n_ctx)

time: 734 us -> 578 us (0.79)
  matrix products: 144 us -> 0 us
  other arithmetic: 20.5 us -> 2.87 us
  Pallas kernels: 519 us -> 531 us
  local copies, waits for them, and re-layouts: 29.5 us -> 19.3 us
    pallas_call x0 -> x4, Pallas kernels: none -> 157 us  [the longest x1 55.4 us: tokens_plan(): pl.pallas_call(lambda *refs: moe_forward(n_dp, *refs), out_shape=[like((g...]
    dot_general x23 -> x0, matrix products: 144 us -> none  [the longest x7 51.2 us: mat_right(): return jnp.dot(left, right.T, preferred_element_type=jnp.float32)]
    pallas_call x1, Pallas kernels: 283 us -> 195 us  [tokens_plan(): pl.pallas_call(lambda *refs: backward_kernel(n_blocks, n_dp, *refs), out_...]
    pallas_call x1, Pallas kernels: 236 us -> 179 us  [tokens_plan(): pl.pallas_call(lambda *refs: forward_kernel(n_blocks, n_dp, *refs), out_s...]
    convert_element_type x5 -> x0, local copies, waits for them, and re-layouts: 10.1 us -> none  [the longest x1 4.79 us: tokens_plan(): left_operand(moe_in, d_sgate).astype(low).reshape(-1, share, hidden_units)]
    unnamed x119 -> x26, local copies, waits for them, and re-layouts: 12.7 us -> 3.31 us
    broadcast_in_dim x3 -> x0, other arithmetic: 7.7 us -> none  [tokens_plan(): (mine[0].astype(f32) + other.astype(f32))[None]]
  transfers between devices with their start and end apart: 2 -> 4, of which waited for: 0 -> 0; matrix products, arithmetic and copies ran while one was open for 22% -> 2% of each run, Pallas kernels for 71% -> 52%
where the time goes in v3:
time: 578 us; the launch traced here: 569 us
  Pallas kernels  531 us (92%)
  local copies, waits for them, and re-layouts  19.3 us (3%)
  between operations  14.5 us (3%)
    pallas_call x1, Pallas kernels, tokens_plan(): pl.pallas_call(lambda *refs: backward_kernel(n_blocks, n_dp, *refs), out_...  195 us
    pallas_call x1, Pallas kernels, tokens_plan(): pl.pallas_call(lambda *refs: forward_kernel(n_blocks, n_dp, *refs), out_s...  179 us
    pallas_call x1, Pallas kernels, tokens_plan(): pl.pallas_call(lambda *refs: moe_forward(n_dp, *refs), out_shape=[like((g...  55.4 us
    pallas_call x1, Pallas kernels, tokens_plan(): pl.pallas_call(lambda *refs: shared_backward(n_dp, *refs), out_shape=[lik...  46.7 us
    pallas_call x1, Pallas kernels, tokens_plan(): pl.pallas_call(routed_backward, out_shape=[like((group_rows, width), low)...  43 us
  transfers between devices with their start and end apart: 4, of which 0 were waited for; matrix products, arithmetic and copies ran while one was open for 2% of the time, Pallas kernels for 52%

profile of v3, /device:TPU:9, one launch (start us, length us, event | category | flops | bytes accessed | tf_op | source)
XLA Modules:
  0.0 569.5 jit_solution(43314118773135245)
XLA Ops:
  7.2 0.0 copy-start
  7.2 0.0 reduce-scatter.2.cloned.1.call-start
  7.3 0.0 copy-start.3
  7.3 0.0 copy-start.4
  7.3 0.0 copy-start.5
  7.3 0.0 copy-start.6
  7.3 0.0 copy-start.7
  7.3 0.0 copy-start.8
  7.3 0.0 copy-start.9
  7.3 0.0 copy-start.10
  7.3 1.5 copy.56
  8.9 1.2 copy.57
  10.0 0.0 copy-done
  10.0 0.3 copy.58
  10.4 1.2 copy.59
  11.5 0.0 copy-done.3
  11.6 0.0 copy-done.4
  11.6 0.6 copy.69
  12.2 0.6 pad.9.refs_2_
  12.8 0.0 copy-done.10
  12.8 0.6 fusion.6.refs_1_
  13.4 179.3 %forward.1 = (bf16[1024,2048]{1,0:T(8,128)(2,1)}, bf16[1024,256]{1,0:T(8,128)(2,1)}, bf16[1024,256]{1,0:T(8,128)(2,1)}, bf16[1024,256]{1,0:T(8,128)(2,1)}, bf16[...) custom-call(bf16[128,2048]{1,0:T(8,128)(2,1)} %refs_13_.1, ...), custom_call_target="tpu_custom_call" | custom-call | tf_op jit(solution)/shard_map/forward/pallas_call | solution.py:2087
  192.7 55.4 %moe_forward.1 = (f32[1024,128]{1,0:T(8,128)}, bf16[8,96,128]{2,1,0:T(8,128)(2,1)}, bf16[1024,704]{1,0:T(8,128)(2,1)}, bf16[1024,704]{1,0:T(8,128)(2,1)}, bf16[1...) custom-call(bf16[128,2048]{1,0:T(8,128)(2,1)} %refs_12_.2, ...), custom_call_target="tpu_custom_call" | custom-call | flops 22145925120 | bytes 68681728 | tf_op jit(solution)/shard_map/moe_forward/pallas_call | solution.py:2148
  248.1 0.0 reduce-scatter.2.cloned.1.call-update
  248.1 46.7 %shared_backward.1 = (bf16[768,2048]{1,0:T(8,128)(2,1)}, bf16[1024,2048]{1,0:T(8,128)(2,1)}, f32[8,8,128]{2,1,0:T(8,128)}, bf16[512,704]{1,0:T(8,128)(2,1)}, bf1...) custom-call(bf16[1024,2048]{1,0:T(8,128)(2,1)} %get-tuple-element.92, ...), custom_call_target="tpu_custom_call" | custom-call | flops 17716740096 | bytes 59506688 | tf_op jit(solution)/shard_map/shared_backward/pallas_call | solution.py:2191
  294.8 1.4 copy.60
  296.2 0.5 collective-permute-start
  296.7 2.3 copy.61
  299.0 1.0 collective-permute-start.1
  300.0 0.5 collective-permute-start.2
  300.4 43.0 %routed_backward.1 = (bf16[1024,2048]{1,0:T(8,128)(2,1)}, bf16[2048,1408]{1,0:T(8,128)(2,1)}, bf16[2048,1408]{1,0:T(8,128)(2,1)}, bf16[1408,2048]{1,0:T(8,128)(2,1)}) custom-call(bf16[768,2048]{1,0:T(8,128)(2,1)} %get-tuple-element.100.grads_in, bf16[768,2048]{1,0:T(8,128)(2,1)} %get-tuple-element.101.rows_in, bf16[2048,1408]{1,0:T(8,128)(2,1)} %bitcast.69, ...), custom_call_target="tpu_custom_call" | custom-call | flops 26575110144 | bytes 85983232 | tf_op jit(solution)/shard_map/routed_backward/pallas_call | solution.py:2237
  343.4 1.2 copy.62
  344.7 0.5 dynamic-slice_bitcast_fusion.4.refs_16_
  345.2 0.6 dynamic-slice_bitcast_fusion.3.refs_15_
  345.8 0.0 collective-permute-done
  345.8 2.3 copy.63.refs_5_
  348.1 0.0 collective-permute-done.1
  348.1 2.3 copy.64.refs_6_
  350.3 0.0 collective-permute-done.2.refs_7_
  350.3 195.0 %backward.1 = (bf16[128,2048]{1,0:T(8,128)(2,1)}, bf16[4,128,768]{2,1,0:T(8,128)(2,1)}, bf16[4,256,128]{2,1,0:T(8,128)(2,1)}, f32[16,128]{1,0:T(8,128)}, f32[4,8...) custom-call(bf16[1024,2048]{1,0:T(8,128)(2,1)} %get-tuple-element.10, ...), custom_call_target="tpu_custom_call" | custom-call | tf_op jit(solution)/shard_map/backward/pallas_call | solution.py:2291
  545.3 0.7 copy.65
  546.1 11.5 %finish_grads.1 = (f32[128,2816]{1,0:T(8,128)}, f32[128,2816]{1,0:T(8,128)}, f32[2816,128]{1,0:T(8,128)}, f32[512,1408]{1,0:T(8,128)}, f32[512,1408]{1,0:T(8,128...) custom-call(bf16[4,128,704]{2,1,0:T(8,128)(2,1)} %get-tuple-element., ...), custom_call_target="tpu_custom_call" | custom-call | tf_op jit(solution)/shard_map/finish_grads/pallas_call | solution.py:2368
  557.5 0.7 dynamic-slice_bitcast_fusion
  558.2 0.0 copy-done.2
  558.2 0.5 slice_bitcast_fusion.1
  558.7 0.6 slice_bitcast_fusion
  559.3 2.3 add_convert_fusion
  561.6 0.8 copy.71
  (11 shorter events, 0.0 us)
Async XLA Ops:
  7.2 2.8 copy-start
  7.2 552.1 %reduce-scatter.2.cloned.1.call-start = ((), (), s32[]{:S(2)}) async-start(), calls=%async_computation.1 | async-start | bytes 4718592 | tf_op jit(solution)/shard_map/reduce_scatter | solution.py:2065
  7.3 4.3 copy-start.3
  7.3 4.3 copy-start.4
  7.3 4.3 copy-start.5
  7.3 4.9 copy-start.6
  7.3 5.5 copy-start.7
  7.3 5.5 copy-start.8
  7.3 5.5 copy-start.9
  7.3 5.4 copy-start.10
  296.2 49.6 %collective-permute-start = (bf16[512,704]{0,1:T(8,128)(2,1)S(1)}, bf16[512,704]{0,1:T(8,128)(2,1)}, u32[]{:S(2)}, u32[]{:S(2)}) collective-permute-start(bf16[512,704]{0,1:T(8,128)(2,1)S(1)} %copy.60), channel_id=1, source_target_pairs={{0,4},{2,6},{4,0},{6,2},{1,5},{3,7},{5,1},{7,3},{8,12},{10,14},{12... | collective-permute-start | bytes 2162696 | tf_op jit(solution)/shard_map/ppermute | solution.py:2235
  299.0 49.1 %collective-permute-start.1 = (bf16[512,704]{0,1:T(8,128)(2,1)}, bf16[512,704]{0,1:T(8,128)(2,1)}, u32[]{:S(2)}, u32[]{:S(2)}) collective-permute-start(bf16[512,704]{0,1:T(8,128)(2,1)} %copy.61), channel_id=1, source_target_pairs={{0,4},{2,6},{4,0},{6,2},{1,5},{3,7},{5,1},{7,3},{8,12},{10,14},{12... | collective-permute-start | bytes 2162696 | tf_op jit(solution)/shard_map/ppermute | solution.py:2235
  300.0 50.4 %collective-permute-start.2 = (bf16[2816,128]{1,0:T(8,128)(2,1)}, bf16[2816,128]{1,0:T(8,128)(2,1)}, u32[]{:S(2)}, u32[]{:S(2)}) collective-permute-start(bf16[2816,128]{1,0:T(8,128)(2,1)} %get-tuple-element.113), channel_id=1, source_target_pairs={{0,4},{2,6},{4,0},{6,2},{1,5},{3,7},{5,1},{7,3},{8,12},{10,14},{12... | collective-permute-start | bytes 2162696 | tf_op jit(solution)/shard_map/ppermute | solution.py:2235
  546.0 12.2 %copy-start.2 = (f32[16,128]{1,0:T(8,128)S(1)}, f32[16,128]{1,0:T(8,128)}, u32[]{:S(2)}) copy-start(f32[16,128]{1,0:T(8,128)} %get-tuple-element.126) | copy-start | bytes 24580
  546.0 15.5 %copy-start.1 = (bf16[128,2048]{1,0:T(8,128)(2,1)S(1)}, bf16[128,2048]{1,0:T(8,128)(2,1)}, u32[]{:S(2)}) copy-start(bf16[128,2048]{1,0:T(8,128)(2,1)} %get-tuple-element.175) | copy-start | bytes 1572868
Sparse Core Ops, SparseCore 0:
  248.2 90.4 reduce-scatter.1

commit v4 on v3

--- a/solution.py
+++ b/solution.py
@@ -595,7 +595,7 @@
     lax.fori_loop(0, total // step, one, 0)
 
 
-def chain_gather(wire, place, refs, arrived=None, own=None):
+def chain_gather(wire, place, refs, arrived=None, begun=False):
     n = place.n_dp
     z = place.z
     width = len(refs(z))
@@ -605,7 +605,7 @@
     def copies(slot, up, dist):
         return [
             wire.copy_to(
-                own[index] if own is not None and dist == 0 else ref,
+                ref,
                 ref,
                 place.up if up else place.down,
                 recv + slot * width + index,
@@ -619,8 +619,9 @@
             item.start()
 
     def land(slot, up, dist):
-        for item in copies(slot, up, dist):
-            item.wait_recv()
+        if dist > 1 or not begun:
+            for item in copies(slot, up, dist):
+                item.wait_recv()
         if arrived is not None:
             arrived(slot)
 
@@ -628,9 +629,10 @@
         for item in copies(slot, up, dist):
             item.wait_send()
 
-    pl.when(z < n - 1)(lambda: start(z, True, 0))
-    pl.when(z > 0)(lambda: start(z, False, 0))
-    yield
+    if not begun:
+        pl.when(z < n - 1)(lambda: start(z, True, 0))
+        pl.when(z > 0)(lambda: start(z, False, 0))
+        yield
     for dist in range(1, n):
         below, above = z - dist, z + dist
 
@@ -645,7 +647,7 @@
             pl.when(z > 0)(lambda: start(above, False, dist))
 
         yield
-    for dist in range(n):
+    for dist in range(1 if begun else 0, n):
         below, above = z - dist, z + dist
         pl.when((below >= 0) & (z < n - 1))(lambda: sent(below, True, dist))
         pl.when((above < n) & (z > 0))(lambda: sent(above, False, dist))
@@ -775,12 +777,13 @@
 
 def forward_kernel(
     n_blocks, n_dp,
-    tokens, small, ids, w_query, w_key, w_value, w_out, s_gate, s_up, s_down,
+    tokens, out_grad, small, ids, w_query, w_key, w_value, w_out, s_gate, s_up, s_down,
     bias, cosine, sine,
     attn_in_to, query_to, keys_to, values_to, attn_to, lse_to, hidden_to, moe_in,
-    heads_weight_to, out_weight_to, gate_weight, up_weight, down_weight, smalls, all_ids,
+    heads_weight_to, out_weight_to, gate_weight, up_weight, down_weight, smalls, all_ids, dy_group,
     x_seq, partial, got_core, got_one, got_two,
-    attn_in, query, keys, values, attn, lse, hidden, heads_weight, out_weight, send, recv, local,
+    attn_in, query, keys, values, attn, lse, hidden, heads_weight, out_weight,
+    shared_raw, shared_packed, send, recv, local,
 ):
     place = Place(n_dp)
     wire = Wire(send, recv)
@@ -799,6 +802,7 @@
     others = [(dz, dc) for dz in range(n_dp) for dc in range(n_ctx) if dz or dc]
     phases = Phases()
     phases.go("entry")
+    raw_in = [inside.start(src, shared_raw.at[k]) for k, src in enumerate((s_gate, s_up))]
 
     def moved(dz, dc, y_to):
         return (lax.bitwise_xor(z, jnp.int32(dz)), lax.bitwise_xor(c, jnp.int32(dc)), y_to)
@@ -812,14 +816,23 @@
     group = z * 2 + y
     shared_pieces = [[], [], []]
 
+    units = gate_weight.shape[3]
+
+    def pack(index):
+        raw_in[index].wait()
+        for part in range(n_dp):
+            shared_packed[index, part] = shared_raw[index, :, part * units : (part + 1) * units]
+
     def shared_along_dp(index):
+        if index < 2:
+            pack(index)
         for dz in (2, 3, 1, 0):
             to = lax.bitwise_xor(z, jnp.int32(dz))
             if index == 2:
                 src = s_down.at[rows_of(to, s_down.shape[0] // n_dp), :]
                 dst = down_weight.at[:, my_rows]
             else:
-                src = (s_gate, s_up)[index].at[to]
+                src = shared_packed.at[index, to]
                 dst = (gate_weight, up_weight)[index].at[z, c]
             if dz == 0:
                 item = inside.start(src, dst)
@@ -861,6 +874,12 @@
                 item = wire.copy(ids, all_ids.at[group], moved(dz, 0, y_to))
                 item.start()
                 small_copies.append(item)
+    def dy_rows(slot, half):
+        return dy_group.at[rows_of(slot * 2 + half, rows), :]
+
+    stores = [inside.start(out_grad, dy_rows(z, y))]
+    dy_over_y = wire.copy(out_grad, dy_rows(z, y), place.over_y)
+    dy_over_y.start()
     phases.go("exchanges")
     for item in exchanges:
         item.wait_recv()
@@ -961,7 +980,7 @@
         partial[at, :] = dot_f32(attn[at, :], out_weight[...], 1, 0).astype(low)
 
     by_rows(seq, block, output)
-    stores = [
+    stores += [
         inside.start(src, dst)
         for src, dst in (
             (attn_in, attn_in_to), (query, query_to), (keys, keys_to), (values, values_to),
@@ -991,39 +1010,54 @@
     here = inside.start(got_core.at[0], moe_in.at[at_group, :])
     here.wait()
 
-    y_recv = wire.take(n_dp)
-    y_send = wire.take_send(n_dp)
-
-    def to_y(slot):
-        at = rows_of(slot * 2 + y, rows)
-        return wire.copy_to(
-            moe_in.at[at, :], moe_in.at[at, :], place.over_y, y_recv + slot, y_send + slot
+    half_width = width // 2
+    y_recv = wire.take(2 * n_dp)
+    y_send = wire.take_send(2 * n_dp)
+
+    def moe_block(slot, half, part):
+        return moe_in.at[rows_of(slot * 2 + half, rows), pl.ds(part * half_width, half_width)]
+
+    def to_y(slot, part, half=None):
+        ref = moe_block(slot, y if half is None else half, part)
+        sem = 2 * slot + part
+        return wire.copy_to(ref, ref, place.over_y, y_recv + sem, y_send + sem)
+
+    chains = [
+        chain_gather(
+            wire,
+            place,
+            lambda slot, part=part: [moe_block(slot, y, part)],
+            arrived=lambda slot, part=part: to_y(slot, part).start(),
         )
-
-    def from_y(slot):
-        at = rows_of(slot * 2 + place.yn, rows)
-        return wire.copy_to(
-            moe_in.at[at, :], moe_in.at[at, :], place.over_y, y_recv + slot, y_send + slot
-        )
-
-    rows_chain = chain_gather(
-        wire,
-        place,
-        lambda slot: [moe_in.at[rows_of(slot * 2 + y, rows), :]],
-        arrived=lambda slot: to_y(slot).start(),
-    )
-    next(rows_chain)
-    to_y(z).start()
-    phases.go("rows_one")
-    next(rows_chain)
+        for part in range(2)
+    ]
+    for part in range(2):
+        next(chains[part])
+        to_y(z, part).start()
     phases.go("shared_one")
     shared_over_x(1)
-    phases.go("rows_two")
-    next(rows_chain)
+    phases.go("rows_one")
+    for chain in chains:
+        next(chain)
     phases.go("shared_two")
     shared_over_x(2)
+    phases.go("rows_two")
+    for chain in chains:
+        next(chain)
     phases.go("rows_three")
-    finish(rows_chain)
+    for chain in chains:
+        next(chain)
+    dy_recv = wire.take(2)
+    dy_send = wire.take_send(2)
+
+    def dy_step(up):
+        ref = dy_rows(z, y)
+        to = place.up if up else place.down
+        return wire.copy_to(out_grad, ref, to, dy_recv + (0 if up else 1), dy_send + (0 if up else 1))
+
+    pl.when(z < n_dp - 1)(lambda: dy_step(True).start())
+    pl.when(z > 0)(lambda: dy_step(False).start())
+    finish(*chains)
     phases.go("shared_close")
     for index in range(3):
         shared_close(index)
@@ -1031,8 +1065,22 @@
         item.wait_recv()
     phases.go("rows_over_y")
     for slot in range(n_dp):
-        from_y(slot).wait_recv()
-        to_y(slot).wait_send()
+        for part in range(2):
+            to_y(slot, part, place.yn).wait_recv()
+            to_y(slot, part).wait_send()
+    phases.go("dy")
+    dy_over_y.wait_recv()
+
+    @pl.when(z > 0)
+    def _():
+        dy_step(True).wait_recv()
+        dy_step(False).wait_send()
+
+    @pl.when(z < n_dp - 1)
+    def _():
+        dy_step(False).wait_recv()
+        dy_step(True).wait_send()
+
     for item in stores:
         item.wait()
     wire.drain()
@@ -1172,17 +1220,16 @@
 
 def backward_kernel(
     n_blocks, n_dp,
-    d_in_part, scalars, k_sgate, k_sup, k_sdown, x_sgate, x_sup, x_sdown, g_egate, g_eup, g_edown,
+    own_sum, got_scalars, k_sup, k_sdown, x_sup, x_sdown, r_eup, r_edown,
     hidden_in, out_grad_in, tokens_in, smalls, probs, mix,
     heads_weight_in, w_out_in, query_in, keys_in, values_in, attn_from, lse_in, attn_in_from,
     cosine_in, sine_in,
     input_grad, heads_grad, out_weight_grad, small_grad, bias_grad,
-    t_sgate, t_sup, t_sdown, r_egate, r_eup, r_edown, x_egate, x_eup, x_edown,
-    s_sgate, s_sup, s_sdown, k_egate, k_eup, k_edown,
-    partial, got_y, got_z, got_scalars, d_hidden, side, moe_own, terms, acc,
+    t_sup, t_sdown, x_eup, x_edown, s_sup, s_sdown,
+    partial, d_hidden, side, moe_own, terms, acc,
     proj, d_attn, d_qkv, d_keys, d_values, got_core, got_one, got_two,
     g_heads, g_out, heads_below, heads_above, out_below, out_above, out_block,
-    stage, landed, over_y, wide_buf, tall_buf, gate_buf, down_buf,
+    stage, landed, over_y, gate_buf, down_buf,
     hidden, out_grad, tokens, heads_weight, w_out, query, keys, values, attn, lse, attn_in,
     cosine, sine, send, recv, local, adds,
 ):
@@ -1209,86 +1256,15 @@
 
     phases = Phases()
     phases.go("entry")
-    fill = inside.start(d_in_part, partial)
     barrier(
         [moved(dz, dc, y) for dz, dc in others] + [moved(dz, 0, place.yn) for dz in range(n_dp)]
     )
-    fill.wait()
-
-    def group_rows(dz, y_of):
-        return rows_of(lax.bitwise_xor(z, jnp.int32(dz)) * 2 + y_of, rows)
-
-    order = (2, 3, 1, 0)
-    y_swaps = {}
-    for dz in order:
-        item = wire.copy(partial.at[group_rows(dz, place.yn), :], got_y.at[dz], place.over_y)
-        item.start()
-        y_swaps[dz] = item
-    group = z * 2 + y
-    scalar_items = []
-    for dz in range(n_dp):
-        for y_to in (y, place.yn):
-            target = lax.bitwise_xor(z, jnp.int32(dz)) * 2 + y_to
-            if dz == 0 and y_to is y:
-                item = inside.start(scalars.at[target], got_scalars.at[group])
-            else:
-                item = wire.copy(
-                    scalars.at[target], got_scalars.at[group], moved(dz, 0, y_to)
-                )
-                item.start()
-            scalar_items.append(item)
-
-    def piece(dx, sibling):
-        side_of = lax.bitwise_xor(lax.div(c, 2), jnp.int32(dx))
-        return side_of * 2 + (1 - core if sibling else core)
-
-    piece_cols = g_edown.shape[1] // n_ctx
-
-    def routed_pieces(dx, sibling):
-        index = piece(dx, sibling)
-        return [g_egate.at[index], g_eup.at[index], g_edown.at[:, rows_of(index, piece_cols)]]
-
-    routed_core = []
-    for index, dst in enumerate((k_egate, k_eup, k_edown)):
-        for dx in (1, 0):
-            item = wire.copy(routed_pieces(dx, True)[index], dst.at[dx], place.core)
-            item.start()
-            routed_core.append(item)
-
-    z_swaps = []
-
-    def over_dp(dz):
-        y_swaps[dz].wait_recv()
-        target = lax.bitwise_xor(z, jnp.int32(dz)) * 2 + y
-        add_into(partial, pl.ds(0, width), target * rows, got_y.at[dz])
-        if dz:
-            item = wire.copy(
-                partial.at[rows_of(target, rows), :], got_z.at[dz - 1], moved(dz, 0, y)
-            )
-            item.start()
-            z_swaps.append(item)
-
-    def routed_sum(index):
-        for item in routed_core[2 * index : 2 * index + 2]:
-            item.wait_recv()
-        kept = (k_egate, k_eup, k_edown)[index]
-        total = (r_egate, r_eup, r_edown)[index]
-        buf = tall_buf if index == 2 else wide_buf
-        step = buf.shape[2]
-        chunks = []
-        for dx in (1, 0):
-            mine = routed_pieces(dx, False)[index]
-            for start in range(0, mine.shape[0], step):
-                at = pl.ds(start, step)
-                chunks.append((mine.at[at, :], kept.at[dx, at, :], total.at[dx, at, :]))
-        adder.run(buf, chunks)
-
     def go_over_x(index, part=0, parts=1):
-        total = (r_egate, r_eup, r_edown)[index]
-        got = (x_egate, x_eup, x_edown)[index]
+        total = (r_eup, r_edown)[index]
+        got = (x_eup, x_edown)[index]
         count = got.shape[0] // parts
         at = pl.ds(part * count, count)
-        item = wire.copy(total.at[1, at, :], got.at[at, :], place.over_x)
+        item = wire.copy(total.at[at, :], got.at[at, :], place.over_x)
         item.start()
         return item
 
@@ -1297,17 +1273,17 @@
         return ref.at[pl.ds(dz * size, size), :]
 
     def shared_ready(index):
-        buf = down_buf if index == 2 else gate_buf
-        kept = (k_sgate, k_sup, k_sdown)[index]
-        got = (x_sgate, x_sup, x_sdown)[index]
-        ready = (s_sgate, s_sup, s_sdown)[index]
+        buf = (gate_buf, down_buf)[index]
+        kept = (k_sup, k_sdown)[index]
+        got = (x_sup, x_sdown)[index]
+        ready = (s_sup, s_sdown)[index]
         adder.run(buf, [(part_of(kept, dz), part_of(got, dz), ready.at[dz]) for dz in range(n_dp)])
 
     shared_last = []
 
     def shared_along_dp(index):
-        ready = (s_sgate, s_sup, s_sdown)[index]
-        target = (t_sgate, t_sup, t_sdown)[index]
+        ready = (s_sup, s_sdown)[index]
+        target = (t_sup, t_sdown)[index]
         for dz in (2, 3, 1, 0):
             to = lax.bitwise_xor(z, jnp.int32(dz))
             if dz:
@@ -1326,31 +1302,7 @@
             (attn_in_from, attn_in),
         )
     ]
-    phases.go("routed_gate")
-    routed_sum(0)
-    routed_over = [go_over_x(0)]
-    phases.go("over_dp_two")
-    over_dp(2)
-    phases.go("routed_up")
-    routed_sum(1)
-    routed_over.append(go_over_x(1, 0, 2))
-    phases.go("over_dp_three")
-    over_dp(3)
-    phases.go("routed_down")
-    routed_sum(2)
-    phases.go("over_dp_one")
-    over_dp(1)
-    phases.go("shared_ready")
-    shared_ready(0)
-    shared_ready(1)
-    phases.go("over_dp_own")
-    over_dp(0)
-    phases.go("shared_ready_last")
-    shared_ready(2)
-
     phases.go("router")
-    for item in scalar_items:
-        item.wait_recv()
     d_rprobs = got_scalars[:, 0, :]
     probs_own = probs[...]
     d_logits = probs_own * (d_rprobs - jnp.sum(probs_own * d_rprobs, axis=0, keepdims=True))
@@ -1370,16 +1322,10 @@
     gain_one = smalls[n_experts + 1 : n_experts + 2, :].astype(f32)
     gain_two = smalls[n_experts + 2 : n_experts + 3, :].astype(f32)
     acc[...] = jnp.zeros_like(acc)
-    phases.go("wait_sums")
-    for item in z_swaps:
-        item.wait_recv()
     own_plane = place.block(c, y) * rows
 
     def norm_two(at):
-        mine = pl.ds(pl.multiple_of(group * rows + at.start, at.size), at.size)
-        d_moe = side[at, :] + partial[mine, :].astype(f32)
-        for dz in range(n_dp - 1):
-            d_moe = d_moe + got_z[dz, at, :].astype(f32)
+        d_moe = side[at, :] + own_sum[at, :]
         total = hidden[at, :]
         rstd = lax.rsqrt(jnp.mean(total * total, axis=1, keepdims=True) + EPS)
         normed = total * rstd
@@ -1393,7 +1339,7 @@
         proj[pl.ds(pl.multiple_of(own_plane + at.start, at.size), at.size), :] = back.astype(low)
 
     phases.go("norm_two")
-    for item in loads:
+    for item in loads[:3]:
         item.wait()
     by_rows(rows, 16, norm_two)
     phases.go("gather_in_plane")
@@ -1401,17 +1347,23 @@
     next(proj_in)
     side[0:48, :] = dot_f32(terms[...], moe_own[...], 1, 0)
 
-    for index in range(3):
-        shared_along_dp(index)
+    phases.go("shared_up")
+    shared_ready(0)
+    shared_along_dp(0)
     phases.go("gather_relay")
     next(proj_in)
+    phases.go("shared_down")
+    shared_ready(1)
+    shared_along_dp(1)
     phases.go("gather_close")
     next(proj_in)
     phases.go("gather_end")
     finish(proj_in)
 
     phases.go("attention")
-    routed_over.append(go_over_x(1, 1, 2))
+    routed_over = [go_over_x(0, 0, 2)]
+    for item in loads[3:]:
+        item.wait()
     by_share = n_ctx * share
 
     def out_weight(target):
@@ -1463,7 +1415,6 @@
         d_qkv[:, 2 * cols + start : 2 * cols + start + head_dim] = d_values[...].astype(low)
 
     phases.go("attention_in_grad")
-    wire.drain(list(y_swaps.values()) + z_swaps)
 
     def output(at):
         partial[at, :] = dot_f32(d_qkv[at, :], heads_weight[...], 1, 1).astype(low)
@@ -1479,7 +1430,6 @@
 
     each(n_dp // 2, heads_weights)
     next(reduce)
-    next(out_chain)
     each(n_dp // 2, lambda index: heads_weights(index + n_dp // 2))
     heads_chain = chain_reduce(
         wire,
@@ -1489,7 +1439,7 @@
     next(heads_chain)
     phases.go("sum_in_plane_end")
     finish(reduce)
-    routed_over.append(go_over_x(2))
+    routed_over += [go_over_x(0, 1, 2), go_over_x(1)]
 
     def norm_one(at):
         d_attn_in = plane_sum(place, partial, got_one, got_two, at)
@@ -1580,7 +1530,7 @@
 
 
 def moe_forward(
-    n_dp, out_grad, moe_in, smalls, ids, s_gate_in, s_up_in, s_down_in, e_gate, e_up, e_down,
+    n_dp, dy_begun, moe_in, smalls, ids, s_gate_in, s_up_in, s_down_in, e_gate, e_up, e_down,
     cols, pick, s_slope, s_silu, s_hidden, e_slope, e_silu, e_hidden, rows_in, part, e_out, shared,
     dy_group,
     x, wg, wu, wd, v_slope, v_silu, v_hidden, r_slope, r_silu, r_hidden, rows, out, sh,
@@ -1618,17 +1568,9 @@
         place_here,
         lambda slot: [block_of(slot)],
         arrived=lambda slot: over_y(slot).start(),
-        own=[out_grad],
+        begun=True,
     )
     next(dy_chain)
-
-    def own_over_y():
-        return wire.copy_to(
-            out_grad, block_of(z), place_here.over_y, y_recv + z, y_send + z
-        )
-
-    own_over_y().start()
-    own = inside.start(out_grad, block_of(z))
     loads += [inside.start(src, dst) for src, dst in ((e_gate, wg), (e_up, wu), (e_down, wd))]
     hit = jnp.concatenate(
         [jnp.any(ids[s] == mine, axis=0, keepdims=True).astype(f32) for s in range(n_experts)], axis=0
@@ -1673,6 +1615,7 @@
 
     phases.go("shared")
     by_rows(x.shape[0], 512, shared_tile)
+    phases.go("dy_two")
     next(dy_chain)
     stores = [
         inside.start(src, dst)
@@ -1701,12 +1644,10 @@
 
     phases.go("routed")
     routed_tile(pl.ds(0, 384))
-    phases.go("dy_two")
+    phases.go("dy_three")
     next(dy_chain)
     phases.go("routed_end")
     routed_tile(pl.ds(384, 384))
-    phases.go("dy_three")
-    next(dy_chain)
     stores.append(inside.start(out, e_out))
     stores += [
         inside.start(src, dst)
@@ -1730,9 +1671,12 @@
     phases.go("over_y")
     finish(dy_chain)
     for slot in range(n_dp):
-        over_y(slot).wait_recv()
-        over_y(slot).wait_send()
-    own.wait()
+
+        @pl.when(z != slot)
+        def _():
+            over_y(slot).wait_recv()
+            over_y(slot).wait_send()
+
     phases.go(None)
 
 
@@ -1740,9 +1684,9 @@
     n_dp, dy_group, cols, pick, s_gate_in, s_up_in, s_down_in, s_slope_in, s_silu_in,
     s_hidden, e_out, shared, moe_in,
     grads_in, part, scalars, keep_gate, keep_up, keep_down, give_gate, give_up, give_down,
-    dy, out, sh, tok, d_sh, rows, grads, total, x, hidden,
+    dy, out, sh, d_sh, rows, grads, total, x, hidden,
     g_gate, g_up, g_down, got_gate, got_up, got_down,
-    s_gate, s_up, s_down, s_slope, s_silu, sums, send, recv, local, slots,
+    s_gate, s_up, s_down, s_slope, s_silu, sums, picked, slot_sums, send, recv, local, slots,
 ):
     f32, low = jnp.float32, jnp.bfloat16
     inside = Local(local)
@@ -1795,21 +1739,32 @@
             coming.append(fetch(index + depth - 1))
         for item in coming[index]:
             item.wait()
-        tok[...] = dot_f32(pick[index], out[slot], 0, 0)
+        here = pl.ds(index * tok_rows, tok_rows)
+        chosen = pick[index].astype(f32)
+        gate = jnp.transpose(cols[here, :])[n_experts + 1 : n_experts + 2, :]
+        gate = jnp.sum(chosen * gate, axis=1, keepdims=True)
+        picked[...] = dot_f32(pick[index], dy[slot], 1, 0)
+
+        def slot_rows(at):
+            grad = picked[at, :]
+            this = out[slot, at, :].astype(f32)
+            slot_sums[at, 0:1] = jnp.sum(this * grad, axis=1, keepdims=True)
+
+        by_rows(CAP, 32, slot_rows)
+        rows[pl.ds(index * CAP, CAP), :] = (gate * picked[...]).astype(low)
+        d_gate = jnp.sum(chosen * slot_sums[:, 0:1], axis=0, keepdims=True)
 
         def chunk(at):
-            here = pl.ds(pl.multiple_of(index * tok_rows + at.start, at.size), at.size)
+            there = pl.ds(pl.multiple_of(index * tok_rows + at.start, at.size), at.size)
             grad = dy[slot, at, :].astype(f32)
-            mix = cols[here, n_experts : n_experts + 1]
-            gate = cols[here, n_experts + 1 : n_experts + 2]
-            d_sh[here, :] = (mix * grad).astype(low)
-            sums[at, 0:1] = jnp.sum(tok[at, :] * grad, axis=1, keepdims=True)
-            sums[at, 1:2] = jnp.sum(sh[slot, at, :].astype(f32) * grad, axis=1, keepdims=True)
-            dy[slot, at, :] = (gate * grad).astype(low)
+            mix = cols[there, n_experts : n_experts + 1]
+            d_sh[there, :] = (mix * grad).astype(low)
+            sums[at, 0:1] = jnp.sum(sh[slot, at, :].astype(f32) * grad, axis=1, keepdims=True)
 
         by_rows(tok_rows, 32, chunk)
-        scalars[index] = jnp.transpose(sums[...])[0:8, :]
-        rows[pl.ds(index * CAP, CAP), :] = dot_f32(pick[index], dy[slot], 1, 0).astype(low)
+        shared_dot = jnp.transpose(sums[...])[0:1, :]
+        row_of = lax.broadcasted_iota(jnp.int32, (8, tok_rows), 0)
+        scalars[index] = jnp.where(row_of == 0, d_gate, jnp.where(row_of == 1, shared_dot, 0.0))
     stores = [inside.start(rows, grads_in)]
 
     def shared_tile(at):
@@ -1887,16 +1842,25 @@
 
 
 def routed_backward(
-    grads_in, rows_in, e_gate, e_up, e_down, slope_in, silu_in, hidden_in, pick, shared_part,
-    part, o_gate, o_up, o_down,
-    wg, wu, wd, grads, rows, slope, silu, hidden, d_hid, d_in, total, buf_gate, buf_up, buf_down,
-    local, stores,
+    n_dp, grads_in, rows_in, e_gate, e_up, e_down, slope_in, silu_in, hidden_in, shared_part, scalars,
+    keep_sgate, give_sgate, give_sup, give_sdown, pick,
+    own_sum, got_scalars, t_sgate, x_sup, x_sdown,
+    keep_gate, keep_up, keep_down, give_up, give_down, x_gate,
+    wg, wu, wd, grads, rows, slope, silu, hidden, d_hid, d_in, total,
+    got_gate, got_up, got_down, got_y, got_dp, x_sgate, sum_sgate, send, recv, local,
 ):
     f32, low = jnp.float32, jnp.bfloat16
     inside = Local(local)
+    wire = Wire(send, recv)
+    place = Place(n_dp)
+    z, c, y = place.z, place.c, place.y
     n_experts = pick.shape[0]
     tok_rows = pick.shape[2]
     units = wg.shape[1]
+    width = rows.shape[1]
+    core = lax.rem(c, 2)
+    chip = lax.div(c, 2)
+    group = z * 2 + y
     phases = Phases()
     phases.go("entry")
     loads = [
@@ -1904,8 +1868,27 @@
         for src, dst in (
             (grads_in, grads), (e_down, wd), (slope_in, slope), (silu_in, silu),
             (e_gate, wg), (e_up, wu), (shared_part, total), (rows_in, rows), (hidden_in, hidden),
+            (keep_sgate, sum_sgate),
         )
     ]
+
+    def near(dz, y_to):
+        return (lax.bitwise_xor(z, jnp.int32(dz)), c, y_to)
+
+    members = [(dz, y_to) for dz in range(n_dp) for y_to in (y, place.yn) if dz or y_to is not y]
+    barrier([place.core, place.over_x] + [near(dz, y_to) for dz, y_to in members])
+
+    over_x = []
+    for src, dst in ((give_sgate, x_sgate), (give_sup, x_sup), (give_sdown, x_sdown)):
+        item = wire.copy(src, dst, place.over_x)
+        item.start()
+        over_x.append(item)
+    scalar_items = [inside.start(scalars.at[group], got_scalars.at[group])]
+    for dz, y_to in members:
+        target = lax.bitwise_xor(z, jnp.int32(dz)) * 2 + y_to
+        item = wire.copy(scalars.at[target], got_scalars.at[group], near(dz, y_to))
+        item.start()
+        scalar_items.append(item)
     for item in loads[:4]:
         item.wait()
     phases.go("routed")
@@ -1934,63 +1917,177 @@
         return carry
 
     lax.fori_loop(0, n_experts, to_tokens, 0)
-    done = inside.start(total, part)
+
+    orders = ((3, 2, 1, 0), (3, 0, 2, 1), (0, 3, 1, 2), (0, 1, 2, 3))
+    lower = 1 - lax.div(z, 2)
+    order = (
+        3 * lower,
+        lower * (2 - 2 * z) + (1 - lower) * (7 - 2 * z),
+        1 + lax.rem(z, 2),
+        z,
+    )
+    y_swaps = []
+    for step in range(n_dp):
+        from_row = order[step] * 2 + place.yn
+        item = wire.copy(total.at[rows_of(from_row, tok_rows), :], got_y.at[step], place.over_y)
+        item.start()
+        y_swaps.append(item)
+    dp_recv = wire.take(2 * n_dp)
+    dp_send = wire.take_send(2 * n_dp)
+
+    def along(target, up):
+        slot = target - 1 if up else n_dp - 1 + target
+        return wire.copy_to(
+            total.at[pl.ds(pl.multiple_of((target * 2 + y) * tok_rows, tok_rows), tok_rows), :],
+            got_dp.at[slot],
+            place.up if up else place.down,
+            dp_recv + slot,
+            dp_send + slot,
+        )
+
+    def add_from(target, up):
+        along(target, up).wait_recv()
+        slot = target - 1 if up else n_dp - 1 + target
+        add_into(total, pl.ds(0, width), (target * 2 + y) * tok_rows, got_dp.at[slot])
+
+    def over_dp(step):
+        y_swaps[step].wait_recv()
+        add_into(total, pl.ds(0, width), (order[step] * 2 + y) * tok_rows, got_y.at[step])
+        for here in range(n_dp):
+            target = orders[here][step]
+
+            @pl.when(z == here)
+            def _():
+                if target == here:
+                    if here > 0:
+                        add_from(target, True)
+                    if here < n_dp - 1:
+                        add_from(target, False)
+                else:
+                    up = target > here
+                    if 0 < here < n_dp - 1:
+                        add_from(target, up)
+                    along(target, up).start()
+
+    phases.go("shared_gate")
+    over_x[0].wait_recv()
+    add_block(sum_sgate, x_sgate)
+    size = t_sgate.shape[1]
+    along_dp = []
+    for dz in (2, 3, 1, 0):
+        to = lax.bitwise_xor(z, jnp.int32(dz))
+        src = sum_sgate.at[rows_of(to, size), :]
+        if dz:
+            item = wire.copy(src, t_sgate.at[z], near(dz, y))
+            item.start()
+        else:
+            item = inside.start(src, t_sgate.at[z])
+        along_dp.append(item)
+
+    def piece(dx, sibling):
+        return lax.bitwise_xor(chip, jnp.int32(dx)) * 2 + (1 - core if sibling else core)
+
+    quarter = width // 4
+    tile = quarter // 2
+
+    def in_grads(index):
+        def one(part, carry):
+            at = pl.ds(pl.multiple_of(index * quarter + part * tile, tile), tile)
+            value = dot_f32(rows[:, at], d_hid[...], 0, 0)
+            wg[at, :] = value[:, 0:units].astype(low)
+            wu[at, :] = value[:, units : 2 * units].astype(low)
+            return carry
+
+        lax.fori_loop(0, 2, one, 0)
+
+    def down_grads(index):
+        at = rows_of(index, quarter)
+        wd[:, at] = dot_f32(hidden[...], grads[:, at], 0, 0).astype(low)
+
     phases.go("in_grads")
-
-    def products(first, steps, size, outs, product):
-        def copy(index, k):
-            slot = lax.rem(index, 2)
-            buf, target = outs[k]
-            return pltpu.make_async_copy(buf.at[slot], target(index), stores.at[slot, first + k])
-
-        def one(index, carry):
-            for k in range(len(outs)):
-
-                @pl.when(index >= 2)
-                def _():
-                    copy(index - 2, k).wait()
-
-            value = product(rows_of(index, size))
-            for k, (buf, _) in enumerate(outs):
-                width = buf.shape[2]
-                buf[lax.rem(index, 2)] = value[:, k * width : (k + 1) * width].astype(low)
-                copy(index, k).start()
-            return carry
-
-        lax.fori_loop(0, steps, one, 0)
-        for k in range(len(outs)):
-            for last in (steps - 2, steps - 1):
-                copy(jnp.int32(last), k).wait()
-
-    tall = buf_gate.shape[1]
-    products(
-        0,
-        rows.shape[1] // tall,
-        tall,
-        [
-            (buf_gate, lambda index: o_gate.at[rows_of(index, tall), :]),
-            (buf_up, lambda index: o_up.at[rows_of(index, tall), :]),
-        ],
-        lambda at: dot_f32(rows[:, at], d_hid[...], 0, 0),
-    )
+    sent = {}
+    for dx in (1, 0):
+        index = piece(dx, True)
+        in_grads(index)
+        at = rows_of(index, quarter)
+        sent[dx] = [
+            wire.copy(wg.at[at, :], got_gate.at[dx], place.core),
+            wire.copy(wu.at[at, :], got_up.at[dx], place.core),
+        ]
+        for item in sent[dx]:
+            item.start()
+    for dx in (1, 0):
+        in_grads(piece(dx, False))
+    phases.go("gate_sums")
+
+    def finish_piece(grad, dx, got, target):
+        at = rows_of(piece(dx, False), quarter)
+        add_block(grad.at[at, :], got.at[dx])
+        if target is not None:
+            stores.append(inside.start(grad.at[at, :], target))
+        return grad.at[at, :]
+
+    stores = []
+    sent[1][0].wait_recv()
+    gate_over = wire.copy(finish_piece(wg, 1, got_gate, None), x_gate, place.over_x)
+    gate_over.start()
+    phases.go("over_dp_one")
+    over_dp(0)
     phases.go("down_grads")
-    wide = buf_down.shape[2]
-    products(
-        2,
-        grads.shape[1] // wide,
-        wide,
-        [(buf_down, lambda index: o_down.at[:, rows_of(index, wide)])],
-        lambda at: dot_f32(hidden[...], grads[:, at], 0, 0),
-    )
-    phases.go("stores")
-    done.wait()
+    down = {}
+    for dx in (1, 0):
+        index = piece(dx, True)
+        down_grads(index)
+        down[dx] = wire.copy(wd.at[:, rows_of(index, quarter)], got_down.at[dx], place.core)
+        down[dx].start()
+    for dx in (1, 0):
+        down_grads(piece(dx, False))
+    phases.go("over_dp_two")
+    over_dp(1)
+    phases.go("sums")
+    sent[1][1].wait_recv()
+    finish_piece(wu, 1, got_up, give_up)
+    for item in sent[0]:
+        item.wait_recv()
+    finish_piece(wg, 0, got_gate, keep_gate)
+    finish_piece(wu, 0, got_up, keep_up)
+    for dx, target in ((1, give_down), (0, keep_down)):
+        down[dx].wait_recv()
+        at = rows_of(piece(dx, False), quarter)
+        add_into(wd, at, 0, got_down.at[dx])
+        stores.append(inside.start(wd.at[:, at], target))
+    phases.go("over_dp_three")
+    over_dp(2)
+    phases.go("over_dp_own")
+    over_dp(3)
+    for here in range(n_dp):
+
+        @pl.when(z == here)
+        def _():
+            for target in range(n_dp):
+                if target != here:
+                    along(target, target > here).wait_send()
+
+
+    def add_up(at):
+        mine = pl.ds(pl.multiple_of(group * tok_rows + at.start, at.size), at.size)
+        own_sum[at, :] = total[mine, :].astype(f32)
+
+    by_rows(tok_rows, 16, add_up)
+    phases.go("wait_all")
+    for item in stores:
+        item.wait()
+    for item in over_x[1:] + scalar_items + along_dp + [gate_over]:
+        item.wait_recv()
+    wire.drain()
     phases.go(None)
 
 
 def finish_grads(n_ctx, *refs):
     (
-        t_gate, t_up, t_down, own_gate, own_up, own_down, far_gate, far_up, far_down, heads, out_weight,
-        o_sgate, o_sup, o_sdown, o_egate, o_eup, o_edown, o_query, o_key, o_value, o_out,
+        t_gate, t_up, t_down, own_gate, own_up, own_down,
+        far_gate, far_up, far_down, heads, out_weight, hidden, moe_sum,
+        o_sgate, o_sup, o_sdown, o_egate, o_eup, o_edown, o_query, o_key, o_value, o_out, o_mixed,
     ) = refs
     f32 = jnp.float32
     n_dp, share, units = t_gate.shape
@@ -2006,6 +2103,7 @@
             target[at, :] = own[at, :].astype(f32) + far[at, :].astype(f32)
 
         by_rows(target.shape[0], 32, add)
+    o_mixed[...] = (hidden[...] + moe_sum[...].astype(f32)).astype(o_mixed.dtype)
     cols = heads.shape[2] // 3
     for k, target in enumerate((o_query, o_key, o_value)):
         for c in range(n_ctx):
@@ -2071,9 +2169,6 @@
     ids = jnp.pad(expert_ids.T, ((0, 8 - expert_ids.shape[1]), (0, 0)), constant_values=-1)
     hidden_units = shared_in_gate.shape[1] // n_dp
 
-    def by_dp(weight):
-        return weight.reshape(weight.shape[0], n_dp, hidden_units).transpose(1, 0, 2)
-
     biases = jnp.stack([query_bias_heads, bias_key, bias_value]).astype(f32)
     biases = lax.dynamic_slice_in_dim(biases, ctx * heads, heads, 1).reshape(3, cols)
     cosine, sine = whole_tables(seq_len, head_dim)
@@ -2083,7 +2178,7 @@
     half_width = width // 2
     (
         attn_in, query, keys, values, attn, lse, hidden_own, moe_in,
-        heads_weight, wo, sg, su, sd, small, ids_group,
+        heads_weight, wo, sg, su, sd, small, ids_group, dy_begun,
     ) = pl.pallas_call(
         lambda *refs: forward_kernel(n_blocks, n_dp, *refs),
         out_shape=[
@@ -2102,9 +2197,10 @@
             like((hidden_units, width), low),
             like((16, width), low),
             like((n_group, 8, tok_rows), jnp.int32),
+            like((n_group * tok_rows, width), low),
         ],
-        in_specs=[anywhere] * 10 + [vmem] * 3,
-        out_specs=[anywhere] * 13 + [vmem, anywhere],
+        in_specs=[anywhere] * 11 + [vmem] * 3,
+        out_specs=[anywhere] * 13 + [vmem] + [anywhere] * 2,
         scratch_shapes=[
             pltpu.VMEM((seq_len, width), low),
             pltpu.VMEM((seq_len, width), low),
@@ -2120,8 +2216,10 @@
             pltpu.VMEM((tok_rows, width), f32),
             pltpu.VMEM((width, 3 * cols), low),
             pltpu.VMEM((cols, width), low),
-            pltpu.SemaphoreType.DMA((144,)),
-            pltpu.SemaphoreType.DMA((144,)),
+            pltpu.VMEM((2, share, n_dp * hidden_units), low),
+            pltpu.VMEM((2, n_dp, share, hidden_units), low),
+            pltpu.SemaphoreType.DMA((160,)),
+            pltpu.SemaphoreType.DMA((160,)),
             pltpu.SemaphoreType.DMA((32,)),
         ],
         name="forward",
@@ -2129,8 +2227,8 @@
             collective_id=1, has_side_effects=True, vmem_limit_bytes=60 * 2**20
         ),
     )(
-        tokens, small, ids, w_query, w_key, w_value, w_out,
-        by_dp(shared_in_gate), by_dp(shared_in_up), shared_down, biases, cosine, sine,
+        tokens, out_grad, small, ids, w_query, w_key, w_value, w_out,
+        shared_in_gate, shared_in_up, shared_down, biases, cosine, sine,
     )
     sg, su = sg.reshape(width, hidden_units), su.reshape(width, hidden_units)
     units = expert_gate.shape[2]
@@ -2184,7 +2282,8 @@
             bytes_accessed=2 * (9 * width * units + 4 * group_rows * width),
             transcendentals=0,
         ),
-    )(out_grad, moe_in, small, ids_group, sg, su, sd, gate_weight, up_weight, down_weight)
+        input_output_aliases={0: 12},
+    )(dy_begun, moe_in, small, ids_group, sg, su, sd, gate_weight, up_weight, down_weight)
     lanes = -(-hidden_units // 128) * 128
     block_kinds = [(n_dp, share, hidden_units)] * 2 + [(n_dp, hidden_units, share)]
     shared_all = [(n_dp * n_ctx, share, hidden_units)] * 2 + [(n_dp * n_ctx, hidden_units, share)]
@@ -2202,7 +2301,6 @@
             pltpu.VMEM((4, tok_rows, width), low),
             pltpu.VMEM((4, CAP, width), low),
             pltpu.VMEM((4, tok_rows, width), low),
-            pltpu.VMEM((tok_rows, width), f32),
             pltpu.VMEM((group_rows, width), low),
             pltpu.VMEM((slots, width), low),
             pltpu.VMEM((group_rows, 2 * lanes), low),
@@ -2214,7 +2312,11 @@
         + [pltpu.VMEM((2, *kind), low) for kind in block_kinds]
         + s_weights
         + [pltpu.VMEM((group_rows, hidden_units), low)] * 2
-        + [pltpu.VMEM((tok_rows, 128), f32)]
+        + [
+            pltpu.VMEM((tok_rows, 128), f32),
+            pltpu.VMEM((CAP, width), f32),
+            pltpu.VMEM((CAP, 128), f32),
+        ]
         + [pltpu.SemaphoreType.DMA((32,))] * 2
         + [pltpu.SemaphoreType.DMA((48,)), pltpu.SemaphoreType.DMA((12,))],
         name="shared_backward",
@@ -2231,19 +2333,21 @@
     )
     grads_in, shared_part, scalars = results[:3]
     keep = results[3:6]
-    over_x = [(index, index ^ 2) for index in range(n_ctx)]
-    got = [lax.ppermute(item, CONTEXT, over_x) for item in results[6:9]]
+    give = results[6:9]
     quarter = width // n_ctx
-    d_in_part, g_egate, g_eup, g_edown = pl.pallas_call(
-        routed_backward,
-        out_shape=[
-            like((group_rows, width), low),
-            like((width, units), low),
-            like((width, units), low),
-            like((units, width), low),
-        ],
-        in_specs=[anywhere] * 8 + [vmem] + [anywhere],
-        out_specs=[anywhere] * 4,
+    e_wide, e_tall = (quarter, units), (units, quarter)
+    flat_kinds = [(kind[0] * kind[1], kind[2]) for kind in block_kinds]
+    (
+        own_sum, got_scalars, t_sgate, x_sup, x_sdown,
+        keep_gate, keep_up, keep_down, give_up, give_down, x_gate,
+    ) = pl.pallas_call(
+        lambda *refs: routed_backward(n_dp, *refs),
+        out_shape=[like((tok_rows, width), f32), like((n_group, 8, tok_rows), f32)]
+        + [like(block_kinds[0], low)]
+        + [like(kind, low) for kind in flat_kinds[1:]]
+        + [like(kind, low) for kind in (e_wide, e_wide, e_tall, e_wide, e_tall, e_wide)],
+        in_specs=[anywhere] * 14 + [vmem],
+        out_specs=[vmem] + [anywhere] * 10,
         scratch_shapes=[
             pltpu.VMEM((width, units), low),
             pltpu.VMEM((width, units), low),
@@ -2256,34 +2360,36 @@
             pltpu.VMEM((slots, 2 * units), low),
             pltpu.VMEM((slots, width), low),
             pltpu.VMEM((group_rows, width), low),
-            pltpu.VMEM((2, quarter // 2, units), low),
-            pltpu.VMEM((2, quarter // 2, units), low),
-            pltpu.VMEM((2, units, quarter), low),
-            pltpu.SemaphoreType.DMA((16,)),
-            pltpu.SemaphoreType.DMA((2, 3)),
+            pltpu.VMEM((2, *e_wide), low),
+            pltpu.VMEM((2, *e_wide), low),
+            pltpu.VMEM((2, *e_tall), low),
+            pltpu.VMEM((n_dp, tok_rows, width), low),
+            pltpu.VMEM((2 * (n_dp - 1), tok_rows, width), low),
+            pltpu.VMEM(flat_kinds[0], low),
+            pltpu.VMEM(flat_kinds[0], low),
+            pltpu.SemaphoreType.DMA((32,)),
+            pltpu.SemaphoreType.DMA((32,)),
+            pltpu.SemaphoreType.DMA((24,)),
         ],
         name="routed_backward",
-        compiler_params=pltpu.CompilerParams(vmem_limit_bytes=63 * 2**20),
+        compiler_params=pltpu.CompilerParams(
+            collective_id=5, has_side_effects=True, vmem_limit_bytes=63 * 2**20
+        ),
         cost_estimate=pl.CostEstimate(
             flops=12 * width * slots * units,
             bytes_accessed=2 * (12 * width * units + 4 * group_rows * width),
             transcendentals=0,
         ),
     )(
-        grads_in, rows_in, gate_weight, up_weight, down_weight, e_slope, e_silu, e_hidden, pick,
-        shared_part,
-    )
-    g_egate = g_egate.reshape(n_ctx, quarter, units)
-    g_eup = g_eup.reshape(n_ctx, quarter, units)
-    moe_sum = group_out(moe_part).astype(f32)
-    mixed = (hidden_own + moe_sum).astype(low)
+        grads_in, rows_in, gate_weight, up_weight, down_weight, e_slope, e_silu, e_hidden,
+        shared_part, scalars, keep[0], *give, pick,
+    )
+    moe_sum = group_out(moe_part)
 
     own_cols = lax.dynamic_slice_in_dim(token_cols, my_expert * tok_rows, tok_rows, 0)
     probs_own = own_cols[:, :n_experts].T
     mix_own = own_cols[:, n_experts][None]
     by_share = n_ctx * share
-    e_wide = (width // n_ctx, units)
-    e_tall = (units, width // n_ctx)
     s_wide = (share, hidden_units)
     s_tall = (hidden_units, share)
     s_kinds = (s_wide, s_wide, s_tall)
@@ -2297,18 +2403,13 @@
             like((16, share), f32),
             like((n_ctx, 8, head_dim), f32),
         ]
-        + [like((n_dp, *kind), low) for kind in s_kinds]
-        + [like((2, *kind), low) for kind in e_kinds]
-        + [like(kind, low) for kind in e_kinds]
-        + [like((n_dp, *kind), low) for kind in s_kinds]
-        + [like((2, *kind), low) for kind in e_kinds],
-        in_specs=[anywhere] * 14 + [vmem] * 3 + [anywhere] * 10,
-        out_specs=[vmem] + [anywhere] * 2 + [vmem] * 2 + [anywhere] * 15,
+        + [like((n_dp, *kind), low) for kind in s_kinds[1:]]
+        + [like(kind, low) for kind in e_kinds[1:]]
+        + [like((n_dp, *kind), low) for kind in s_kinds[1:]],
+        in_specs=[vmem] * 2 + [anywhere] * 9 + [vmem] * 3 + [anywhere] * 10,
+        out_specs=[vmem] + [anywhere] * 2 + [vmem] * 2 + [anywhere] * 6,
         scratch_shapes=[
             pltpu.VMEM((seq_len, width), low),
-            pltpu.VMEM((n_dp, tok_rows, width), low),
-            pltpu.VMEM((n_dp - 1, tok_rows, width), low),
-            pltpu.VMEM((n_group, 8, tok_rows), f32),
             pltpu.VMEM((tok_rows, width), f32),
             pltpu.VMEM((tok_rows, width), f32),
             pltpu.VMEM((tok_rows, width), low),
@@ -2332,8 +2433,6 @@
             pltpu.VMEM((n_dp * n_ctx, 24, share), f32),
             pltpu.VMEM((n_dp * n_ctx, 24, share), f32),
             pltpu.VMEM((2, 16, share), f32),
-            pltpu.VMEM((3, 2, 128, units), low),
-            pltpu.VMEM((3, 2, units // 4, width // n_ctx), low),
             pltpu.VMEM((3, 2, *s_wide), low),
             pltpu.VMEM((3, 2, *s_tall), low),
             pltpu.VMEM((tok_rows, width), f32),
@@ -2359,12 +2458,13 @@
             collective_id=2, has_side_effects=True, vmem_limit_bytes=63 * 2**20
         ),
     )(
-        d_in_part, scalars, *keep, *got, g_egate, g_eup, g_edown,
+        own_sum, got_scalars, *keep[1:], x_sup, x_sdown, give_up, give_down,
         hidden_own, out_grad, tokens, small, probs_own, mix_own,
         heads_weight, wo, query, keys, values, attn, lse, attn_in, cosine, sine,
     )
     input_grad, heads_grad, out_weight_grad, small_grad, bias_grad = results[:5]
-    s_done, e_own, e_other = results[5:8], results[8:11], results[11:14]
+    s_done = (t_sgate, *results[5:7])
+    e_own, e_other = (keep_gate, keep_up, keep_down), (x_gate, *results[7:9])
     finished = pl.pallas_call(
         lambda *refs: finish_grads(n_ctx, *refs),
         out_shape=[
@@ -2378,14 +2478,16 @@
             like((share, n_ctx * cols), f32),
             like((share, n_ctx * cols), f32),
             like((n_ctx * cols, share), f32),
+            like((tok_rows, width), low),
         ],
         grid=(1,),
         in_specs=[pl.BlockSpec((n_dp, *kind), lambda i: (0, 0, 0)) for kind in s_kinds]
-        + [pl.BlockSpec((None, *kind), lambda i: (0, 0, 0)) for kind in e_kinds]
-        + [pl.BlockSpec(kind, lambda i: (0, 0)) for kind in e_kinds]
+        + [pl.BlockSpec(kind, lambda i: (0, 0)) for kind in e_kinds * 2]
         + [
             pl.BlockSpec(heads_grad.shape, lambda i: (0, 0, 0)),
             pl.BlockSpec(out_weight_grad.shape, lambda i: (0, 0, 0)),
+            pl.BlockSpec((tok_rows, width), lambda i: (0, 0)),
+            pl.BlockSpec((tok_rows, width), lambda i: (0, 0)),
         ],
         out_specs=[
             pl.BlockSpec((share, n_dp * hidden_units), lambda i: (0, 0)),
@@ -2398,14 +2500,15 @@
             pl.BlockSpec((share, n_ctx * cols), lambda i: (0, 0)),
             pl.BlockSpec((share, n_ctx * cols), lambda i: (0, 0)),
             pl.BlockSpec((n_ctx * cols, share), lambda i: (0, 0)),
+            pl.BlockSpec((tok_rows, width), lambda i: (0, 0)),
         ],
         name="finish_grads",
         compiler_params=pltpu.CompilerParams(vmem_limit_bytes=63 * 2**20),
-    )(*s_done, *e_own, *e_other, heads_grad, out_weight_grad)
+    )(*s_done, *e_own, *e_other, heads_grad, out_weight_grad, hidden_own, moe_sum)
     grad_sgate, grad_sup, grad_sdown = finished[:3]
     routed = [item[None] for item in finished[3:6]]
     heads_grad = finished[6:9]
-    grad_out = finished[9]
+    grad_out, mixed = finished[9:11]
     bias_sum = bias_grad[:, : 3 * heads].reshape(n_ctx, 3, heads, head_dim)
     bias_sum = bias_sum.transpose(1, 0, 2, 3).reshape(3, half_heads, head_dim)
     bias_share = head_dim // (n_dp * n_ctx)

time: 578 us -> 540 us (0.934)
  Pallas kernels: 531 us -> 511 us
  local copies, waits for them, and re-layouts: 19.3 us -> 8.98 us
    pallas_call x1, Pallas kernels: 195 us -> 133 us  [tokens_plan(): pl.pallas_call(lambda *refs: backward_kernel(n_blocks, n_dp, *refs), out_...]
    pallas_call x1, Pallas kernels: 43 us -> 87.5 us  [tokens_plan(): pl.pallas_call(lambda *refs: routed_backward(n_dp, *refs), out_shape=[lik...]
    pallas_call x1, Pallas kernels: 55.4 us -> 42.2 us  [tokens_plan(): pl.pallas_call(lambda *refs: moe_forward(n_dp, *refs), out_shape=[like((g...]
    pallas_call x1, Pallas kernels: 46.7 us -> 57 us  [tokens_plan(): pl.pallas_call(lambda *refs: shared_backward(n_dp, *refs), out_shape=[lik...]
  transfers between devices with their start and end apart: 4 -> 1, of which waited for: 0 -> 0; matrix products, arithmetic and copies ran while one was open for 2% -> 1% of each run, Pallas kernels for 52% -> 52%
where the time goes in v4:
time: 540 us; the launch traced here: 536 us
  Pallas kernels  511 us (95%)
  between operations  14.3 us (3%)
  local copies, waits for them, and re-layouts  8.98 us (2%)
    pallas_call x1, Pallas kernels, tokens_plan(): pl.pallas_call(lambda *refs: forward_kernel(n_blocks, n_dp, *refs), out_s...  179 us
    pallas_call x1, Pallas kernels, tokens_plan(): pl.pallas_call(lambda *refs: backward_kernel(n_blocks, n_dp, *refs), out_...  133 us
    pallas_call x1, Pallas kernels, tokens_plan(): pl.pallas_call(lambda *refs: routed_backward(n_dp, *refs), out_shape=[lik...  87.5 us
    pallas_call x1, Pallas kernels, tokens_plan(): pl.pallas_call(lambda *refs: shared_backward(n_dp, *refs), out_shape=[lik...  57 us
    pallas_call x1, Pallas kernels, tokens_plan(): pl.pallas_call(lambda *refs: moe_forward(n_dp, *refs), out_shape=[like((g...  42.2 us
    pallas_call x1, Pallas kernels, tokens_plan(): pl.pallas_call(lambda *refs: finish_grads(n_ctx, *refs), out_shape=[like(...  12 us
  transfers between devices with their start and end apart: 1, of which 0 were waited for; matrix products, arithmetic and copies ran while one was open for 1% of the time, Pallas kernels for 52%

profile of v4, /device:TPU:9, one launch (start us, length us, event | category | flops | bytes accessed | tf_op | source)
XLA Modules:
  0.0 536.1 jit_solution(14577006685161782921)
XLA Ops:
  7.2 0.0 reduce-scatter.2.cloned.1.call-start
  7.2 0.7 convert_bitcast_fusion
  8.0 0.6 copy.51
  8.6 1.3 pad.9.refs_3_
  9.8 1.3 fusion.6.refs_2_
  11.2 179.1 %forward.1 = (bf16[1024,2048]{1,0:T(8,128)(2,1)}, bf16[1024,256]{1,0:T(8,128)(2,1)}, bf16[1024,256]{1,0:T(8,128)(2,1)}, bf16[1024,256]{1,0:T(8,128)(2,1)}, bf16[...) custom-call(bf16[128,2048]{1,0:T(8,128)(2,1)} %refs_10_.3, ...), custom_call_target="tpu_custom_call" | custom-call | tf_op jit(solution)/shard_map/forward/pallas_call | solution.py:2182
  190.3 42.2 %moe_forward.1 = (f32[1024,128]{1,0:T(8,128)}, bf16[8,96,128]{2,1,0:T(8,128)(2,1)}, bf16[1024,704]{1,0:T(8,128)(2,1)}, bf16[1024,704]{1,0:T(8,128)(2,1)}, bf16[1...) custom-call(bf16[1024,2048]{1,0:T(8,128)(2,1)} %get-tuple-element.88, ...), custom_call_target="tpu_custom_call", output_to_operand_aliasing={{12}: (0, {})} | custom-call | flops 22145925120 | bytes 68681728 | tf_op jit(solution)/shard_map/moe_forward/pallas_call | solution.py:2246
  232.5 0.0 copy-start.1
  232.5 0.0 reduce-scatter.2.cloned.1.call-update
  232.6 1.0 copy-done.1
  233.6 0.2 copy.46
  233.8 0.5 dynamic-slice_bitcast_fusion.4.refs_13_
  234.3 0.6 dynamic-slice_bitcast_fusion.3.refs_12_
  234.9 57.0 %shared_backward.1 = (bf16[768,2048]{1,0:T(8,128)(2,1)}, bf16[1024,2048]{1,0:T(8,128)(2,1)}, f32[8,8,128]{2,1,0:T(8,128)}, bf16[512,704]{1,0:T(8,128)(2,1)}, bf1...) custom-call(bf16[1024,2048]{1,0:T(8,128)(2,1)} %get-tuple-element.95, ...), custom_call_target="tpu_custom_call" | custom-call | flops 17716740096 | bytes 59506688 | tf_op jit(solution)/shard_map/shared_backward/pallas_call | solution.py:2290
  291.9 87.5 %routed_backward.1 = (f32[128,2048]{1,0:T(8,128)}, f32[8,8,128]{2,1,0:T(8,128)}, bf16[4,128,704]{2,1,0:T(8,128)(2,1)}, bf16[512,704]{1,0:T(8,128)(2,1)}, bf16[28...) custom-call(bf16[768,2048]{1,0:T(8,128)(2,1)} %get-tuple-element.103, ...), custom_call_target="tpu_custom_call" | custom-call | flops 26575110144 | bytes 85983232 | tf_op jit(solution)/shard_map/routed_backward/pallas_call | solution.py:2343
  379.4 132.9 %backward.1 = (bf16[128,2048]{1,0:T(8,128)(2,1)}, bf16[4,128,768]{2,1,0:T(8,128)(2,1)}, bf16[4,256,128]{2,1,0:T(8,128)(2,1)}, f32[16,128]{1,0:T(8,128)}, f32[4,8...) custom-call(f32[128,2048]{1,0:T(8,128)} %get-tuple-element.115.refs_, ...), custom_call_target="tpu_custom_call" | custom-call | tf_op jit(solution)/shard_map/backward/pallas_call | solution.py:2397
  512.3 0.7 copy.47
  513.0 0.7 dynamic-slice_bitcast_fusion
  513.7 1.3 slice_bitcast_fusion.1
  515.0 1.3 slice_bitcast_fusion
  516.3 0.0 reduce-scatter.2.cloned.1.call-done.refs_12_
  516.3 0.0 copy-start
  516.3 12.0 %finish_grads.1 = (f32[128,2816]{1,0:T(8,128)}, f32[128,2816]{1,0:T(8,128)}, f32[2816,128]{1,0:T(8,128)}, f32[512,1408]{1,0:T(8,128)}, f32[512,1408]{1,0:T(8,128...) custom-call(bf16[4,128,704]{2,1,0:T(8,128)(2,1)} %get-tuple-element., ...), custom_call_target="tpu_custom_call" | custom-call | tf_op jit(solution)/shard_map/finish_grads/pallas_call | solution.py:2468
  528.3 0.0 copy-done
  528.3 0.8 copy.54
  (1 shorter events, 0.0 us)
Async XLA Ops:
  7.2 509.1 %reduce-scatter.2.cloned.1.call-start = ((), (), s32[]{:S(2)}) async-start(), calls=%async_computation.1 | async-start | bytes 4718592 | tf_op jit(solution)/shard_map/reduce_scatter | solution.py:2163
  232.5 1.0 copy-start.1
  516.3 12.0 %copy-start = (bf16[128,2048]{1,0:T(8,128)(2,1)S(1)}, bf16[128,2048]{1,0:T(8,128)(2,1)}, u32[]{:S(2)}) copy-start(bf16[128,2048]{1,0:T(8,128)(2,1)} %get-tuple-element.183) | copy-start | bytes 1572868
Sparse Core Ops, SparseCore 0:
  232.7 90.0 reduce-scatter.1

commit v5 on v4

--- a/solution.py
+++ b/solution.py
@@ -1361,7 +1361,7 @@
     finish(proj_in)
 
     phases.go("attention")
-    routed_over = [go_over_x(0, 0, 2)]
+    routed_over = [go_over_x(0, part, 4) for part in range(3)]
     for item in loads[3:]:
         item.wait()
     by_share = n_ctx * share
@@ -1414,6 +1414,19 @@
         d_qkv[:, cols + start : cols + start + head_dim] = turn(d_keys[...], every).astype(low)
         d_qkv[:, 2 * cols + start : 2 * cols + start + head_dim] = d_values[...].astype(low)
 
+    phases.go("heads_grad")
+
+    def heads_weights(target):
+        at = rows_of(target, by_share)
+        g_heads[at, :] = dot_f32(attn_in[:, at], d_qkv[...], 0, 0).astype(low)
+
+    each(n_dp, heads_weights)
+    heads_chain = chain_reduce(
+        wire,
+        place,
+        [(lambda t: g_heads.at[rows_of(t, by_share), :], heads_below, heads_above)],
+    )
+    next(heads_chain)
     phases.go("attention_in_grad")
 
     def output(at):
@@ -1423,23 +1436,12 @@
     phases.go("sum_in_plane")
     reduce = plane_reduce(wire, place, partial, got_core, got_one, got_two)
     next(reduce)
-
-    def heads_weights(target):
-        at = rows_of(target, by_share)
-        g_heads[at, :] = dot_f32(attn_in[:, at], d_qkv[...], 0, 0).astype(low)
-
-    each(n_dp // 2, heads_weights)
+    next(out_chain)
     next(reduce)
-    each(n_dp // 2, lambda index: heads_weights(index + n_dp // 2))
-    heads_chain = chain_reduce(
-        wire,
-        place,
-        [(lambda t: g_heads.at[rows_of(t, by_share), :], heads_below, heads_above)],
-    )
-    next(heads_chain)
+    next(out_chain)
     phases.go("sum_in_plane_end")
     finish(reduce)
-    routed_over += [go_over_x(0, 1, 2), go_over_x(1)]
+    routed_over += [go_over_x(0, 3, 4), go_over_x(1)]
 
     def norm_one(at):
         d_attn_in = plane_sum(place, partial, got_one, got_two, at)
@@ -1453,6 +1455,8 @@
             + rstd * (d_norm - normed * jnp.mean(d_norm * normed, axis=1, keepdims=True))
         ).astype(low)
 
+    phases.go("heads_chain_one")
+    next(heads_chain)
     phases.go("norm_one")
     by_rows(rows, 16, norm_one)
 
@@ -1482,6 +1486,7 @@
         item.start()
         small_items.append(item)
     phases.go("chains")
+    next(heads_chain)
     finish(out_chain)
     phases.go("heads_chain")
     finish(heads_chain)
@@ -1663,9 +1668,13 @@
         return carry
 
     phases.go("scatter")
-    lax.fori_loop(0, n_experts, scatter, 0)
+    lax.fori_loop(0, n_experts // 2, scatter, 0)
+    first = pl.ds(0, n_experts // 2 * tok_rows)
+    last = pl.ds(n_experts // 2 * tok_rows, n_experts // 2 * tok_rows)
+    stores.append(inside.start(x.at[first, :], part.at[first, :]))
+    lax.fori_loop(n_experts // 2, n_experts, scatter, 0)
     phases.go("stores")
-    stores.append(inside.start(x, part))
+    stores.append(inside.start(x.at[last, :], part.at[last, :]))
     for item in stores:
         item.wait()
     phases.go("over_y")
@@ -1723,13 +1732,11 @@
         return items
 
     coming = [fetch(index) for index in range(depth - 1)]
-    loads = [
-        inside.start(src, dst)
-        for src, dst in (
-            (s_down_in, s_down), (s_slope_in, s_slope), (s_silu_in, s_silu),
-            (s_gate_in, s_gate), (s_up_in, s_up), (moe_in, x), (s_hidden, hidden),
-        )
+    to_load = [
+        (s_down_in, s_down), (s_slope_in, s_slope), (s_silu_in, s_silu),
+        (s_gate_in, s_gate), (s_up_in, s_up), (moe_in, x), (s_hidden, hidden),
     ]
+    loads = []
     barrier([place.core])
     grads[...] = jnp.zeros_like(grads)
     sums[...] = jnp.zeros_like(sums)
@@ -1737,6 +1744,8 @@
         slot = index % depth
         if index + depth - 1 < n_experts:
             coming.append(fetch(index + depth - 1))
+        if index < len(to_load):
+            loads.append(inside.start(*to_load[index]))
         for item in coming[index]:
             item.wait()
         here = pl.ds(index * tok_rows, tok_rows)
@@ -1879,10 +1888,13 @@
     barrier([place.core, place.over_x] + [near(dz, y_to) for dz, y_to in members])
 
     over_x = []
-    for src, dst in ((give_sgate, x_sgate), (give_sup, x_sup), (give_sdown, x_sdown)):
+
+    def go_over_x(src, dst):
         item = wire.copy(src, dst, place.over_x)
         item.start()
         over_x.append(item)
+
+    go_over_x(give_sgate, x_sgate)
     scalar_items = [inside.start(scalars.at[group], got_scalars.at[group])]
     for dz, y_to in members:
         target = lax.bitwise_xor(z, jnp.int32(dz)) * 2 + y_to
@@ -1905,6 +1917,8 @@
         d_in[at, :] = (dot_f32(d_gate, wg[...], 1, 1) + dot_f32(d_up, wu[...], 1, 1)).astype(low)
 
     routed_tile(pl.ds(0, half), loads[4:6])
+    go_over_x(give_sup, x_sup)
+    go_over_x(give_sdown, x_sdown)
     routed_tile(pl.ds(half, half), [])
     for item in loads[6:]:
         item.wait()
@@ -2093,8 +2107,7 @@
     n_dp, share, units = t_gate.shape
     for source, target in ((t_gate, o_sgate), (t_up, o_sup)):
         target[...] = jnp.concatenate([source[k].astype(f32) for k in range(n_dp)], axis=1)
-    for k in range(n_dp):
-        o_sdown[k * units : (k + 1) * units, :] = t_down[k].astype(f32)
+    o_sdown[...] = t_down[0].astype(f32)
     for own, far, target in (
         (own_gate, far_gate, o_egate), (own_up, far_up, o_eup), (own_down, far_down, o_edown),
     ):
@@ -2103,13 +2116,13 @@
             target[at, :] = own[at, :].astype(f32) + far[at, :].astype(f32)
 
         by_rows(target.shape[0], 32, add)
+
     o_mixed[...] = (hidden[...] + moe_sum[...].astype(f32)).astype(o_mixed.dtype)
     cols = heads.shape[2] // 3
     for k, target in enumerate((o_query, o_key, o_value)):
         for c in range(n_ctx):
             target[:, c * cols : (c + 1) * cols] = heads[c, :, k * cols : (k + 1) * cols].astype(f32)
-    for c in range(n_ctx):
-        o_out[c * cols : (c + 1) * cols, :] = out_weight[c].astype(f32)
+    o_out[...] = out_weight[0].astype(f32)
 
 
 def whole_tables(seq_len, head_dim):
@@ -2480,27 +2493,23 @@
             like((n_ctx * cols, share), f32),
             like((tok_rows, width), low),
         ],
-        grid=(1,),
-        in_specs=[pl.BlockSpec((n_dp, *kind), lambda i: (0, 0, 0)) for kind in s_kinds]
-        + [pl.BlockSpec(kind, lambda i: (0, 0)) for kind in e_kinds * 2]
+        grid=(4,),
+        in_specs=[pl.BlockSpec((n_dp, share // 4, hidden_units), lambda i: (0, i, 0))] * 2
+        + [pl.BlockSpec((1, hidden_units, share), lambda i: (i, 0, 0))]
+        + [pl.BlockSpec((kind[0] // 4, kind[1]), lambda i: (i, 0)) for kind in e_kinds * 2]
         + [
-            pl.BlockSpec(heads_grad.shape, lambda i: (0, 0, 0)),
-            pl.BlockSpec(out_weight_grad.shape, lambda i: (0, 0, 0)),
-            pl.BlockSpec((tok_rows, width), lambda i: (0, 0)),
-            pl.BlockSpec((tok_rows, width), lambda i: (0, 0)),
+            pl.BlockSpec((n_ctx, share // 4, 3 * cols), lambda i: (0, i, 0)),
+            pl.BlockSpec((1, cols, share), lambda i: (i, 0, 0)),
+            pl.BlockSpec((tok_rows // 4, width), lambda i: (i, 0)),
+            pl.BlockSpec((tok_rows // 4, width), lambda i: (i, 0)),
         ],
-        out_specs=[
-            pl.BlockSpec((share, n_dp * hidden_units), lambda i: (0, 0)),
-            pl.BlockSpec((share, n_dp * hidden_units), lambda i: (0, 0)),
-            pl.BlockSpec((n_dp * hidden_units, share), lambda i: (0, 0)),
-            pl.BlockSpec(e_wide, lambda i: (0, 0)),
-            pl.BlockSpec(e_wide, lambda i: (0, 0)),
-            pl.BlockSpec(e_tall, lambda i: (0, 0)),
-            pl.BlockSpec((share, n_ctx * cols), lambda i: (0, 0)),
-            pl.BlockSpec((share, n_ctx * cols), lambda i: (0, 0)),
-            pl.BlockSpec((share, n_ctx * cols), lambda i: (0, 0)),
-            pl.BlockSpec((n_ctx * cols, share), lambda i: (0, 0)),
-            pl.BlockSpec((tok_rows, width), lambda i: (0, 0)),
+        out_specs=[pl.BlockSpec((share // 4, n_dp * hidden_units), lambda i: (i, 0))] * 2
+        + [pl.BlockSpec((hidden_units, share), lambda i: (i, 0))]
+        + [pl.BlockSpec((kind[0] // 4, kind[1]), lambda i: (i, 0)) for kind in e_kinds]
+        + [pl.BlockSpec((share // 4, n_ctx * cols), lambda i: (i, 0))] * 3
+        + [
+            pl.BlockSpec((cols, share), lambda i: (i, 0)),
+            pl.BlockSpec((tok_rows // 4, width), lambda i: (i, 0)),
         ],
         name="finish_grads",
         compiler_params=pltpu.CompilerParams(vmem_limit_bytes=63 * 2**20),

time: 540 us -> 536 us (level)
  no operation moved by 1% of the time
where the time goes in v5:
time: 536 us; the launch traced here: 531 us
  Pallas kernels  506 us (94%)
  between operations  14.3 us (3%)
  local copies, waits for them, and re-layouts  8.98 us (2%)
    pallas_call x1, Pallas kernels, tokens_plan(): pl.pallas_call(lambda *refs: forward_kernel(n_blocks, n_dp, *refs), out_s...  179 us
    pallas_call x1, Pallas kernels, tokens_plan(): pl.pallas_call(lambda *refs: backward_kernel(n_blocks, n_dp, *refs), out_...  132 us
    pallas_call x1, Pallas kernels, tokens_plan(): pl.pallas_call(lambda *refs: routed_backward(n_dp, *refs), out_shape=[lik...  87.6 us
    pallas_call x1, Pallas kernels, tokens_plan(): pl.pallas_call(lambda *refs: shared_backward(n_dp, *refs), out_shape=[lik...  53.8 us
    pallas_call x1, Pallas kernels, tokens_plan(): pl.pallas_call(lambda *refs: moe_forward(n_dp, *refs), out_shape=[like((g...  42.2 us
  transfers between devices with their start and end apart: 1, of which 0 were waited for; matrix products, arithmetic and copies ran while one was open for 1% of the time, Pallas kernels for 52%

profile of v5, /device:TPU:9, one launch (start us, length us, event | category | flops | bytes accessed | tf_op | source)
XLA Modules:
  0.0 531.1 jit_solution(7057605534881910433)
XLA Ops:
  7.2 0.0 reduce-scatter.2.cloned.1.call-start
  7.2 0.7 convert_bitcast_fusion
  8.0 0.6 copy.51
  8.6 1.3 pad.9.refs_3_
  9.8 1.3 fusion.6.refs_2_
  11.2 179.1 %forward.1 = (bf16[1024,2048]{1,0:T(8,128)(2,1)}, bf16[1024,256]{1,0:T(8,128)(2,1)}, bf16[1024,256]{1,0:T(8,128)(2,1)}, bf16[1024,256]{1,0:T(8,128)(2,1)}, bf16[...) custom-call(bf16[128,2048]{1,0:T(8,128)(2,1)} %refs_10_.3, ...), custom_call_target="tpu_custom_call" | custom-call | tf_op jit(solution)/shard_map/forward/pallas_call | solution.py:2195
  190.3 42.2 %moe_forward.1 = (f32[1024,128]{1,0:T(8,128)}, bf16[8,96,128]{2,1,0:T(8,128)(2,1)}, bf16[1024,704]{1,0:T(8,128)(2,1)}, bf16[1024,704]{1,0:T(8,128)(2,1)}, bf16[1...) custom-call(bf16[1024,2048]{1,0:T(8,128)(2,1)} %get-tuple-element.88, ...), custom_call_target="tpu_custom_call", output_to_operand_aliasing={{12}: (0, {})} | custom-call | flops 22145925120 | bytes 68681728 | tf_op jit(solution)/shard_map/moe_forward/pallas_call | solution.py:2259
  232.5 0.0 copy-start.1
  232.5 0.0 reduce-scatter.2.cloned.1.call-update
  232.6 1.0 copy-done.1
  233.6 0.2 copy.46
  233.8 0.5 dynamic-slice_bitcast_fusion.4.refs_13_
  234.3 0.6 dynamic-slice_bitcast_fusion.3.refs_12_
  234.9 53.8 %shared_backward.1 = (bf16[768,2048]{1,0:T(8,128)(2,1)}, bf16[1024,2048]{1,0:T(8,128)(2,1)}, f32[8,8,128]{2,1,0:T(8,128)}, bf16[512,704]{1,0:T(8,128)(2,1)}, bf1...) custom-call(bf16[1024,2048]{1,0:T(8,128)(2,1)} %get-tuple-element.95, ...), custom_call_target="tpu_custom_call" | custom-call | flops 17716740096 | bytes 59506688 | tf_op jit(solution)/shard_map/shared_backward/pallas_call | solution.py:2303
  288.7 87.6 %routed_backward.1 = (f32[128,2048]{1,0:T(8,128)}, f32[8,8,128]{2,1,0:T(8,128)}, bf16[4,128,704]{2,1,0:T(8,128)(2,1)}, bf16[512,704]{1,0:T(8,128)(2,1)}, bf16[28...) custom-call(bf16[768,2048]{1,0:T(8,128)(2,1)} %get-tuple-element.103, ...), custom_call_target="tpu_custom_call" | custom-call | flops 26575110144 | bytes 85983232 | tf_op jit(solution)/shard_map/routed_backward/pallas_call | solution.py:2356
  376.2 132.4 %backward.1 = (bf16[128,2048]{1,0:T(8,128)(2,1)}, bf16[4,128,768]{2,1,0:T(8,128)(2,1)}, bf16[4,256,128]{2,1,0:T(8,128)(2,1)}, f32[16,128]{1,0:T(8,128)}, f32[4,8...) custom-call(f32[128,2048]{1,0:T(8,128)} %get-tuple-element.115.refs_, ...), custom_call_target="tpu_custom_call" | custom-call | tf_op jit(solution)/shard_map/backward/pallas_call | solution.py:2410
  508.6 0.7 copy.47
  509.3 0.7 dynamic-slice_bitcast_fusion
  510.0 1.3 slice_bitcast_fusion.1
  511.3 1.3 slice_bitcast_fusion
  512.6 0.0 reduce-scatter.2.cloned.1.call-done.refs_12_
  512.6 0.0 copy-start
  512.6 10.6 %finish_grads.1 = (f32[128,2816]{1,0:T(8,128)}, f32[128,2816]{1,0:T(8,128)}, f32[2816,128]{1,0:T(8,128)}, f32[512,1408]{1,0:T(8,128)}, f32[512,1408]{1,0:T(8,128...) custom-call(bf16[4,128,704]{2,1,0:T(8,128)(2,1)} %get-tuple-element., ...), custom_call_target="tpu_custom_call" | custom-call | tf_op jit(solution)/shard_map/finish_grads/pallas_call | solution.py:2481
  523.2 0.0 copy-done
  523.2 0.8 copy.54
  (1 shorter events, 0.0 us)
Async XLA Ops:
  7.2 505.4 %reduce-scatter.2.cloned.1.call-start = ((), (), s32[]{:S(2)}) async-start(), calls=%async_computation.1 | async-start | bytes 4718592 | tf_op jit(solution)/shard_map/reduce_scatter | solution.py:2176
  232.5 1.0 copy-start.1
  512.6 10.6 %copy-start = (bf16[128,2048]{1,0:T(8,128)(2,1)S(1)}, bf16[128,2048]{1,0:T(8,128)(2,1)}, u32[]{:S(2)}) copy-start(bf16[128,2048]{1,0:T(8,128)(2,1)} %get-tuple-element.183) | copy-start | bytes 1572868
Sparse Core Ops, SparseCore 0:
  232.7 98.6 reduce-scatter.1

commit v6 on v5

--- a/solution.py
+++ b/solution.py
@@ -1488,29 +1488,29 @@
     phases.go("chains")
     next(heads_chain)
     finish(out_chain)
+
+    out_block[...] = g_out[:, rows_of(z, by_share)]
+    last = []
+
+    def to_pieces(src_of, target):
+        for dc in range(n_ctx):
+            src = src_of(lax.bitwise_xor(c, jnp.int32(dc)))
+            if dc:
+                item = wire.copy(src, target.at[c], moved(0, dc, y))
+                item.start()
+            else:
+                item = inside.start(src, target.at[c])
+            last.append(item)
+
+    to_pieces(lambda to: out_block.at[:, rows_of(to, share)], out_weight_grad)
     phases.go("heads_chain")
     finish(heads_chain)
     phases.go("last")
 
-    out_block[...] = g_out[:, rows_of(z, by_share)]
-    last = []
-    for dc in range(n_ctx):
-        to = lax.bitwise_xor(c, jnp.int32(dc))
-        pairs = [
-            (
-                g_heads.at[pl.ds(pl.multiple_of(z * by_share + to * share, share), share), :],
-                heads_grad.at[c],
-            ),
-            (out_block.at[:, rows_of(to, share)], out_weight_grad.at[c]),
-        ]
-        for src, dst in pairs:
-            if dc:
-                item = wire.copy(src, dst, moved(0, dc, y))
-                item.start()
-            else:
-                item = inside.start(src, dst)
-            last.append(item)
-
+    to_pieces(
+        lambda to: g_heads.at[pl.ds(pl.multiple_of(z * by_share + to * share, share), share), :],
+        heads_grad,
+    )
     phases.go("small")
     for item in small_items:
         item.wait_recv()

time: 536 us -> 536 us (level)
  transfers between devices with their start and end apart: 1 -> 1, of which waited for: 0 -> 0; matrix products, arithmetic and copies ran while one was open for 1% -> 1% of each run, Pallas kernels for 52% -> 51%
where the time goes in v6:
time: 536 us; the launch traced here: 529 us
  Pallas kernels  503 us (94%)
  between operations  14.3 us (3%)
  local copies, waits for them, and re-layouts  8.98 us (2%)
    pallas_call x1, Pallas kernels, tokens_plan(): pl.pallas_call(lambda *refs: forward_kernel(n_blocks, n_dp, *refs), out_s...  179 us
    pallas_call x1, Pallas kernels, tokens_plan(): pl.pallas_call(lambda *refs: backward_kernel(n_blocks, n_dp, *refs), out_...  130 us
    pallas_call x1, Pallas kernels, tokens_plan(): pl.pallas_call(lambda *refs: routed_backward(n_dp, *refs), out_shape=[lik...  87.6 us
    pallas_call x1, Pallas kernels, tokens_plan(): pl.pallas_call(lambda *refs: shared_backward(n_dp, *refs), out_shape=[lik...  53.8 us
    pallas_call x1, Pallas kernels, tokens_plan(): pl.pallas_call(lambda *refs: moe_forward(n_dp, *refs), out_shape=[like((g...  42.2 us
  transfers between devices with their start and end apart: 1, of which 0 were waited for; matrix products, arithmetic and copies ran while one was open for 1% of the time, Pallas kernels for 51%

profile of v6, /device:TPU:9, one launch (start us, length us, event | category | flops | bytes accessed | tf_op | source)
XLA Modules:
  0.0 528.7 jit_solution(6464278598196734025)
XLA Ops:
  7.2 0.0 reduce-scatter.2.cloned.1.call-start
  7.2 0.7 convert_bitcast_fusion
  8.0 0.6 copy.51
  8.6 1.3 pad.9.refs_3_
  9.8 1.3 fusion.6.refs_2_
  11.2 179.1 %forward.1 = (bf16[1024,2048]{1,0:T(8,128)(2,1)}, bf16[1024,256]{1,0:T(8,128)(2,1)}, bf16[1024,256]{1,0:T(8,128)(2,1)}, bf16[1024,256]{1,0:T(8,128)(2,1)}, bf16[...) custom-call(bf16[128,2048]{1,0:T(8,128)(2,1)} %refs_10_.3, ...), custom_call_target="tpu_custom_call" | custom-call | tf_op jit(solution)/shard_map/forward/pallas_call | solution.py:2195
  190.3 42.2 %moe_forward.1 = (f32[1024,128]{1,0:T(8,128)}, bf16[8,96,128]{2,1,0:T(8,128)(2,1)}, bf16[1024,704]{1,0:T(8,128)(2,1)}, bf16[1024,704]{1,0:T(8,128)(2,1)}, bf16[1...) custom-call(bf16[1024,2048]{1,0:T(8,128)(2,1)} %get-tuple-element.88, ...), custom_call_target="tpu_custom_call", output_to_operand_aliasing={{12}: (0, {})} | custom-call | flops 22145925120 | bytes 68681728 | tf_op jit(solution)/shard_map/moe_forward/pallas_call | solution.py:2259
  232.5 0.0 copy-start.1
  232.5 0.0 reduce-scatter.2.cloned.1.call-update
  232.6 1.0 copy-done.1
  233.6 0.2 copy.46
  233.8 0.5 dynamic-slice_bitcast_fusion.4.refs_13_
  234.3 0.6 dynamic-slice_bitcast_fusion.3.refs_12_
  234.9 53.8 %shared_backward.1 = (bf16[768,2048]{1,0:T(8,128)(2,1)}, bf16[1024,2048]{1,0:T(8,128)(2,1)}, f32[8,8,128]{2,1,0:T(8,128)}, bf16[512,704]{1,0:T(8,128)(2,1)}, bf1...) custom-call(bf16[1024,2048]{1,0:T(8,128)(2,1)} %get-tuple-element.95, ...), custom_call_target="tpu_custom_call" | custom-call | flops 17716740096 | bytes 59506688 | tf_op jit(solution)/shard_map/shared_backward/pallas_call | solution.py:2303
  288.7 87.6 %routed_backward.1 = (f32[128,2048]{1,0:T(8,128)}, f32[8,8,128]{2,1,0:T(8,128)}, bf16[4,128,704]{2,1,0:T(8,128)(2,1)}, bf16[512,704]{1,0:T(8,128)(2,1)}, bf16[28...) custom-call(bf16[768,2048]{1,0:T(8,128)(2,1)} %get-tuple-element.103, ...), custom_call_target="tpu_custom_call" | custom-call | flops 26575110144 | bytes 85983232 | tf_op jit(solution)/shard_map/routed_backward/pallas_call | solution.py:2356
  376.2 130.0 %backward.1 = (bf16[128,2048]{1,0:T(8,128)(2,1)}, bf16[4,128,768]{2,1,0:T(8,128)(2,1)}, bf16[4,256,128]{2,1,0:T(8,128)(2,1)}, f32[16,128]{1,0:T(8,128)}, f32[4,8...) custom-call(f32[128,2048]{1,0:T(8,128)} %get-tuple-element.115.refs_, ...), custom_call_target="tpu_custom_call" | custom-call | tf_op jit(solution)/shard_map/backward/pallas_call | solution.py:2410
  506.2 0.7 copy.47
  507.0 0.7 dynamic-slice_bitcast_fusion
  507.7 1.3 slice_bitcast_fusion.1
  509.0 1.3 slice_bitcast_fusion
  510.2 0.0 reduce-scatter.2.cloned.1.call-done.refs_12_
  510.2 0.0 copy-start
  510.2 10.6 %finish_grads.1 = (f32[128,2816]{1,0:T(8,128)}, f32[128,2816]{1,0:T(8,128)}, f32[2816,128]{1,0:T(8,128)}, f32[512,1408]{1,0:T(8,128)}, f32[512,1408]{1,0:T(8,128...) custom-call(bf16[4,128,704]{2,1,0:T(8,128)(2,1)} %get-tuple-element., ...), custom_call_target="tpu_custom_call" | custom-call | tf_op jit(solution)/shard_map/finish_grads/pallas_call | solution.py:2481
  520.9 0.0 copy-done
  520.9 0.8 copy.54
  (1 shorter events, 0.0 us)
Async XLA Ops:
  7.2 503.1 %reduce-scatter.2.cloned.1.call-start = ((), (), s32[]{:S(2)}) async-start(), calls=%async_computation.1 | async-start | bytes 4718592 | tf_op jit(solution)/shard_map/reduce_scatter | solution.py:2176
  232.5 1.0 copy-start.1
  510.2 10.6 %copy-start = (bf16[128,2048]{1,0:T(8,128)(2,1)S(1)}, bf16[128,2048]{1,0:T(8,128)(2,1)}, u32[]{:S(2)}) copy-start(bf16[128,2048]{1,0:T(8,128)(2,1)} %get-tuple-element.183) | copy-start | bytes 1572868
Sparse Core Ops, SparseCore 0:
  232.7 98.6 reduce-scatter.1
